TPU v7x, 32 devices: a whole 2x2x4 slice. The times are simulated.
32 devices in a mesh: segment: 2 (over y), win: 4 (over z), seq: 4 (over x, core).
Axes of the slice: x: 2, y: 2, z: 4, core: 2. Of those that a mesh axis runs over, the one named last changes fastest.
Arguments:
- latents: bfloat16 [2, 32, 128, 1536], P('segment', 'seq', 'win'), may hold values from -6 to 6
- timesteps: int32 [2], P('segment'), may hold values from 0 to 31, as said below
- offsets: int32 [2, 2], P('segment'), may hold values from 1 to 31
- qkv_weight: bfloat16 [2, 1536, 16, 288], P('segment', None, 'seq'), may hold values from -0.15309311 to 0.15309311
- logit_scale: float32 [2, 16], P('segment', 'seq'), may hold values from 4 to 256
- out_weight: bfloat16 [2, 1536, 1536], P('segment'), may hold values from -0.15625 to 0.15625
- mod_shift: float32 [2, 32, 1536], P('segment'), may hold values from -3 to 3
- mod_scale: float32 [2, 32, 1536], P('segment'), may hold values from 0.5 to 1.5
- mod_gate: float32 [2, 32, 1536], P('segment'), may hold values from 1 to 3
Outputs:
- handed: bfloat16 [2, 32, 128, 1536], P('segment', 'seq', 'win')
Inputs may be any that keep to these rules, and one draw needn't show every extreme that they name: `timesteps`: the sections' noise levels differ from one another.
All inputs are finite; a program needn't handle non-finite values.
Results may differ from a plain program's by a relative error of at most 0.015.
Values may be sent and summed in bfloat16 or wider, within the bound.
No kernel may reach another device: no remote copies, remote signals or barrier semaphores. Data moves between devices by JAX's collectives and lax.ppermute only.
A program may use at most 64 MiB of HBM per device.

v0:
```python
import jax
import jax.numpy as jnp
from jax import lax
from jax.sharding import PartitionSpec as P

eps_norm = 1e-06
masked = -1e30


def passed_along(block, axis, distance):
    devices = range(lax.axis_size(axis))
    route = [((i - distance) % len(devices), i) for i in devices]
    return lax.ppermute(block, axis, route)


def unit_split(mixture, size):
    queries = mixture[..., :size]
    key_part = mixture[..., size : 2 * size]
    values = mixture[..., 2 * size :]
    queries = queries * lax.rsqrt(jnp.sum(queries * queries, -1, keepdims=True) + eps_norm)
    key_part = key_part * lax.rsqrt(jnp.sum(key_part * key_part, -1, keepdims=True) + eps_norm)
    return jnp.concatenate([queries, key_part, values], -1).astype(jnp.bfloat16)


def table_row(table, noise_level):
    onehot = (lax.iota(jnp.int32, table.shape[0]) == noise_level).astype(jnp.float32)
    return jnp.dot(
        onehot, table, precision=lax.Precision.HIGHEST, preferred_element_type=jnp.float32
    )


def shards(
    latents, timesteps, offsets, qkv_weight, logit_scale, out_weight, mod_shift, mod_scale, mod_gate
):
    local_tile = latents[0]
    row_count, col_count, model_width = local_tile.shape
    heads_here = qkv_weight.shape[2]
    head_size = qkv_weight.shape[3] // 3
    seq_count = lax.axis_size("seq")
    inner_here = heads_here * head_size
    noise_level = timesteps[0]
    lat_offset = offsets[0, 0]
    lon_offset = offsets[0, 1]
    shift_row = table_row(mod_shift[0], noise_level)
    scale_row = table_row(mod_scale[0], noise_level)
    gate_row = table_row(mod_gate[0], noise_level)
    neighbour = passed_along(local_tile, "win", -1)
    joined = jnp.concatenate([local_tile, neighbour], axis=1)
    shifted = lax.dynamic_slice_in_dim(joined, lon_offset, col_count, 1)
    residual = shifted.astype(jnp.float32)
    average = jnp.mean(residual, -1, keepdims=True)
    centred = residual - average
    variance = jnp.mean(centred * centred, -1, keepdims=True)
    normed = (centred * lax.rsqrt(variance + eps_norm) * scale_row + shift_row).astype(jnp.bfloat16)
    weights = qkv_weight[0].reshape(model_width, heads_here * 3 * head_size)
    shard_rows = lax.all_gather(normed, "seq", axis=0, tiled=True)
    mixture = jnp.dot(
        shard_rows.reshape(-1, model_width), weights, preferred_element_type=jnp.float32
    )
    mixture = mixture.reshape(shard_rows.shape[0], col_count, heads_here, 3 * head_size)
    gathered = unit_split(mixture, head_size)
    window = jnp.roll(gathered, -lat_offset, axis=0)
    side = window.shape[0]
    token_total = side * col_count
    tokens = window.reshape(token_total, heads_here, 3 * head_size)
    query_unit = tokens[..., :head_size]
    key_unit = tokens[..., head_size : 2 * head_size]
    value_rows = tokens[..., 2 * head_size :]
    token_group = lax.iota(jnp.int32, token_total) // col_count >= side - lat_offset
    scales = logit_scale[0]
    block_rows = min(512, token_total)
    block_count = token_total // block_rows

    def attend(block_index):
        first = block_index * block_rows
        query_block = lax.dynamic_slice_in_dim(query_unit, first, block_rows, 0)
        group_block = lax.dynamic_slice_in_dim(token_group, first, block_rows, 0)
        scores = (
            jnp.einsum("qhd,khd->hqk", query_block, key_unit, preferred_element_type=jnp.float32)
            * scales[:, None, None]
        )
        allowed = group_block[:, None] == token_group[None, :]
        scores = jnp.where(allowed[None], scores, masked)
        row_max = jnp.max(scores, -1, keepdims=True)
        lifted = jnp.exp(scores - row_max)
        probabilities = (lifted / jnp.sum(lifted, -1, keepdims=True)).astype(jnp.bfloat16)
        return jnp.einsum(
            "hqk,khd->qhd", probabilities, value_rows, preferred_element_type=jnp.float32
        ).astype(jnp.bfloat16)

    heads_out = lax.map(attend, lax.iota(jnp.int32, block_count)).reshape(
        side, col_count, inner_here
    )
    heads_out = jnp.roll(heads_out, lat_offset, axis=0)
    spread = lax.all_to_all(heads_out, "seq", split_axis=0, concat_axis=2, tiled=True)
    grouped = spread.reshape(row_count * col_count, seq_count, inner_here)
    full_out = out_weight[0].reshape(seq_count, inner_here, model_width)
    partial_value = jnp.einsum(
        "tgk,gke->tge", grouped, full_out, preferred_element_type=jnp.float32
    ).astype(jnp.bfloat16)
    branch = jnp.sum(partial_value.astype(jnp.float32), 1).reshape(
        row_count, col_count, model_width
    )
    attention = branch.astype(jnp.bfloat16)
    result = (residual + gate_row * attention.astype(jnp.float32)).astype(jnp.bfloat16)
    carried = passed_along(result, "win", 1)
    joined_back = jnp.concatenate([carried, result], axis=1)
    restored = lax.dynamic_slice_in_dim(joined_back, col_count - lon_offset, col_count, 1)
    handed = passed_along(restored, "segment", 1)
    return handed[None]


def solution(mesh):
    in_specs = (
        P("segment", "seq", "win", None),
        P("segment"),
        P("segment", None),
        P("segment", None, "seq", None),
        P("segment", "seq"),
        P("segment", None, None),
        P("segment", None, None),
        P("segment", None, None),
        P("segment", None, None),
    )
    out_specs = P("segment", "seq", "win", None)
    return jax.shard_map(shards, mesh=mesh, in_specs=in_specs, out_specs=out_specs, check_vma=False)
```

profile of v0, /device:TPU:0, one launch (start us, length us, event | category | flops | bytes accessed | tf_op | source)
XLA Modules:
  0.0 201.9 jit_solution(16388572729148039079)
XLA Ops:
  6.5 5.0 %collective-permute-start = (bf16[8,32,1536]{2,1,0:T(8,128)(2,1)}, bf16[8,32,1536]{2,1,0:T(8,128)(2,1)}, u32[]{:S(2)}, u32[]{:S(2)}) collective-permute-start(bf16[8,32,1536]{2,1,0:T(8,128)(2,1)} %bitcast.74), channel_id=1, source_target_pairs={{4,0},{8,4},{12,8},{0,12},{5,1},{9,5},{13,9},{1,13},{6,2},{10,6},{... | collective-permute-start | bytes 2359304 | tf_op jit(solution)/shard_map/ppermute | solution.py:13
  11.6 1.4 fusion.62
  17.8 10.9 %collective-permute-done = bf16[8,32,1536]{2,1,0:T(8,128)(2,1)} collective-permute-done((bf16[8,32,1536]{2,1,0:T(8,128)(2,1)}, bf16[8,32,1536]{2,1,0:T(8,128)(2,1)}, u32[]{:S(2)}, u32[]{:S(2)}) %collective-permute-start) | collective-permute-done | bytes 786464 | tf_op jit(solution)/shard_map/ppermute | solution.py:13
  28.7 1.8 convert_reduce_fusion
  31.4 1.2 fusion.37
  35.8 27.6 %all-gather.2.cloned.1.call-done = bf16[32,32,1536]{2,1,0:T(8,128)(2,1)} async-done(((bf16[8,32,1536]{2,1,0:T(8,128)(2,1)}), bf16[32,32,1536]{2,1,0:T(8,128)(2,1)}) %all-gather.2.cloned.1.call-update) | async-done | bytes 3145744 | tf_op jit(solution)/shard_map/all_gather | solution.py:56
  63.4 6.9 %fusion.23 = f32[32,32,4,288]{3,1,2,0:T(8,128)S(1)} fusion(bf16[1,1536,4,288]{1,3,2,0:T(8,128)(2,1)S(1)} %copy-done, bf16[32,32,1536]{2,1,0:T(8,128)(2,1)} %all-gather.2.cloned.1.call-done), kind=kOutput, calls=%fused_computation.27 | convolution fusion | flops 3623878656 | bytes 11403264 | tf_op jit(solution)/shard_map/dot_general | solution.py:57
  70.3 1.8 multiply_reduce_fusion
  72.6 2.0 multiply_convert_fusion
  74.6 6.8 %fusion.27 = bf16[32,32,4,288]{3,1,2,0:T(8,128)(2,1)S(1)} fusion(s32[]{:T(128)S(6)} %select_n.45, bf16[32,32,4,96]{3,1,2,0:T(8,128)(2,1)S(1)} %get-tuple-element.87, bf16[32,32,4,96]{3,1,2,0:T(8,128)(2,1)S(1)} %get-tuple-element.86, bf16[32,32,4,96]{3,1,2,0:T(8,128)(2,1)S(1)} %slice.44), kind=kLoop, calls=%fused_computation.31 | loop fusion | flops 14155776 | bytes 4718596 | tf_op jit(solution)/shard_map/jit(_roll_dynamic)/concatenate | solution.py:62
  81.8 2.4 %fusion.61 = (bf16[1024,4,96]{2,0,1:T(8,128)(2,1)}, bf16[1024,4,96]{2,0,1:T(8,128)(2,1)}, bf16[1024,4,96]{2,0,1:T(8,128)(2,1)}) fusion(bf16[1024,4,288]{2,0,1:T(8,128)(2,1)S(1)} %bitcast.72), kind=kLoop, calls=%fused_computation.87 | loop fusion | bytes 4718592 | tf_op jit(solution)/shard_map/slice | solution.py:68
  84.3 2.2 %copy.16 = bf16[1024,4,96]{0,2,1:T(8,128)(2,1)} copy(bf16[1024,4,96]{2,0,1:T(8,128)(2,1)} %get-tuple-element.90) | data formatting | bytes 1572864 | tf_op jit(solution)/shard_map/while | solution.py:91
  86.5 2.2 %copy.17 = bf16[1024,4,96]{0,2,1:T(8,128)(2,1)} copy(bf16[1024,4,96]{2,0,1:T(8,128)(2,1)} %get-tuple-element.89) | data formatting | bytes 1572864 | tf_op jit(solution)/shard_map/while | solution.py:91
  88.7 2.2 %copy.18 = bf16[1024,4,96]{0,2,1:T(8,128)(2,1)} copy(bf16[1024,4,96]{2,0,1:T(8,128)(2,1)} %get-tuple-element.88) | data formatting | bytes 1572864 | tf_op jit(solution)/shard_map/while | solution.py:91
  91.0 33.0 %while.10 = (s32[]{:T(128)}, bf16[2,512,4,96]{1,3,2,0:T(8,128)(2,1)}, s32[2]{0:T(128)S(1)}, pred[1024]{0:T(1024)(128)(4,1)S(1)}, bf16[1024,4,96]{0,2,1:T(8,128)(...) while((s32[]{:T(128)}, ...), condition=%wide.region_7.8_spmd, body=%wide.region_4.7_spmd.sunk | while | flops 818611200 | bytes 20204744 | solution.py:91
  92.3 1.2 broadcast_compare_fusion.2
  93.4 8.2 %fusion.76 = (f32[4,512]{1,0:T(4,128)}, f32[4,512,1024]{2,1,0:T(8,128)}) fusion(f32[4]{0:T(128)S(1)} %bitcast.78, pred[512,1024]{1,0:T(8,128)(4,1)} %broadcast_compare_fusion.2, bf16[1024,4,96]{0,2,1:T(8,128)(2,1)} %get-tuple-element.177, bf16[1024,4,96]{0,2,1:T(8,128)(2,1)} %get-tuple-element.176, s32[]{:T(128)S(6)} %select_n.65), kind=kOutput, calls=%fused_computation.86.clone.1 | convolution fusion | flops 411042816 | bytes 10100756 | tf_op jit(solution)/shard_map/while/body/eval_jaxpr/sub | solution.py:85
  101.7 5.8 %fusion.77 = bf16[2,512,4,96]{1,3,2,0:T(8,128)(2,1)} fusion(bf16[2,512,4,96]{1,3,2,0:T(8,128)(2,1)} %get-tuple-element.161, s32[]{:T(128)} %get-tuple-element.160, bf16[1024,4,96]{0,2,1:T(8,128)(2,1)} %get-tuple-element.179, f32[4,512,1024]{2,1,0:T(8,128)} %get-tuple-element.146, f32[4,512]{1,0:T(4,128)} %get-tuple-element.147), kind=kOutput, calls=%fused_computation.11.clone.1 | convolution fusion | flops 407044096 | bytes 9576960 | tf_op jit(solution)/shard_map/while/body/eval_jaxpr/hqk,khd->qhd/dot_general | solution.py:87
  108.8 1.2 broadcast_compare_fusion.2
  109.9 8.2 %fusion.76 = (f32[4,512]{1,0:T(4,128)}, f32[4,512,1024]{2,1,0:T(8,128)}) fusion(f32[4]{0:T(128)S(1)} %bitcast.78, pred[512,1024]{1,0:T(8,128)(4,1)} %broadcast_compare_fusion.2, bf16[1024,4,96]{0,2,1:T(8,128)(2,1)} %get-tuple-element.177, bf16[1024,4,96]{0,2,1:T(8,128)(2,1)} %get-tuple-element.176, s32[]{:T(128)S(6)} %select_n.65), kind=kOutput, calls=%fused_computation.86.clone.1 | convolution fusion | flops 411042816 | bytes 10100756 | tf_op jit(solution)/shard_map/while/body/eval_jaxpr/sub | solution.py:85
  118.2 5.8 %fusion.77 = bf16[2,512,4,96]{1,3,2,0:T(8,128)(2,1)} fusion(bf16[2,512,4,96]{1,3,2,0:T(8,128)(2,1)} %get-tuple-element.161, s32[]{:T(128)} %get-tuple-element.160, bf16[1024,4,96]{0,2,1:T(8,128)(2,1)} %get-tuple-element.179, f32[4,512,1024]{2,1,0:T(8,128)} %get-tuple-element.146, f32[4,512]{1,0:T(4,128)} %get-tuple-element.147), kind=kOutput, calls=%fused_computation.11.clone.1 | convolution fusion | flops 407044096 | bytes 9576960 | tf_op jit(solution)/shard_map/while/body/eval_jaxpr/hqk,khd->qhd/dot_general | solution.py:87
  124.0 2.4 %copy.19 = bf16[2,512,4,96]{3,2,1,0:T(4,128)(2,1)} copy(bf16[2,512,4,96]{1,3,2,0:T(8,128)(2,1)} %get-tuple-element.47) | data formatting | bytes 1572864 | tf_op jit(solution)/shard_map/while | solution.py:91
  126.3 2.7 %reshape.79 = bf16[32,32,384]{2,1,0:T(8,128)(2,1)} reshape(bf16[2,512,4,96]{3,2,1,0:T(4,128)(2,1)} %copy.19) | data formatting | bytes 1572864 | tf_op jit(solution)/shard_map/reshape | solution.py:91
  129.1 2.4 %fusion.40 = bf16[32,32,384]{2,1,0:T(8,128)(2,1)} fusion(s32[]{:T(128)S(6)} %select_n.47, bf16[32,32,384]{2,1,0:T(8,128)(2,1)} %reshape.79), kind=kLoop, calls=%fused_computation.62 | loop fusion | flops 393216 | bytes 1572868 | tf_op jit(solution)/shard_map/jit(_roll_dynamic)/concatenate | solution.py:94
  131.5 4.2 %all-to-all-start = ((bf16[32,32,384]{2,1,0:T(8,128)(2,1)}), bf16[32,32,384]{2,1,0:T(8,128)(2,1)}, u32[]{:S(2)}, u32[]{:S(2)}) async-start(bf16[32,32,384]{2,1,0:T(8,128)(2,1)} %fusion.40), calls=%async_computation | async-start | bytes 1572864 | tf_op jit(solution)/shard_map/all_to_all | solution.py:95
  136.8 10.6 %all-to-all-done = bf16[32,32,384]{2,1,0:T(8,128)(2,1)} async-done(((bf16[32,32,384]{2,1,0:T(8,128)(2,1)}), bf16[32,32,384]{2,1,0:T(8,128)(2,1)}, u32[]{:S(2)}, u32[]{:S(2)}) %all-to-all-start) | async-done | bytes 786464 | tf_op jit(solution)/shard_map/all_to_all | solution.py:95
  147.4 4.5 %fusion.33 = bf16[256,1536]{1,0:T(8,128)(2,1)S(1)} fusion(bf16[256,4,384]{2,0,1:T(8,128)(2,1)} %bitcast.23, bf16[4,384,1536]{2,1,0:T(8,128)(2,1)} %bitcast.77), kind=kOutput, calls=%fused_computation.45 | convolution fusion | flops 1210712064 | bytes 6291456 | tf_op jit(solution)/shard_map/tgk,gke->tge/dot_general | solution.py:98
  153.0 1.5 collective-permute-start.1
  155.8 18.4 %collective-permute-done.1 = bf16[8,32,1536]{2,1,0:T(8,128)(2,1)} collective-permute-done((bf16[8,32,1536]{2,1,0:T(8,128)(2,1)}, bf16[8,32,1536]{2,1,0:T(8,128)(2,1)}, u32[]{:S(2)}, u32[]{:S(2)}) %collective-permute-start.1) | collective-permute-done | bytes 786464 | tf_op jit(solution)/shard_map/ppermute | solution.py:13
  174.2 1.7 fusion.39
  175.9 1.5 collective-permute-start.2
  177.4 16.7 %collective-permute-done.2 = bf16[8,32,1536]{2,1,0:T(8,128)(2,1)S(1)} collective-permute-done((bf16[8,32,1536]{2,1,0:T(8,128)(2,1)S(1)}, bf16[8,32,1536]{2,1,0:T(8,128)(2,1)S(1)}, u32[]{:S(2)}, u32[]{:S(2)}) %collective-permute-start.2) | collective-permute-done | bytes 786464 | tf_op jit(solution)/shard_map/ppermute | solution.py:13
  (28 shorter events, 8.5 us)
Async XLA Ops:
  6.5 56.8 %copy-start = (bf16[1,1536,4,288]{1,3,2,0:T(8,128)(2,1)S(1)}, bf16[1,1536,4,288]{1,3,2,0:T(8,128)(2,1)}, u32[]{:S(2)}) copy-start(bf16[1,1536,4,288]{1,3,2,0:T(8,128)(2,1)} %param.14) | copy-start | bytes 10616836
  6.5 56.8 %all-gather.2.cloned.1.call-start = ((), (), s32[]{:S(2)}) async-start(), calls=%async_computation.1 | async-start | bytes 3932160 | tf_op jit(solution)/shard_map/all_gather | solution.py:56
  6.5 22.2 %collective-permute-start = (bf16[8,32,1536]{2,1,0:T(8,128)(2,1)}, bf16[8,32,1536]{2,1,0:T(8,128)(2,1)}, u32[]{:S(2)}, u32[]{:S(2)}) collective-permute-start(bf16[8,32,1536]{2,1,0:T(8,128)(2,1)} %bitcast.74), channel_id=1, source_target_pairs={{4,0},{8,4},{12,8},{0,12},{5,1},{9,5},{13,9},{1,13},{6,2},{10,6},{... | collective-permute-start | bytes 2359304 | tf_op jit(solution)/shard_map/ppermute | solution.py:13
  30.5 0.9 copy-start.1
  84.3 6.7 %copy-start.3 = (f32[1,4]{1,0:T(1,128)S(1)}, f32[1,4]{1,0:T(1,128)}, u32[]{:S(2)}) copy-start(f32[1,4]{1,0:T(1,128)} %param.15) | copy-start | bytes 52
  131.5 15.9 %all-to-all-start = ((bf16[32,32,384]{2,1,0:T(8,128)(2,1)}), bf16[32,32,384]{2,1,0:T(8,128)(2,1)}, u32[]{:S(2)}, u32[]{:S(2)}) async-start(bf16[32,32,384]{2,1,0:T(8,128)(2,1)} %fusion.40), calls=%async_computation | async-start | bytes 1572864 | tf_op jit(solution)/shard_map/all_to_all | solution.py:95
  147.4 4.5 %copy-start.2 = (bf16[8,32,1536]{2,1,0:T(8,128)(2,1)S(1)}, bf16[8,32,1536]{2,1,0:T(8,128)(2,1)}, u32[]{:S(2)}) copy-start(bf16[8,32,1536]{2,1,0:T(8,128)(2,1)} %copy-done.1) | copy-start | bytes 2359300
  153.0 21.2 %collective-permute-start.1 = (bf16[8,32,1536]{2,1,0:T(8,128)(2,1)}, bf16[8,32,1536]{2,1,0:T(8,128)(2,1)}, u32[]{:S(2)}, u32[]{:S(2)}) collective-permute-start(bf16[8,32,1536]{2,1,0:T(8,128)(2,1)} %fusion.38), channel_id=1, source_target_pairs={{12,0},{0,4},{4,8},{8,12},{13,1},{1,5},{5,9},{9,13},{14,2},{2,6},{... | collective-permute-start | bytes 2359304 | tf_op jit(solution)/shard_map/ppermute | solution.py:13
  175.9 18.2 %collective-permute-start.2 = (bf16[8,32,1536]{2,1,0:T(8,128)(2,1)S(1)}, bf16[8,32,1536]{2,1,0:T(8,128)(2,1)S(1)}, u32[]{:S(2)}, u32[]{:S(2)}) collective-permute-start(bf16[8,32,1536]{2,1,0:T(8,128)(2,1)S(1)} %fusion.39), channel_id=1, source_target_pairs={{16,0},{0,16},{17,1},{1,17},{18,2},{2,18},{19,3},{3,19},{20,4},{4,... | collective-permute-start | bytes 2359304 | tf_op jit(solution)/shard_map/ppermute | solution.py:13
Sparse Core Ops, SparseCore 0:
  32.8 30.5 all-gather.1
where the time goes:
time: 202 us
  waiting for transfers between devices  84.3 us (42%)
  matrix products  42.9 us (21%)
  other arithmetic  21.6 us (11%)
  between operations  20.4 us (10%)
  local copies, waits for them, and re-layouts  19.2 us (10%)
  starting transfers between devices  12.3 us (6%)
    ppermute x3, waiting for transfers between devices, passed_along(): return lax.ppermute(block, axis, route)  46.1 us
    all_gather x1, waiting for transfers between devices, shards(): shard_rows = lax.all_gather(normed, 'seq', axis=0, tiled=True)  27.6 us
    sub x2, matrix products, attend(): lifted = jnp.exp(scores - row_max)  16.4 us
    dot_general x2, matrix products, attend(): jnp.einsum('hqk,khd->qhd', probabilities, value_rows, preferred_element_t...  11.6 us
    all_to_all x1, waiting for transfers between devices, shards(): lax.all_to_all(heads_out, 'seq', split_axis=0, concat_axis=2, tiled=True)  10.6 us
    while x4, local copies, waits for them, and re-layouts, shards(): lax.map(attend, lax.iota(jnp.int32, block_count))  9.04 us
    ppermute x3, starting transfers between devices, passed_along(): return lax.ppermute(block, axis, route)  8.09 us
    dot_general x1, matrix products, shards(): jnp.dot(shard_rows.reshape(-1, model_width), weights, preferred_element_t...  6.94 us
  transfers between devices with their start and end apart: 5, of which 5 were waited for; matrix products, arithmetic and copies ran while one was open for 2% of the time, Pallas kernels for 0%

commit v1 on v0

v1 whole, which is shorter than its diff:
```python
import functools
import math

import jax
import jax.numpy as jnp
from jax import lax
from jax.experimental import pallas as pl
from jax.experimental.pallas import tpu as pltpu
from jax.sharding import PartitionSpec as P

eps_norm = 1e-06
lane = 128
far = 1e30
constant_shift_scale = 32.0

SMEM = pl.BlockSpec(memory_space=pltpu.SMEM)
VMEM = pl.BlockSpec(memory_space=pltpu.VMEM)


small = pl.CostEstimate(flops=1, bytes_accessed=1, transcendentals=0)


def params(mib=40):
    return pltpu.CompilerParams(vmem_limit_bytes=mib << 20)


def passed_along(block, axis, distance):
    n = lax.axis_size(axis)
    return lax.ppermute(block, axis, [(i, (i + distance) % n) for i in range(n)])


def swapped(block, axis, mask):
    return lax.ppermute(block, axis, [(i, i ^ mask) for i in range(lax.axis_size(axis))])


def normalise(x, scale_row, shift_row):
    x = x - jnp.mean(x, -1, keepdims=True)
    variance = jnp.mean(x * x, -1, keepdims=True)
    return (x * lax.rsqrt(variance + eps_norm) * scale_row + shift_row).astype(jnp.bfloat16)


def local_half_kernel(ints, tile, shift, scale, out):
    rows, cols, _ = tile.shape
    half = cols // 2
    level, lon = ints[0], ints[2]
    first = pl.multiple_of(jnp.where(lon > half, 0, half), half)
    shift_row, scale_row = shift[pl.ds(level, 1), :], scale[pl.ds(level, 1), :]
    for r in range(rows):
        x = tile[r, pl.ds(first, half), :].astype(jnp.float32)
        out[r] = normalise(x, scale_row, shift_row)


def mixed_half(r, lon, tile, left, right):
    rows, cols, _ = tile.shape
    half = cols // 2
    big = lon > half
    first = pl.multiple_of(jnp.where(big, half, 0), half)
    column = lax.broadcasted_iota(jnp.int32, (half, 1), 0) + first
    far_side = jnp.where(big, (column >= lon).astype(jnp.int32), (column < lon).astype(jnp.int32)) == 1
    bigs = jnp.full((half, 1), lon, jnp.int32) > half
    own = tile[r, pl.ds(first, half), :].astype(jnp.float32)
    other = jnp.where(bigs, left[r].astype(jnp.float32), right[r].astype(jnp.float32))
    return jnp.where(far_side, other, own)


def mixed_half_kernel(ints, tile, left, right, shift, scale, out):
    rows = tile.shape[0]
    level, lon = ints[0], ints[2]
    shift_row, scale_row = shift[pl.ds(level, 1), :], scale[pl.ds(level, 1), :]
    for r in range(rows):
        x = mixed_half(r, lon, tile, left, right)
        out[r] = normalise(x, scale_row, shift_row)


def project_kernel(count, half, size, ints, places, fast, scales, *refs):
    pieces, weight, out = refs[:count], refs[count], refs[count + 1]
    tokens, padded, query_extra, key_extra = refs[count + 2 :]
    piece_rows = pieces[0].shape[0]
    group = weight.shape[0]
    total = tokens.shape[0]
    step = pl.program_id(0)

    @pl.when(step == 0)
    def _():
        padded[...] = jnp.zeros_like(padded)
        for j in range(count):
            tokens[pl.ds(pl.multiple_of(places[j] * piece_rows, piece_rows), piece_rows), :] = pieces[j][...]
        row = lax.broadcasted_iota(jnp.int32, (total, lane), 0) // half
        column = lax.broadcasted_iota(jnp.int32, (total, lane), 1)
        low = jnp.where(row < ints[1], 1.0, 0.0)
        query_extra[...] = jnp.where(
            column == size, low, jnp.where(column == size + 1, 1.0 - low, jnp.where(column == size + 2, 1.0, 0.0))
        )
        key_extra[...] = jnp.where(
            column == size,
            far * (low - 1.0),
            jnp.where(column == size + 1, -far * low, jnp.where(column == size + 2, -1.0, 0.0)),
        )

    for g in range(group):
        for i in range(3):
            begin = (3 * g + i) * lane
            padded[begin : begin + size, :] = weight[g, i * size : (i + 1) * size, :]
    mixture = lax.dot_general(
        tokens[...], padded[...], (((1,), (1,)), ((), ())), preferred_element_type=jnp.float32
    )
    ones = jnp.where(lax.broadcasted_iota(jnp.int32, (1, lane), 1) == size, 1.0, 0.0)
    for g in range(group):
        strength = jnp.where(fast[0] == 1, scales[step * group + g] * math.log2(math.e), 1.0)
        query, key, value = (mixture[:, (3 * g + i) * lane : (3 * g + i + 1) * lane] for i in range(3))
        query = query * (lax.rsqrt(jnp.sum(query * query, -1, keepdims=True) + eps_norm) * strength) + query_extra[...]
        key = key * lax.rsqrt(jnp.sum(key * key, -1, keepdims=True) + eps_norm) + key_extra[...] * strength
        out[g, 0] = query.astype(jnp.bfloat16)
        out[g, 1] = key.astype(jnp.bfloat16)
        out[g, 2] = (value + ones).astype(jnp.bfloat16)


def attend_kernel(size, places, fast, scales, queries, first, second, out, held):
    head = pl.program_id(0)
    heads, total = held.shape[0], held.shape[1]
    count, piece_rows, _ = out.shape
    halves = (first, second)
    contract = (((1,), (1,)), ((), ()))
    block = math.gcd(total, 256)

    def body(with_max):
        for begin in range(0, total, block):
            query = queries[0, 0, begin : begin + block, :]
            scores = [
                lax.dot_general(query, part[0, 1], contract, preferred_element_type=jnp.float32) for part in halves
            ]
            if with_max:
                strength = scales[head] * math.log2(math.e)
                top = jnp.maximum(jnp.max(scores[0], -1, keepdims=True), jnp.max(scores[1], -1, keepdims=True))
                scores = [(s - top) * strength for s in scores]
            mixed = sum(
                jnp.dot(jnp.exp2(s).astype(jnp.bfloat16), part[0, 2], preferred_element_type=jnp.float32)
                for s, part in zip(scores, halves)
            )
            held[head, begin : begin + block, :] = mixed[:, :size] / mixed[:, size : size + 1]

    @pl.when(fast[0] == 1)
    def _():
        body(False)

    @pl.when(fast[0] == 0)
    def _():
        body(True)

    @pl.when(head == heads - 1)
    def _():
        for j in range(count):
            rows = pl.ds(pl.multiple_of(places[j] * piece_rows, piece_rows), piece_rows)
            out[j] = jnp.concatenate([held[h, rows, :] for h in range(heads)], -1).astype(jnp.bfloat16)


def finish_kernel(count, mixed, ints, places, *refs):
    if mixed:
        tile, left, right = refs[:3]
        refs = refs[3:]
    else:
        tile = refs[0]
        refs = refs[1:]
    pieces, weight, gate, out = refs[:count], refs[count], refs[count + 1], refs[count + 2]
    inner = pieces[0].shape[-1]
    rows, cols, _ = tile.shape
    half = cols // 2
    level, lon = ints[0], ints[2]
    total = 0.0
    for j in range(count):
        begin = pl.multiple_of(places[j] * inner, inner)
        total = total + jnp.dot(pieces[j][...], weight[pl.ds(begin, inner), :], preferred_element_type=jnp.float32)
    branch = gate[pl.ds(level, 1), :] * total.astype(jnp.bfloat16).astype(jnp.float32)
    first = pl.multiple_of(jnp.where(lon > half, 0, half), half)
    for r in range(rows):
        if mixed:
            residual = mixed_half(r, lon, tile, left, right)
        else:
            residual = tile[r, pl.ds(first, half), :].astype(jnp.float32)
        out[r] = (residual + branch[r * half : (r + 1) * half]).astype(jnp.bfloat16)


def shards(
    latents, timesteps, offsets, qkv_weight, logit_scale, out_weight, mod_shift, mod_scale, mod_gate
):
    tile = latents[0]
    rows, cols, width = tile.shape
    half = cols // 2
    heads = qkv_weight.shape[2]
    size = qkv_weight.shape[3] // 3
    inner = heads * size
    n = lax.axis_size("seq")
    me = lax.axis_index("seq")
    masks = [0]
    bits = [1 << i for i in range(n.bit_length() - 1)]
    for bit in reversed(bits):
        masks = masks + [m | bit for m in masks]
    places = jnp.bitwise_xor(me, jnp.asarray(masks, jnp.int32))
    lat, lon = offsets[0, 0], offsets[0, 1]
    ints = jnp.stack([timesteps[0], lat, lon])
    scales = logit_scale[0]
    fast = (jnp.max(scales) <= constant_shift_scale).astype(jnp.int32)[None]
    shift, scale, gate = mod_shift[0], mod_scale[0], mod_gate[0]
    piece_rows = rows * half
    half_tokens = n * piece_rows

    right = passed_along(tile[:, :half], "win", -1)
    left = passed_along(tile[:, half:], "win", 1)

    weight = jnp.transpose(qkv_weight[0], (1, 2, 0))
    group = 2 if heads % 2 == 0 else 1

    def gathered(piece):
        pieces = [piece]
        for bit in reversed(bits):
            pieces = pieces + [swapped(p, "seq", bit) for p in pieces]
        return pieces

    def projected(pieces):
        return pl.pallas_call(
            functools.partial(project_kernel, n, half, size),
            grid=(heads // group,),
            out_shape=jax.ShapeDtypeStruct((heads, 3, half_tokens, lane), jnp.bfloat16),
            in_specs=[SMEM, SMEM, SMEM, SMEM]
            + [pl.BlockSpec((piece_rows, width), lambda h: (0, 0))] * n
            + [pl.BlockSpec((group, 3 * size, width), lambda h: (h, 0, 0))],
            out_specs=pl.BlockSpec((group, 3, half_tokens, lane), lambda h: (h, 0, 0, 0)),
            scratch_shapes=[
                pltpu.VMEM((half_tokens, width), jnp.bfloat16),
                pltpu.VMEM((group * 3 * lane, width), jnp.bfloat16),
                pltpu.VMEM((half_tokens, lane), jnp.float32),
                pltpu.VMEM((half_tokens, lane), jnp.float32),
            ],
            compiler_params=params(),
            cost_estimate=small,
            name="project",
        )(ints, places, fast, scales, *[p.reshape(piece_rows, width) for p in pieces], weight)

    half_shape = jax.ShapeDtypeStruct((rows, half, width), jnp.bfloat16)
    local = pl.pallas_call(
        local_half_kernel,
        out_shape=half_shape,
        in_specs=[SMEM, VMEM, VMEM, VMEM],
        out_specs=VMEM,
        compiler_params=params(),
        cost_estimate=small,
        name="norm_local",
    )(ints, tile, shift, scale)
    local_pieces = gathered(local)
    mixed = pl.pallas_call(
        mixed_half_kernel,
        out_shape=half_shape,
        in_specs=[SMEM, VMEM, VMEM, VMEM, VMEM, VMEM],
        out_specs=VMEM,
        compiler_params=params(),
        cost_estimate=small,
        name="norm_mixed",
    )(ints, tile, left, right, shift, scale)
    mixed_pieces = gathered(mixed)
    local_heads = projected(local_pieces)
    mixed_heads = projected(mixed_pieces)

    def attended(own, first, second):
        whole = pl.BlockSpec((1, 3, half_tokens, lane), lambda h, *_: (h, 0, 0, 0))
        return pl.pallas_call(
            functools.partial(attend_kernel, size),
            grid_spec=pltpu.PrefetchScalarGridSpec(
                num_scalar_prefetch=3,
                grid=(heads,),
                in_specs=[
                    pl.BlockSpec((1, 1, half_tokens, lane), lambda h, *_: (h, 0, 0, 0)),
                    whole,
                    whole,
                ],
                out_specs=pl.BlockSpec((n, piece_rows, inner), lambda h, *_: (0, 0, 0)),
                scratch_shapes=[pltpu.VMEM((heads, half_tokens, size), jnp.float32)],
            ),
            out_shape=jax.ShapeDtypeStruct((n, piece_rows, inner), jnp.bfloat16),
            compiler_params=params(),
            cost_estimate=small,
            name="attend",
        )(places, fast, scales, own, first, second)

    def hop(held, bit):
        middle = held.shape[1] // 2
        return held[:, :middle], swapped(held[:, middle:], "seq", bit)

    def returned(held):
        held = jnp.concatenate(held, 0)
        for bit in bits[1:]:
            held = jnp.concatenate(hop(held, bit), 0)
        return [held[g, 0] for g in range(n)]

    order = [0]
    for bit in bits:
        order = order + [m | bit for m in order]
    sources = jnp.bitwise_xor(me, jnp.asarray(order, jnp.int32))

    def finished(groups, extra, is_mixed):
        block = width // 3 if width % (3 * lane) == 0 else width
        sides = pl.BlockSpec((rows, half, block), lambda i: (0, 0, i))
        return pl.pallas_call(
            functools.partial(finish_kernel, n, is_mixed),
            grid=(width // block,),
            out_shape=half_shape,
            in_specs=[SMEM, SMEM, pl.BlockSpec((rows, cols, block), lambda i: (0, 0, i))]
            + [sides] * len(extra)
            + [pl.BlockSpec((piece_rows, inner), lambda i: (0, 0))] * n
            + [pl.BlockSpec((width, block), lambda i: (0, i)), pl.BlockSpec((gate.shape[0], block), lambda i: (0, i))],
            out_specs=sides,
            compiler_params=params(),
            cost_estimate=small,
            name="finish",
        )(ints, sources, tile, *extra, *groups, out_weight[0], gate)

    mixed_kept, mixed_received = hop(attended(mixed_heads, local_heads, mixed_heads)[None], bits[0])
    local_query, mixed_received = lax.optimization_barrier((local_heads, mixed_received))
    mixed_out = returned((mixed_kept, mixed_received))
    local_out = returned(hop(attended(local_query, local_query, mixed_heads)[None], bits[0]))
    mixed_done = finished(mixed_out, [left, right], True)
    up = passed_along(mixed_done, "win", 1)
    down = passed_along(mixed_done, "win", -1)
    local_done = finished(local_out, [], False)
    local_sent = passed_along(local_done, "segment", 1)
    big = lon > half
    column = lax.iota(jnp.int32, half) + jnp.where(big, half, 0)
    far_side = jnp.where(big, column >= lon, column < lon)
    mixed_back = jnp.where(far_side[None, :, None], jnp.where(big, down, up), mixed_done)
    mixed_sent = passed_along(mixed_back, "segment", 1)
    source_lon = passed_along(offsets, "segment", 1)[0, 1]
    source_big = source_lon > half
    low = jnp.where(source_big, local_sent, mixed_sent)
    high = jnp.where(source_big, mixed_sent, local_sent)
    return jnp.concatenate([low, high], axis=1)[None]


def solution(mesh):
    in_specs = (
        P("segment", "seq", "win", None),
        P("segment"),
        P("segment", None),
        P("segment", None, "seq", None),
        P("segment", "seq"),
        P("segment", None, None),
        P("segment", None, None),
        P("segment", None, None),
        P("segment", None, None),
    )
    out_specs = P("segment", "seq", "win", None)
    return jax.shard_map(shards, mesh=mesh, in_specs=in_specs, out_specs=out_specs, check_vma=False)
```

time: 202 us -> 97.3 us (0.48)
  matrix products: 42.9 us -> 0 us
  waiting for transfers between devices: 84.3 us -> 42.8 us
  Pallas kernels: 0 us -> 26.1 us
  other arithmetic: 21.6 us -> 3.6 us
  between operations: 20.4 us -> 2.83 us
  local copies, waits for them, and re-layouts: 19.2 us -> 4.62 us
  starting transfers between devices: 12.3 us -> 17.1 us
    all_gather x1 -> x0, waiting for transfers between devices: 27.6 us -> none  [shards(): shard_rows = lax.all_gather(normed, 'seq', axis=0, tiled=True)]
    dot_general x7 -> x0, matrix products: 26.5 us -> none  [the longest x2 11.6 us: attend(): jnp.einsum('hqk,khd->qhd', probabilities, value_rows, preferred_element_t...]
    pallas_call x0 -> x8, Pallas kernels: none -> 26.1 us  [the longest x2 10.8 us: attended(): pl.pallas_call(functools.partial(attend_kernel, size), grid_spec=pltpu.Pr...]
    sub x2 -> x0, matrix products: 16.4 us -> none  [attend(): lifted = jnp.exp(scores - row_max)]
    concatenate x3 -> x2, other arithmetic: 10.9 us -> 0.05 us  [returned(): held = jnp.concatenate(held, 0)]
    all_to_all x1 -> x0, waiting for transfers between devices: 10.6 us -> none  [shards(): lax.all_to_all(heads_out, 'seq', split_axis=0, concat_axis=2, tiled=True)]
    while x4 -> x0, local copies, waits for them, and re-layouts: 9.04 us -> none  [shards(): lax.map(attend, lax.iota(jnp.int32, block_count))]
    ppermute x3 -> x17, starting transfers between devices: 8.09 us -> 17.1 us  [the longest x7 10.8 us: passed_along(): lax.ppermute(block, axis, [(i, (i + distance) % n) for i in range(n)])]
  transfers between devices with their start and end apart: 5 -> 17, of which waited for: 5 -> 8; matrix products, arithmetic and copies ran while one was open for 2% -> 3% of each run, Pallas kernels for 0% -> 17%
where the time goes in v1:
time: 97.3 us; the launch traced here: 97 us
  waiting for transfers between devices  42.8 us (44%)
  Pallas kernels  26.1 us (27%)
  starting transfers between devices  17.1 us (18%)
  local copies, waits for them, and re-layouts  4.62 us (5%)
  other arithmetic  3.6 us (4%)
  between operations  2.83 us (3%)
    ppermute x7, waiting for transfers between devices, passed_along(): lax.ppermute(block, axis, [(i, (i + distance) % n) for i in range(n)])  27.4 us
    ppermute x10, waiting for transfers between devices, swapped(): lax.ppermute(block, axis, [(i, i ^ mask) for i in range(lax.axis_size(axi...  15.4 us
    ppermute x7, starting transfers between devices, passed_along(): lax.ppermute(block, axis, [(i, (i + distance) % n) for i in range(n)])  10.8 us
    pallas_call x2, Pallas kernels, attended(): pl.pallas_call(functools.partial(attend_kernel, size), grid_spec=pltpu.Pr...  10.8 us
    pallas_call x2, Pallas kernels, projected(): pl.pallas_call(functools.partial(project_kernel, n, half, size), grid=(he...  8.97 us
    ppermute x10, starting transfers between devices, swapped(): lax.ppermute(block, axis, [(i, i ^ mask) for i in range(lax.axis_size(axi...  6.27 us
    pallas_call x2, Pallas kernels, finished(): pl.pallas_call(functools.partial(finish_kernel, n, is_mixed), grid=(width...  4.58 us
    unnamed x22, local copies, waits for them, and re-layouts  2.05 us
  transfers between devices with their start and end apart: 17, of which 8 were waited for; matrix products, arithmetic and copies ran while one was open for 3% of the time, Pallas kernels for 17%

profile of v1, /device:TPU:0, one launch (start us, length us, event | category | flops | bytes accessed | tf_op | source)
XLA Modules:
  0.0 97.0 jit_solution(12872605852451025217)
XLA Ops:
  0.0 1.3 %fusion = (bf16[8,16,1536]{2,1,0:T(8,128)(2,1)S(1)}, bf16[8,16,1536]{2,1,0:T(8,128)(2,1)S(1)}) fusion(bf16[8,32,1536]{2,1,0:T(8,128)(2,1)} %bitcast.42), kind=kLoop, calls=%fused_computation.18 | loop fusion | bytes 1572864 | tf_op jit(solution)/shard_map/slice | solution.py:207
  1.3 3.1 %collective-permute-start.4 = (bf16[8,16,1536]{2,1,0:T(8,128)(2,1)S(1)}, bf16[8,16,1536]{2,1,0:T(8,128)(2,1)S(1)}, u32[]{:S(2)}, u32[]{:S(2)}) collective-permute-start(bf16[8,16,1536]{2,1,0:T(8,128)(2,1)S(1)} %get-tuple-element.12), channel_id=1, source_target_pairs={{0,4},{4,8},{8,12},{12,0},{1,5},{5,9},{9,13},{13,1},{2,6},{6,10},{... | collective-permute-start | bytes 1179656 | tf_op jit(solution)/shard_map/ppermute | solution.py:29
  4.4 2.1 %collective-permute-start.5 = (bf16[8,16,1536]{2,1,0:T(8,128)(2,1)S(1)}, bf16[8,16,1536]{2,1,0:T(8,128)(2,1)S(1)}, u32[]{:S(2)}, u32[]{:S(2)}) collective-permute-start(bf16[8,16,1536]{2,1,0:T(8,128)(2,1)S(1)} %get-tuple-element.11), channel_id=1, source_target_pairs={{0,12},{4,0},{8,4},{12,8},{1,13},{5,1},{9,5},{13,9},{2,14},{6,2},{... | collective-permute-start | bytes 1179656 | tf_op jit(solution)/shard_map/ppermute | solution.py:29
  7.7 1.3 %pad_add_fusion.ints = s32[3]{0:T(128)S(1)} fusion(s32[1]{0:T(128)} %bitcast.2, s32[1]{0:T(128)} %bitcast.1, s32[1]{0:T(128)S(6)} %copy.12), kind=kLoop, calls=%fused_computation.15 | loop fusion | flops 6 | bytes 24 | tf_op jit(solution)/shard_map/stack | solution.py:200
  9.0 0.9 norm_local.1
  9.9 1.7 %collective-permute-start.1 = (bf16[8,16,1536]{2,1,0:T(8,128)(2,1)S(1)}, bf16[8,16,1536]{2,1,0:T(8,128)(2,1)S(1)}, u32[]{:S(2)}, u32[]{:S(2)}) collective-permute-start(bf16[8,16,1536]{2,1,0:T(8,128)(2,1)S(1)} %norm_local.1), channel_id=1, source_target_pairs={{0,2},{1,3},{2,0},{3,1},{4,6},{5,7},{6,4},{7,5},{8,10},{9,11},{10,... | collective-permute-start | bytes 1179656 | tf_op jit(solution)/shard_map/ppermute | solution.py:33
  11.6 4.8 %collective-permute-done.4.left.refs_1_ = bf16[8,16,1536]{2,1,0:T(8,128)(2,1)S(1)} collective-permute-done((bf16[8,16,1536]{2,1,0:T(8,128)(2,1)S(1)}, bf16[8,16,1536]{2,1,0:T(8,128)(2,1)S(1)}, u32[]{:S(2)}, u32[]{:S(2)}) %collective-permute-start.4) | collective-permute-done | bytes 393248 | tf_op jit(solution)/shard_map/ppermute | solution.py:29
  16.4 7.0 %collective-permute-done.5.right.refs_2_ = bf16[8,16,1536]{2,1,0:T(8,128)(2,1)S(1)} collective-permute-done((bf16[8,16,1536]{2,1,0:T(8,128)(2,1)S(1)}, bf16[8,16,1536]{2,1,0:T(8,128)(2,1)S(1)}, u32[]{:S(2)}, u32[]{:S(2)}) %collective-permute-start.5) | collective-permute-done | bytes 393248 | tf_op jit(solution)/shard_map/ppermute | solution.py:29
  23.4 0.9 norm_mixed.1
  24.3 1.6 %collective-permute-start.6 = (bf16[8,16,1536]{2,1,0:T(8,128)(2,1)S(1)}, bf16[8,16,1536]{2,1,0:T(8,128)(2,1)S(1)}, u32[]{:S(2)}, u32[]{:S(2)}) collective-permute-start(bf16[8,16,1536]{2,1,0:T(8,128)(2,1)S(1)} %norm_mixed.1), channel_id=1, source_target_pairs={{0,2},{1,3},{2,0},{3,1},{4,6},{5,7},{6,4},{7,5},{8,10},{9,11},{10,... | collective-permute-start | bytes 1179656 | tf_op jit(solution)/shard_map/ppermute | solution.py:33
  26.4 8.4 %collective-permute-done.6 = bf16[8,16,1536]{2,1,0:T(8,128)(2,1)S(1)} collective-permute-done((bf16[8,16,1536]{2,1,0:T(8,128)(2,1)S(1)}, bf16[8,16,1536]{2,1,0:T(8,128)(2,1)S(1)}, u32[]{:S(2)}, u32[]{:S(2)}) %collective-permute-start.6) | collective-permute-done | bytes 393248 | tf_op jit(solution)/shard_map/ppermute | solution.py:33
  34.8 0.6 reduce_max.9
  36.6 2.0 %copy-done.1 = bf16[1,1536,4,288]{1,3,2,0:T(8,128)(2,1)S(1)} copy-done((bf16[1,1536,4,288]{1,3,2,0:T(8,128)(2,1)S(1)}, bf16[1,1536,4,288]{1,3,2,0:T(8,128)(2,1)}, u32[]{:S(2)}) %copy-start.1) | copy-done | bytes 3538968
  38.6 4.4 %project.2.first.queries = bf16[4,3,512,128]{3,2,1,0:T(8,128)(2,1)S(1)} custom-call(s32[3]{0:T(128)S(1)} %pad_add_fusion.ints, s32[4]{0:T(128)S(1)} %broadcast_xor_fusion.places, s32[1]{0:T(128)} %bitcast.4.fast, f32[4]{0:T(128)S(1)} %bitcast.68, bf16[128,1536]{1,0:T(8,128)(2,1)S(1)} %bitcast.58, bf16[128,1536]{1,0:T(8,128)(2,1)S(1)} %bitcast.65, ...), custom_call_target="tpu_custom_call" | custom-call | flops 1 | bytes 1 | tf_op jit(solution)/shard_map/project/pallas_call | solution.py:220
  43.1 4.6 %project.3.queries.second = bf16[4,3,512,128]{3,2,1,0:T(8,128)(2,1)S(1)} custom-call(s32[3]{0:T(128)S(1)} %pad_add_fusion.ints, s32[4]{0:T(128)S(1)} %broadcast_xor_fusion.places, s32[1]{0:T(128)} %bitcast.4.fast, f32[4]{0:T(128)S(1)} %bitcast.69, bf16[128,1536]{1,0:T(8,128)(2,1)S(1)} %bitcast.57, bf16[128,1536]{1,0:T(8,128)(2,1)S(1)} %bitcast.66, ...), custom_call_target="tpu_custom_call" | custom-call | flops 1 | bytes 1 | tf_op jit(solution)/shard_map/project/pallas_call | solution.py:220
  48.2 5.4 %attend.2 = bf16[4,128,384]{2,1,0:T(8,128)(2,1)S(1)} custom-call(s32[4]{0:T(128)S(1)} %broadcast_xor_fusion.places, s32[1]{0:T(128)} %bitcast.4.fast, f32[4]{0:T(128)S(1)} %bitcast.70, bf16[4,3,512,128]{3,2,1,0:T(8,128)(2,1)S(1)} %project.3.queries.second, bf16[4,3,512,128]{3,2,1,0:T(8,128)(2,1)S(1)} %project.2.first.queries, ...), custom_call_target="tpu_custom_call" | custom-call | flops 1 | bytes 1 | tf_op jit(solution)/shard_map/attend/pallas_call | solution.py:265
  54.3 1.1 %collective-permute-done.9 = bf16[1,2,128,384]{3,2,1,0:T(8,128)(2,1)S(1)} collective-permute-done((bf16[1,2,128,384]{3,2,1,0:T(8,128)(2,1)S(1)}, bf16[1,2,128,384]{3,2,1,0:T(8,128)(2,1)S(1)}, u32[]{:S(2)}, u32[]{:S(2)}) %collective-permute-start.9) | collective-permute-done | bytes 196640 | tf_op jit(solution)/shard_map/ppermute | solution.py:33
  55.4 0.9 collective-permute-start.13
  56.3 5.4 %attend.3 = bf16[4,128,384]{2,1,0:T(8,128)(2,1)S(1)} custom-call(s32[4]{0:T(128)S(1)} %broadcast_xor_fusion.places, s32[1]{0:T(128)} %bitcast.4.fast, f32[4]{0:T(128)S(1)} %bitcast.71, bf16[4,3,512,128]{3,2,1,0:T(8,128)(2,1)S(1)} %project.2.first.queries, bf16[4,3,512,128]{3,2,1,0:T(8,128)(2,1)S(1)} %project.2.first.queries, ...), custom_call_target="tpu_custom_call" | custom-call | flops 1 | bytes 1 | tf_op jit(solution)/shard_map/attend/pallas_call | solution.py:265
  61.9 0.8 collective-permute-done.13
  62.7 2.3 %finish.3 = bf16[8,16,1536]{2,1,0:T(8,128)(2,1)S(1)} custom-call(s32[3]{0:T(128)S(1)} %pad_add_fusion.ints, s32[4]{0:T(128)S(1)} %iota_xor_fusion.places, bf16[8,32,1536]{2,1,0:T(8,128)(2,1)S(1)} %bitcast.45, bf16[8,16,1536]{2,1,0:T(8,128)(2,1)S(1)} %collective-permute-done.4.left.refs_1_, bf16[8,16,1536]{2,1,0:T(8,128)(2,1)S(1)} %collective-permute-done.5.right.refs_2_, ...), custom_call_target="tpu_custom_call" | custom-call | flops 1 | bytes 1 | tf_op jit(solution)/shard_map/finish/pallas_call | solution.py:302
  65.0 1.7 %collective-permute-start.14 = (bf16[8,16,1536]{2,1,0:T(8,128)(2,1)S(1)}, bf16[8,16,1536]{2,1,0:T(8,128)(2,1)S(1)}, u32[]{:S(2)}, u32[]{:S(2)}) collective-permute-start(bf16[8,16,1536]{2,1,0:T(8,128)(2,1)S(1)} %finish.3), channel_id=1, source_target_pairs={{0,12},{4,0},{8,4},{12,8},{1,13},{5,1},{9,5},{13,9},{2,14},{6,2},{... | collective-permute-start | bytes 1179656 | tf_op jit(solution)/shard_map/ppermute | solution.py:29
  67.1 0.9 collective-permute-start.11
  68.0 5.2 %collective-permute-done.11 = bf16[2,1,128,384]{3,2,1,0:T(8,128)(2,1)S(1)} collective-permute-done((bf16[2,1,128,384]{3,2,1,0:T(8,128)(2,1)S(1)}, bf16[2,1,128,384]{3,2,1,0:T(8,128)(2,1)S(1)}, u32[]{:S(2)}, u32[]{:S(2)}) %collective-permute-start.11) | collective-permute-done | bytes 196640 | tf_op jit(solution)/shard_map/ppermute | solution.py:33
  73.2 2.3 %finish.2 = bf16[8,16,1536]{2,1,0:T(8,128)(2,1)S(1)} custom-call(s32[3]{0:T(128)S(1)} %pad_add_fusion.ints, s32[4]{0:T(128)S(1)} %iota_xor_fusion.places, bf16[8,32,1536]{2,1,0:T(8,128)(2,1)S(1)} %bitcast.46, bf16[128,384]{1,0:T(8,128)(2,1)S(1)} %slice_bitcast_fusion.6.refs_1_, bf16[128,384]{1,0:T(8,128)(2,1)S(1)} %slice_bitcast_fusion.5.refs_2_, ...), custom_call_target="tpu_custom_call" | custom-call | flops 1 | bytes 1 | tf_op jit(solution)/shard_map/finish/pallas_call | solution.py:302
  75.5 1.4 %collective-permute-start.12 = (bf16[8,16,1536]{2,1,0:T(8,128)(2,1)S(1)}, bf16[8,16,1536]{2,1,0:T(8,128)(2,1)S(1)}, u32[]{:S(2)}, u32[]{:S(2)}) collective-permute-start(bf16[8,16,1536]{2,1,0:T(8,128)(2,1)S(1)} %finish.2), channel_id=1, source_target_pairs={{0,16},{16,0},{1,17},{17,1},{2,18},{18,2},{3,19},{19,3},{4,20},{20... | collective-permute-start | bytes 1179656 | tf_op jit(solution)/shard_map/ppermute | solution.py:29
  76.9 7.7 %collective-permute-done.15 = bf16[8,16,1536]{2,1,0:T(8,128)(2,1)S(1)} collective-permute-done((bf16[8,16,1536]{2,1,0:T(8,128)(2,1)S(1)}, bf16[8,16,1536]{2,1,0:T(8,128)(2,1)S(1)}, u32[]{:S(2)}, u32[]{:S(2)}) %collective-permute-start.15) | collective-permute-done | bytes 393248 | tf_op jit(solution)/shard_map/ppermute | solution.py:29
  84.8 1.3 %collective-permute-start.16 = (bf16[8,16,1536]{2,1,0:T(8,128)(2,1)S(1)}, bf16[8,16,1536]{2,1,0:T(8,128)(2,1)S(1)}, u32[]{:S(2)}, u32[]{:S(2)}) collective-permute-start(bf16[8,16,1536]{2,1,0:T(8,128)(2,1)S(1)} %select_select_fusion), channel_id=1, source_target_pairs={{0,16},{16,0},{1,17},{17,1},{2,18},{18,2},{3,19},{19,3},{4,20},{20... | collective-permute-start | bytes 1179656 | tf_op jit(solution)/shard_map/ppermute | solution.py:29
  86.1 0.8 collective-permute-start
  86.9 7.8 %collective-permute-done = s32[1,2]{1,0:T(1,128)S(1)} collective-permute-done((s32[1,2]{1,0:T(1,128)S(1)}, s32[1,2]{1,0:T(1,128)S(1)}, u32[]{:S(2)}, u32[]{:S(2)}) %collective-permute-start) | collective-permute-done | bytes 40 | tf_op jit(solution)/shard_map/ppermute | solution.py:29
  94.7 0.6 slice.69
  96.0 0.9 maximum_bitcast_fusion
  (54 shorter events, 3.2 us)
Async XLA Ops:
  0.0 8.9 %copy-start = (bf16[1,8,32,1536]{3,2,1,0:T(8,128)(2,1)S(1)}, bf16[1,8,32,1536]{3,2,1,0:T(8,128)(2,1)}, u32[]{:S(2)}) copy-start(bf16[1,8,32,1536]{3,2,1,0:T(8,128)(2,1)} %param.11) | copy-start | bytes 2359300
  0.0 7.1 %copy-start.7 = (s32[1,2]{1,0:T(1,128)S(1)}, s32[1,2]{1,0:T(1,128)}, u32[]{:S(2)}) copy-start(s32[1,2]{1,0:T(1,128)} %param.13) | copy-start | bytes 28
  0.0 8.9 %copy-start.4 = (f32[1,32,1536]{2,1,0:T(8,128)S(1)}, f32[1,32,1536]{2,1,0:T(8,128)}, u32[]{:S(2)}) copy-start(f32[1,32,1536]{2,1,0:T(8,128)} %param.17) | copy-start | bytes 589828
  0.0 8.9 %copy-start.5 = (f32[1,32,1536]{2,1,0:T(8,128)S(1)}, f32[1,32,1536]{2,1,0:T(8,128)}, u32[]{:S(2)}) copy-start(f32[1,32,1536]{2,1,0:T(8,128)} %param.18) | copy-start | bytes 589828
  1.3 15.1 %collective-permute-start.4 = (bf16[8,16,1536]{2,1,0:T(8,128)(2,1)S(1)}, bf16[8,16,1536]{2,1,0:T(8,128)(2,1)S(1)}, u32[]{:S(2)}, u32[]{:S(2)}) collective-permute-start(bf16[8,16,1536]{2,1,0:T(8,128)(2,1)S(1)} %get-tuple-element.12), channel_id=1, source_target_pairs={{0,4},{4,8},{8,12},{12,0},{1,5},{5,9},{9,13},{13,1},{2,6},{6,10},{... | collective-permute-start | bytes 1179656 | tf_op jit(solution)/shard_map/ppermute | solution.py:29
  4.4 19.0 %collective-permute-start.5 = (bf16[8,16,1536]{2,1,0:T(8,128)(2,1)S(1)}, bf16[8,16,1536]{2,1,0:T(8,128)(2,1)S(1)}, u32[]{:S(2)}, u32[]{:S(2)}) collective-permute-start(bf16[8,16,1536]{2,1,0:T(8,128)(2,1)S(1)} %get-tuple-element.11), channel_id=1, source_target_pairs={{0,12},{4,0},{8,4},{12,8},{1,13},{5,1},{9,5},{13,9},{2,14},{6,2},{... | collective-permute-start | bytes 1179656 | tf_op jit(solution)/shard_map/ppermute | solution.py:29
  9.8 24.9 %copy-start.6 = (f32[1,4]{1,0:T(1,128)S(1)}, f32[1,4]{1,0:T(1,128)}, u32[]{:S(2)}) copy-start(f32[1,4]{1,0:T(1,128)} %param.15) | copy-start | bytes 52
  9.8 26.7 %copy-start.8 = (s32[4]{0:T(128)S(1)}, s32[4]{0:T(128)}, u32[]{:S(2)}) copy-start(s32[4]{0:T(128)} %constant.18.clone) | copy-start | bytes 52
  9.9 16.0 %collective-permute-start.1 = (bf16[8,16,1536]{2,1,0:T(8,128)(2,1)S(1)}, bf16[8,16,1536]{2,1,0:T(8,128)(2,1)S(1)}, u32[]{:S(2)}, u32[]{:S(2)}) collective-permute-start(bf16[8,16,1536]{2,1,0:T(8,128)(2,1)S(1)} %norm_local.1), channel_id=1, source_target_pairs={{0,2},{1,3},{2,0},{3,1},{4,6},{5,7},{6,4},{7,5},{8,10},{9,11},{10,... | collective-permute-start | bytes 1179656 | tf_op jit(solution)/shard_map/ppermute | solution.py:33
  24.3 10.5 %collective-permute-start.6 = (bf16[8,16,1536]{2,1,0:T(8,128)(2,1)S(1)}, bf16[8,16,1536]{2,1,0:T(8,128)(2,1)S(1)}, u32[]{:S(2)}, u32[]{:S(2)}) collective-permute-start(bf16[8,16,1536]{2,1,0:T(8,128)(2,1)S(1)} %norm_mixed.1), channel_id=1, source_target_pairs={{0,2},{1,3},{2,0},{3,1},{4,6},{5,7},{6,4},{7,5},{8,10},{9,11},{10,... | collective-permute-start | bytes 1179656 | tf_op jit(solution)/shard_map/ppermute | solution.py:33
  25.8 10.8 %collective-permute-start.2 = (bf16[8,16,1536]{2,1,0:T(8,128)(2,1)S(1)}, bf16[8,16,1536]{2,1,0:T(8,128)(2,1)S(1)}, u32[]{:S(2)}, u32[]{:S(2)}) collective-permute-start(bf16[8,16,1536]{2,1,0:T(8,128)(2,1)S(1)} %norm_local.1), channel_id=1, source_target_pairs={{0,1},{1,0},{2,3},{3,2},{4,5},{5,4},{6,7},{7,6},{8,9},{9,8},{10,11... | collective-permute-start | bytes 1179656 | tf_op jit(solution)/shard_map/ppermute | solution.py:33
  25.8 10.8 %collective-permute-start.3 = (bf16[8,16,1536]{2,1,0:T(8,128)(2,1)S(1)}, bf16[8,16,1536]{2,1,0:T(8,128)(2,1)}, u32[]{:S(2)}, u32[]{:S(2)}) collective-permute-start(bf16[8,16,1536]{2,1,0:T(8,128)(2,1)S(1)} %collective-permute-done.1), channel_id=1, source_target_pairs={{0,1},{1,0},{2,3},{3,2},{4,5},{5,4},{6,7},{7,6},{8,9},{9,8},{10,11... | collective-permute-start | bytes 1179656 | tf_op jit(solution)/shard_map/ppermute | solution.py:33
  26.3 16.7 %collective-permute-start.7 = (bf16[8,16,1536]{2,1,0:T(8,128)(2,1)S(1)}, bf16[8,16,1536]{2,1,0:T(8,128)(2,1)}, u32[]{:S(2)}, u32[]{:S(2)}) collective-permute-start(bf16[8,16,1536]{2,1,0:T(8,128)(2,1)S(1)} %norm_mixed.1), channel_id=1, source_target_pairs={{0,1},{1,0},{2,3},{3,2},{4,5},{5,4},{6,7},{7,6},{8,9},{9,8},{10,11... | collective-permute-start | bytes 1179656 | tf_op jit(solution)/shard_map/ppermute | solution.py:33
  34.8 8.3 %collective-permute-start.8 = (bf16[8,16,1536]{2,1,0:T(8,128)(2,1)S(1)}, bf16[8,16,1536]{2,1,0:T(8,128)(2,1)}, u32[]{:S(2)}, u32[]{:S(2)}) collective-permute-start(bf16[8,16,1536]{2,1,0:T(8,128)(2,1)S(1)} %collective-permute-done.6), channel_id=1, source_target_pairs={{0,1},{1,0},{2,3},{3,2},{4,5},{5,4},{6,7},{7,6},{8,9},{9,8},{10,11... | collective-permute-start | bytes 1179656 | tf_op jit(solution)/shard_map/ppermute | solution.py:33
  36.6 2.0 %copy-start.1 = (bf16[1,1536,4,288]{1,3,2,0:T(8,128)(2,1)S(1)}, bf16[1,1536,4,288]{1,3,2,0:T(8,128)(2,1)}, u32[]{:S(2)}) copy-start(bf16[1,1536,4,288]{1,3,2,0:T(8,128)(2,1)} %param.14) | copy-start | bytes 10616836
  38.6 4.4 %copy-start.2 = (bf16[1,1536,4,288]{1,3,2,0:T(8,128)(2,1)S(1)}, bf16[1,1536,4,288]{1,3,2,0:T(8,128)(2,1)}, u32[]{:S(2)}) copy-start(bf16[1,1536,4,288]{1,3,2,0:T(8,128)(2,1)} %param.14) | copy-start | bytes 10616836
  43.1 19.6 %slice-start = ((s8[4718592]{0:T(1024)(128)(4,1)}), s8[4194304]{0:T(1024)(128)(4,1)S(1)}, s32[]{:S(2)}) async-start(s8[4718592]{0:T(1024)(128)(4,1)} %bitcast.47), calls=%async_computation | async-start | bytes 8388608
  48.2 14.4 %slice-start.1 = ((s8[4718592]{0:T(1024)(128)(4,1)}), s8[524288]{0:T(1024)(128)(4,1)S(1)}, s32[]{:S(2)}) async-start(s8[4718592]{0:T(1024)(128)(4,1)} %bitcast.47), calls=%async_computation.1 | async-start | bytes 1048576
  53.7 1.6 %collective-permute-start.9 = (bf16[1,2,128,384]{3,2,1,0:T(8,128)(2,1)S(1)}, bf16[1,2,128,384]{3,2,1,0:T(8,128)(2,1)S(1)}, u32[]{:S(2)}, u32[]{:S(2)}) collective-permute-start(bf16[1,2,128,384]{3,2,1,0:T(8,128)(2,1)S(1)} %get-tuple-element.16), channel_id=1, source_target_pairs={{0,1},{1,0},{2,3},{3,2},{4,5},{5,4},{6,7},{7,6},{8,9},{9,8},{10,11... | collective-permute-start | bytes 589832 | tf_op jit(solution)/shard_map/ppermute | solution.py:33
  55.4 7.3 %copy-start.3 = (f32[1,32,1536]{2,1,0:T(8,128)S(1)}, f32[1,32,1536]{2,1,0:T(8,128)}, u32[]{:S(2)}) copy-start(f32[1,32,1536]{2,1,0:T(8,128)} %param.19) | copy-start | bytes 589828
  55.4 7.2 %collective-permute-start.13 = (bf16[2,1,128,384]{3,2,1,0:T(8,128)(2,1)S(1)}, bf16[2,1,128,384]{3,2,1,0:T(8,128)(2,1)S(1)}, u32[]{:S(2)}, u32[]{:S(2)}) collective-permute-start(bf16[2,1,128,384]{3,2,1,0:T(8,128)(2,1)S(1)} %pad_maximum_fusion), channel_id=1, source_target_pairs={{0,2},{1,3},{2,0},{3,1},{4,6},{5,7},{6,4},{7,5},{8,10},{9,11},{10,... | collective-permute-start | bytes 589832 | tf_op jit(solution)/shard_map/ppermute | solution.py:33
  61.7 5.4 %collective-permute-start.10 = (bf16[1,2,128,384]{3,2,1,0:T(8,128)(2,1)S(1)}, bf16[1,2,128,384]{3,2,1,0:T(8,128)(2,1)S(1)}, u32[]{:S(2)}, u32[]{:S(2)}) collective-permute-start(bf16[1,2,128,384]{3,2,1,0:T(8,128)(2,1)S(1)} %get-tuple-element.14), channel_id=1, source_target_pairs={{0,1},{1,0},{2,3},{3,2},{4,5},{5,4},{6,7},{7,6},{8,9},{9,8},{10,11... | collective-permute-start | bytes 589832 | tf_op jit(solution)/shard_map/ppermute | solution.py:33
  65.0 11.9 %collective-permute-start.14 = (bf16[8,16,1536]{2,1,0:T(8,128)(2,1)S(1)}, bf16[8,16,1536]{2,1,0:T(8,128)(2,1)S(1)}, u32[]{:S(2)}, u32[]{:S(2)}) collective-permute-start(bf16[8,16,1536]{2,1,0:T(8,128)(2,1)S(1)} %finish.3), channel_id=1, source_target_pairs={{0,12},{4,0},{8,4},{12,8},{1,13},{5,1},{9,5},{13,9},{2,14},{6,2},{... | collective-permute-start | bytes 1179656 | tf_op jit(solution)/shard_map/ppermute | solution.py:29
  66.8 17.9 %collective-permute-start.15 = (bf16[8,16,1536]{2,1,0:T(8,128)(2,1)S(1)}, bf16[8,16,1536]{2,1,0:T(8,128)(2,1)S(1)}, u32[]{:S(2)}, u32[]{:S(2)}) collective-permute-start(bf16[8,16,1536]{2,1,0:T(8,128)(2,1)S(1)} %finish.3), channel_id=1, source_target_pairs={{0,4},{4,8},{8,12},{12,0},{1,5},{5,9},{9,13},{13,1},{2,6},{6,10},{... | collective-permute-start | bytes 1179656 | tf_op jit(solution)/shard_map/ppermute | solution.py:29
  67.1 6.1 %collective-permute-start.11 = (bf16[2,1,128,384]{3,2,1,0:T(8,128)(2,1)S(1)}, bf16[2,1,128,384]{3,2,1,0:T(8,128)(2,1)S(1)}, u32[]{:S(2)}, u32[]{:S(2)}) collective-permute-start(bf16[2,1,128,384]{3,2,1,0:T(8,128)(2,1)S(1)} %pad_maximum_fusion.1), channel_id=1, source_target_pairs={{0,2},{1,3},{2,0},{3,1},{4,6},{5,7},{6,4},{7,5},{8,10},{9,11},{10,... | collective-permute-start | bytes 589832 | tf_op jit(solution)/shard_map/ppermute | solution.py:33
  75.5 20.5 %collective-permute-start.12 = (bf16[8,16,1536]{2,1,0:T(8,128)(2,1)S(1)}, bf16[8,16,1536]{2,1,0:T(8,128)(2,1)S(1)}, u32[]{:S(2)}, u32[]{:S(2)}) collective-permute-start(bf16[8,16,1536]{2,1,0:T(8,128)(2,1)S(1)} %finish.2), channel_id=1, source_target_pairs={{0,16},{16,0},{1,17},{17,1},{2,18},{18,2},{3,19},{19,3},{4,20},{20... | collective-permute-start | bytes 1179656 | tf_op jit(solution)/shard_map/ppermute | solution.py:29
  84.8 11.2 %collective-permute-start.16 = (bf16[8,16,1536]{2,1,0:T(8,128)(2,1)S(1)}, bf16[8,16,1536]{2,1,0:T(8,128)(2,1)S(1)}, u32[]{:S(2)}, u32[]{:S(2)}) collective-permute-start(bf16[8,16,1536]{2,1,0:T(8,128)(2,1)S(1)} %select_select_fusion), channel_id=1, source_target_pairs={{0,16},{16,0},{1,17},{17,1},{2,18},{18,2},{3,19},{19,3},{4,20},{20... | collective-permute-start | bytes 1179656 | tf_op jit(solution)/shard_map/ppermute | solution.py:29
  86.1 8.6 %collective-permute-start = (s32[1,2]{1,0:T(1,128)S(1)}, s32[1,2]{1,0:T(1,128)S(1)}, u32[]{:S(2)}, u32[]{:S(2)}) collective-permute-start(s32[1,2]{1,0:T(1,128)S(1)} %copy-done.7), channel_id=1, source_target_pairs={{0,16},{16,0},{1,17},{17,1},{2,18},{18,2},{3,19},{19,3},{4,20},{20... | collective-permute-start | bytes 32 | tf_op jit(solution)/shard_map/ppermute | solution.py:29

commit v2 on v1

v2 whole, which is shorter than its diff:
```python
import functools
import math

import jax
import jax.numpy as jnp
from jax import lax
from jax.experimental import pallas as pl
from jax.experimental.pallas import tpu as pltpu
from jax.sharding import PartitionSpec as P

eps_norm = 1e-06
lane = 128
far = 1e30
constant_shift_scale = 32.0

SMEM = pl.BlockSpec(memory_space=pltpu.SMEM)
VMEM = pl.BlockSpec(memory_space=pltpu.VMEM)


small = pl.CostEstimate(flops=1, bytes_accessed=1, transcendentals=0)


def params(mib=40):
    return pltpu.CompilerParams(vmem_limit_bytes=mib << 20)


def passed_along(block, axis, distance):
    n = lax.axis_size(axis)
    return lax.ppermute(block, axis, [(i, (i + distance) % n) for i in range(n)])


def swapped(block, axis, mask):
    return lax.ppermute(block, axis, [(i, i ^ mask) for i in range(lax.axis_size(axis))])


def places_of(masks):
    me = lax.axis_index("seq")
    return [me ^ m for m in masks]


def all_gentle(scales):
    top = scales[0, 0]
    for h in range(1, scales.shape[1]):
        top = jnp.maximum(top, scales[0, h])
    return top <= constant_shift_scale


def normalise(x, scale_row, shift_row):
    x = x - jnp.mean(x, -1, keepdims=True)
    variance = jnp.mean(x * x, -1, keepdims=True)
    return (x * lax.rsqrt(variance + eps_norm) * scale_row + shift_row).astype(jnp.bfloat16)


def local_half_kernel(level, offsets, tile, shift, scale, out):
    row = pl.ds(level[0] % shift.shape[0], 1)
    for r in range(tile.shape[0]):
        out[r] = normalise(tile[r].astype(jnp.float32), scale[row, :], shift[row, :])


def mixed_half(r, lon, half, tile, borrowed):
    big = lon > half
    column = lax.broadcasted_iota(jnp.int32, (half, 1), 0) + jnp.where(big, half, 0)
    far_side = jnp.where(big, (column >= lon).astype(jnp.int32), (column < lon).astype(jnp.int32)) == 1
    return jnp.where(far_side, borrowed[r].astype(jnp.float32), tile[r].astype(jnp.float32))


def mixed_half_kernel(level, offsets, tile, borrowed, shift, scale, out):
    row = pl.ds(level[0] % shift.shape[0], 1)
    for r in range(tile.shape[0]):
        x = mixed_half(r, offsets[0, 1], tile.shape[1], tile, borrowed)
        out[r] = normalise(x, scale[row, :], shift[row, :])


def project_kernel(masks, half, size, offsets, scales, *refs):
    count = len(masks)
    places = places_of(masks)
    pieces, weight, out = refs[:count], refs[count], refs[count + 1]
    tokens, padded, query_extra, key_extra = refs[count + 2 :]
    piece_rows = pieces[0].shape[0]
    group = weight.shape[0]
    total = tokens.shape[0]
    step = pl.program_id(0)

    @pl.when(step == 0)
    def _():
        padded[...] = jnp.zeros_like(padded)
        for j in range(count):
            tokens[pl.ds(pl.multiple_of(places[j] * piece_rows, piece_rows), piece_rows), :] = pieces[j][...]
        row = lax.broadcasted_iota(jnp.int32, (total, lane), 0) // half
        column = lax.broadcasted_iota(jnp.int32, (total, lane), 1)
        low = jnp.where(row < offsets[0, 0], 1.0, 0.0)
        query_extra[...] = jnp.where(
            column == size, low, jnp.where(column == size + 1, 1.0 - low, jnp.where(column == size + 2, 1.0, 0.0))
        )
        key_extra[...] = jnp.where(
            column == size,
            far * (low - 1.0),
            jnp.where(column == size + 1, -far * low, jnp.where(column == size + 2, -1.0, 0.0)),
        )

    for g in range(group):
        for i in range(3):
            begin = (3 * g + i) * lane
            padded[begin : begin + size, :] = weight[g, i * size : (i + 1) * size, :]
    mixture = lax.dot_general(
        tokens[...], padded[...], (((1,), (1,)), ((), ())), preferred_element_type=jnp.float32
    )
    ones = jnp.where(lax.broadcasted_iota(jnp.int32, (1, lane), 1) == size, 1.0, 0.0)
    fast = all_gentle(scales)
    for g in range(group):
        strength = jnp.where(fast, scales[0, step * group + g] * math.log2(math.e), 1.0)
        query, key, value = (mixture[:, (3 * g + i) * lane : (3 * g + i + 1) * lane] for i in range(3))
        query = query * (lax.rsqrt(jnp.sum(query * query, -1, keepdims=True) + eps_norm) * strength) + query_extra[...]
        key = key * lax.rsqrt(jnp.sum(key * key, -1, keepdims=True) + eps_norm) + key_extra[...] * strength
        out[g, 0] = query.astype(jnp.bfloat16)
        out[g, 1] = key.astype(jnp.bfloat16)
        out[g, 2] = (value + ones).astype(jnp.bfloat16)


def attend_kernel(masks, size, scales, queries, first, second, out, held):
    places = places_of(masks)
    fast = all_gentle(scales)
    head = pl.program_id(0)
    heads, total = held.shape[0], held.shape[1]
    count, piece_rows, _ = out.shape
    halves = (first, second)
    contract = (((1,), (1,)), ((), ()))
    block = math.gcd(total, 256)

    def body(with_max):
        for begin in range(0, total, block):
            query = queries[0, 0, begin : begin + block, :]
            scores = [
                lax.dot_general(query, part[0, 1], contract, preferred_element_type=jnp.float32) for part in halves
            ]
            if with_max:
                strength = scales[0, head] * math.log2(math.e)
                top = jnp.maximum(jnp.max(scores[0], -1, keepdims=True), jnp.max(scores[1], -1, keepdims=True))
                scores = [(s - top) * strength for s in scores]
            mixed = sum(
                jnp.dot(jnp.exp2(s).astype(jnp.bfloat16), part[0, 2], preferred_element_type=jnp.float32)
                for s, part in zip(scores, halves)
            )
            held[head, begin : begin + block, :] = mixed[:, :size] / mixed[:, size : size + 1]

    @pl.when(fast)
    def _():
        body(False)

    @pl.when(jnp.logical_not(fast))
    def _():
        body(True)

    @pl.when(head == heads - 1)
    def _():
        for j in range(count):
            rows = pl.ds(pl.multiple_of(places[j] * piece_rows, piece_rows), piece_rows)
            out[j] = jnp.concatenate([held[h, rows, :] for h in range(heads)], -1).astype(jnp.bfloat16)


def finish_kernel(masks, mixed, level, offsets, tile, *refs):
    count = len(masks)
    places = places_of(masks)
    if mixed:
        borrowed, refs = refs[0], refs[1:]
    pieces, weight, gate, out = refs[:count], refs[count], refs[count + 1], refs[count + 2]
    inner = pieces[0].shape[-1]
    rows, half, _ = tile.shape
    total = 0.0
    for j in range(count):
        begin = pl.multiple_of(places[j] * inner, inner)
        total = total + jnp.dot(pieces[j][...], weight[pl.ds(begin, inner), :], preferred_element_type=jnp.float32)
    branch = gate[pl.ds(level[0] % gate.shape[0], 1), :] * total.astype(jnp.bfloat16).astype(jnp.float32)
    for r in range(rows):
        if mixed:
            residual = mixed_half(r, offsets[0, 1], half, tile, borrowed)
        else:
            residual = tile[r].astype(jnp.float32)
        out[r] = (residual + branch[r * half : (r + 1) * half]).astype(jnp.bfloat16)


def assemble_kernel(source_offsets, local, mixed, out):
    half = local.shape[1]
    big = source_offsets[0, 1] > half
    first = pl.multiple_of(jnp.where(big, 0, half), half)
    second = pl.multiple_of(jnp.where(big, half, 0), half)
    out[0, :, pl.ds(first, half), :] = local[...]
    out[0, :, pl.ds(second, half), :] = mixed[...]


def shards(
    latents, timesteps, offsets, qkv_weight, logit_scale, out_weight, mod_shift, mod_scale, mod_gate
):
    tile = latents[0]
    rows, cols, width = tile.shape
    half = cols // 2
    heads = qkv_weight.shape[2]
    size = qkv_weight.shape[3] // 3
    inner = heads * size
    n = lax.axis_size("seq")
    masks = [0]
    bits = [1 << i for i in range(n.bit_length() - 1)]
    for bit in reversed(bits):
        masks = masks + [m | bit for m in masks]
    shift, scale, gate = mod_shift[0], mod_scale[0], mod_gate[0]
    piece_rows = rows * half
    half_tokens = n * piece_rows

    weight = jnp.transpose(qkv_weight[0], (1, 2, 0))
    group = 2 if heads % 2 == 0 else 1

    source_offsets = passed_along(offsets, "segment", 1)
    lon = offsets[0, 1]
    big = lon > half

    def gathered(pieces):
        for bit in reversed(bits[:-1]):
            pieces = pieces + [swapped(p, "seq", bit) for p in pieces]
        return pieces

    def projected(pieces):
        return pl.pallas_call(
            functools.partial(project_kernel, masks, half, size),
            grid=(heads // group,),
            out_shape=jax.ShapeDtypeStruct((heads, 3, half_tokens, lane), jnp.bfloat16),
            in_specs=[SMEM, SMEM]
            + [pl.BlockSpec((piece_rows, width), lambda h: (0, 0))] * n
            + [pl.BlockSpec((group, 3 * size, width), lambda h: (h, 0, 0))],
            out_specs=pl.BlockSpec((group, 3, half_tokens, lane), lambda h: (h, 0, 0, 0)),
            scratch_shapes=[
                pltpu.VMEM((half_tokens, width), jnp.bfloat16),
                pltpu.VMEM((group * 3 * lane, width), jnp.bfloat16),
                pltpu.VMEM((half_tokens, lane), jnp.float32),
                pltpu.VMEM((half_tokens, lane), jnp.float32),
            ],
            compiler_params=params(),
            cost_estimate=small,
            name="project",
        )(offsets, logit_scale, *[p.reshape(piece_rows, width) for p in pieces], weight)

    half_shape = jax.ShapeDtypeStruct((rows, half, width), jnp.bfloat16)
    def is_big(offsets):
        return (offsets[0, 1] > half).astype(jnp.int32)

    def normed(kernel, name, low_if_big, *arrays):
        block = math.gcd(rows, 4)
        table = math.gcd(shift.shape[0], 8)

        def own(i, level, offsets):
            return i, is_big(offsets) ^ low_if_big, 0

        return pl.pallas_call(
            kernel,
            grid_spec=pltpu.PrefetchScalarGridSpec(
                num_scalar_prefetch=2,
                grid=(rows // block,),
                in_specs=[pl.BlockSpec((block, half, width), own)]
                + [pl.BlockSpec((block, half, width), lambda i, *_: (i, 0, 0))] * (len(arrays) - 1)
                + [pl.BlockSpec((table, width), lambda i, level, offsets: (level[0] // table, 0))] * 2,
                out_specs=pl.BlockSpec((block, half, width), lambda i, *_: (i, 0, 0)),
            ),
            out_shape=half_shape,
            compiler_params=params(),
            cost_estimate=small,
            name=name,
        )(timesteps, offsets, *arrays, shift, scale)

    def window_heads(borrowed):
        local = normed(local_half_kernel, "norm_local", 1, tile)
        local_far = swapped(local, "seq", bits[-1])
        mixed = normed(mixed_half_kernel, "norm_mixed", 0, tile, *borrowed)
        local_far, mixed = lax.optimization_barrier((local_far, mixed))
        local_heads = projected(gathered([local, local_far]))
        mixed_far = swapped(mixed, "seq", bits[-1])
        mixed_far, local_heads = lax.optimization_barrier((mixed_far, local_heads))
        return local_heads, projected(gathered([mixed, mixed_far])), borrowed

    def from_next(tile):
        return window_heads([passed_along(tile[:, :half], "win", -1)])

    def from_before(tile):
        return window_heads([passed_along(tile[:, half:], "win", 1)])

    local_heads, mixed_heads, borrowed = lax.cond(big, from_before, from_next, tile)
    local_heads, source_offsets = lax.optimization_barrier((local_heads, source_offsets))

    def attended(own, first, second):
        whole = pl.BlockSpec((1, 3, half_tokens, lane), lambda h: (h, 0, 0, 0))
        return pl.pallas_call(
            functools.partial(attend_kernel, masks, size),
            grid=(heads,),
            in_specs=[SMEM, pl.BlockSpec((1, 1, half_tokens, lane), lambda h: (h, 0, 0, 0)), whole, whole],
            out_specs=pl.BlockSpec((n, piece_rows, inner), lambda h: (0, 0, 0)),
            scratch_shapes=[pltpu.VMEM((heads, half_tokens, size), jnp.float32)],
            out_shape=jax.ShapeDtypeStruct((n, piece_rows, inner), jnp.bfloat16),
            compiler_params=params(),
            cost_estimate=small,
            name="attend",
        )(logit_scale, own, first, second)

    def hop(held, bit):
        middle = held.shape[1] // 2
        return held[:, :middle], swapped(held[:, middle:], "seq", bit)

    def returned(held):
        held = jnp.concatenate(held, 0)
        for bit in bits[1:]:
            held = jnp.concatenate(hop(held, bit), 0)
        return [held[g, 0] for g in range(n)]

    order = [0]
    for bit in bits:
        order = order + [m | bit for m in order]

    def finished(groups, extra, is_mixed):
        block = width // 3 if width % (3 * lane) == 0 else width
        table = math.gcd(gate.shape[0], 8)
        sides = pl.BlockSpec((rows, half, block), lambda i, *_: (0, 0, i))
        low_if_big = 0 if is_mixed else 1
        return pl.pallas_call(
            functools.partial(finish_kernel, order, is_mixed),
            grid_spec=pltpu.PrefetchScalarGridSpec(
                num_scalar_prefetch=2,
                grid=(width // block,),
                in_specs=[
                    pl.BlockSpec(
                        (rows, half, block), lambda i, level, offsets: (0, is_big(offsets) ^ low_if_big, i)
                    )
                ]
                + [sides] * len(extra)
                + [pl.BlockSpec((piece_rows, inner), lambda i, *_: (0, 0))] * n
                + [
                    pl.BlockSpec((width, block), lambda i, *_: (0, i)),
                    pl.BlockSpec((table, block), lambda i, level, offsets: (level[0] // table, i)),
                ],
                out_specs=sides,
            ),
            out_shape=half_shape,
            compiler_params=params(),
            cost_estimate=small,
            name="finish",
        )(timesteps, offsets, tile, *extra, *groups, out_weight[0], gate)

    mixed_kept, mixed_received = hop(attended(mixed_heads, local_heads, mixed_heads)[None], bits[0])
    local_query, mixed_received = lax.optimization_barrier((local_heads, mixed_received))
    mixed_out = returned((mixed_kept, mixed_received))
    local_out = returned(hop(attended(local_query, local_query, mixed_heads)[None], bits[0]))
    mixed_done = finished(mixed_out, borrowed, True)
    up = passed_along(mixed_done, "win", 1)
    down = passed_along(mixed_done, "win", -1)
    local_done = finished(local_out, [], False)
    local_sent = passed_along(local_done, "segment", 1)
    column = lax.iota(jnp.int32, half) + jnp.where(big, half, 0)
    far_side = jnp.where(big, column >= lon, column < lon)
    mixed_back = jnp.where(far_side[None, :, None], jnp.where(big, down, up), mixed_done)
    mixed_sent = passed_along(mixed_back, "segment", 1)
    return pl.pallas_call(
        assemble_kernel,
        out_shape=jax.ShapeDtypeStruct((1, rows, cols, width), jnp.bfloat16),
        in_specs=[SMEM, VMEM, VMEM],
        out_specs=VMEM,
        compiler_params=params(),
        cost_estimate=small,
        name="assemble",
    )(source_offsets, local_sent, mixed_sent)


def solution(mesh):
    in_specs = (
        P("segment", "seq", "win", None),
        P("segment"),
        P("segment", None),
        P("segment", None, "seq", None),
        P("segment", "seq"),
        P("segment", None, None),
        P("segment", None, None),
        P("segment", None, None),
        P("segment", None, None),
    )
    out_specs = P("segment", "seq", "win", None)
    return jax.shard_map(shards, mesh=mesh, in_specs=in_specs, out_specs=out_specs, check_vma=False)
```

time: 97.3 us -> 90.2 us (0.927)
  Pallas kernels: 26.1 us -> 30.6 us
  waiting for transfers between devices: 42.8 us -> 39.5 us
  other arithmetic: 3.6 us -> 0.82 us
  starting transfers between devices: 17.1 us -> 14.4 us
  local copies, waits for them, and re-layouts: 4.62 us -> 3.06 us
  between operations: 2.83 us -> 1.53 us
    ppermute x7 -> x6, waiting for transfers between devices: 27.4 us -> 21.7 us  [passed_along(): lax.ppermute(block, axis, [(i, (i + distance) % n) for i in range(n)])]
    pallas_call x8 -> x9, Pallas kernels: 26.1 us -> 30.6 us  [the longest x2 10.9 us: attended(): pl.pallas_call(functools.partial(attend_kernel, masks, size), grid=(heads...]
    ppermute x10, waiting for transfers between devices: 15.4 us -> 17.8 us  [swapped(): lax.ppermute(block, axis, [(i, i ^ mask) for i in range(lax.axis_size(axi...]
    unnamed x22 -> x16, local copies, waits for them, and re-layouts: 2.05 us -> 0.5 us
    ppermute x7 -> x6, starting transfers between devices: 10.8 us -> 9.34 us  [passed_along(): lax.ppermute(block, axis, [(i, (i + distance) % n) for i in range(n)])]
    another operation x1 -> x0, other arithmetic: 1.27 us -> none  [shards(): ints = jnp.stack([timesteps[0], lat, lon])]
    ppermute x10, starting transfers between devices: 6.27 us -> 5.04 us  [swapped(): lax.ppermute(block, axis, [(i, i ^ mask) for i in range(lax.axis_size(axi...]
    slice x3 -> x2, local copies, waits for them, and re-layouts: 2.4 us -> 2.36 us  [the longest x1 1.27 us: shards(): lon = offsets[0, 1]]
  transfers between devices with their start and end apart: 17 -> 16, of which waited for: 8 -> 11; matrix products, arithmetic and copies ran while one was open for 3% -> 4% of each run, Pallas kernels for 17% -> 26%
where the time goes in v2:
time: 90.2 us
  waiting for transfers between devices  39.5 us (44%)
  Pallas kernels  30.6 us (34%)
  starting transfers between devices  14.4 us (16%)
  local copies, waits for them, and re-layouts  3.06 us (3%)
  between operations  1.53 us (2%)
    ppermute x6, waiting for transfers between devices, passed_along(): lax.ppermute(block, axis, [(i, (i + distance) % n) for i in range(n)])  21.7 us
    ppermute x10, waiting for transfers between devices, swapped(): lax.ppermute(block, axis, [(i, i ^ mask) for i in range(lax.axis_size(axi...  17.8 us
    pallas_call x2, Pallas kernels, attended(): pl.pallas_call(functools.partial(attend_kernel, masks, size), grid=(heads...  10.9 us
    ppermute x6, starting transfers between devices, passed_along(): lax.ppermute(block, axis, [(i, (i + distance) % n) for i in range(n)])  9.34 us
    pallas_call x2, Pallas kernels, projected(): pl.pallas_call(functools.partial(project_kernel, masks, half, size), grid...  7.7 us
    pallas_call x2, Pallas kernels, normed(): pl.pallas_call(kernel, grid_spec=pltpu.PrefetchScalarGridSpec(num_scalar_...  5.72 us
    ppermute x10, starting transfers between devices, swapped(): lax.ppermute(block, axis, [(i, i ^ mask) for i in range(lax.axis_size(axi...  5.04 us
    pallas_call x2, Pallas kernels, finished(): pl.pallas_call(functools.partial(finish_kernel, order, is_mixed), grid_sp...  4.76 us
  transfers between devices with their start and end apart: 16, of which 11 were waited for; matrix products, arithmetic and copies ran while one was open for 4% of the time, Pallas kernels for 26%

profile of v2, /device:TPU:0, one launch (start us, length us, event | category | flops | bytes accessed | tf_op | source)
XLA Modules:
  0.0 90.2 jit_solution(13457092118255789951)
XLA Ops:
  0.0 3.0 %collective-permute-start.14 = (s32[1,2]{1,0:T(1,128)}, s32[1,2]{1,0:T(1,128)S(1)}, u32[]{:S(2)}, u32[]{:S(2)}) collective-permute-start(s32[1,2]{1,0:T(1,128)} %offsets.3), channel_id=1, source_target_pairs={{0,16},{16,0},{1,17},{17,1},{2,18},{18,2},{3,19},{19,3},{4,20},{20... | collective-permute-start | bytes 32 | tf_op jit(solution)/shard_map/ppermute | solution.py:29
  3.0 1.3 %slice.63 = s32[1,1]{1,0:T(1,128)} slice(s32[1,2]{1,0:T(1,128)} %offsets.3), slice={[0:1], [1:2]} | slice | bytes 8 | tf_op jit(solution)/shard_map/slice | solution.py:213
  5.5 0.7 compare_select_fusion
  6.2 35.5 %conditional.1 = (bf16[4,3,512,128]{3,2,1,0:T(8,128)(2,1)S(1)}, bf16[4,3,512,128]{3,2,1,0:T(8,128)(2,1)S(1)}, bf16[8,16,1536]{2,1,0:T(8,128)(2,1)}) conditional(s32[]{:T(128)} %convert_element_type.3, (s32[1]{0:T(128)}, s32[1,2]{1,0:T(1,128)}, bf16[8,32,1536]{2,1,0:T(8,128)(2,1)}, f32[32,1536]{1,0:T(8,128)}, f32[32,1536]{1,0:T(8,128)}, ...), branch_computations={%region_0.0_spmd, %region_1.0_spmd} | conditional | flops 4 | bytes 30671388 | solution.py:284
  6.2 1.1 %slice.46 = bf16[8,16,1536]{2,1,0:T(8,128)(2,1)S(1)} slice(bf16[8,32,1536]{2,1,0:T(8,128)(2,1)} %get-tuple-element.35.tile), slice={[0:8], [0:16], [0:1536]} | slice | bytes 786432 | tf_op jit(solution)/shard_map/cond/branch_0_fun/slice | solution.py:279
  7.3 3.7 %collective-permute-start.1 = (bf16[8,16,1536]{2,1,0:T(8,128)(2,1)S(1)}, bf16[8,16,1536]{2,1,0:T(8,128)(2,1)S(1)}, u32[]{:S(2)}, u32[]{:S(2)}) collective-permute-start(bf16[8,16,1536]{2,1,0:T(8,128)(2,1)S(1)} %slice.46), channel_id=1, source_target_pairs={{0,12},{4,0},{8,4},{12,8},{1,13},{5,1},{9,5},{13,9},{2,14},{6,2},{... | collective-permute-start | bytes 1179656 | tf_op jit(solution)/shard_map/cond/branch_0_fun/ppermute | solution.py:29
  11.0 3.1 %norm_local.2 = bf16[8,16,1536]{2,1,0:T(8,128)(2,1)S(1)} custom-call(s32[1]{0:T(128)} %get-tuple-element.33.level, s32[1,2]{1,0:T(1,128)} %get-tuple-element.34.offsets, bf16[8,32,1536]{2,1,0:T(8,128)(2,1)} %get-tuple-element.35.tile, f32[32,1536]{1,0:T(8,128)} %get-tuple-element.36.shift, f32[32,1536]{1,0:T(8,128)} %get-tuple-element.37.scale), custom_call_target="tpu_custom_call" | custom-call | flops 1 | bytes 1 | tf_op jit(solution)/shard_map/cond/branch_0_fun/norm_local/pallas_call | solution.py:252
  14.1 1.6 %collective-permute-start = (bf16[8,16,1536]{2,1,0:T(8,128)(2,1)S(1)}, bf16[8,16,1536]{2,1,0:T(8,128)(2,1)S(1)}, u32[]{:S(2)}, u32[]{:S(2)}) collective-permute-start(bf16[8,16,1536]{2,1,0:T(8,128)(2,1)S(1)} %norm_local.2), channel_id=1, source_target_pairs={{0,2},{1,3},{2,0},{3,1},{4,6},{5,7},{6,4},{7,5},{8,10},{9,11},{10,... | collective-permute-start | bytes 1179656 | tf_op jit(solution)/shard_map/cond/branch_0_fun/ppermute | solution.py:33
  15.7 3.4 %collective-permute-done.1.borrowed = bf16[8,16,1536]{2,1,0:T(8,128)(2,1)S(1)} collective-permute-done((bf16[8,16,1536]{2,1,0:T(8,128)(2,1)S(1)}, bf16[8,16,1536]{2,1,0:T(8,128)(2,1)S(1)}, u32[]{:S(2)}, u32[]{:S(2)}) %collective-permute-start.1) | collective-permute-done | bytes 393248 | tf_op jit(solution)/shard_map/cond/branch_0_fun/ppermute | solution.py:29
  19.1 2.6 %norm_mixed.2 = bf16[8,16,1536]{2,1,0:T(8,128)(2,1)S(1)} custom-call(s32[1]{0:T(128)} %get-tuple-element.33.level, s32[1,2]{1,0:T(1,128)S(1)} %copy-done.13, bf16[8,32,1536]{2,1,0:T(8,128)(2,1)S(1)} %copy-done.5, bf16[8,16,1536]{2,1,0:T(8,128)(2,1)S(1)} %collective-permute-done.1.borrowed, f32[32,1536]{1,0:T(8,128)} %get-tuple-element.36.shift, ...), custom_call_target="tpu_custom_call" | custom-call | flops 1 | bytes 1 | tf_op jit(solution)/shard_map/cond/branch_0_fun/norm_mixed/pallas_call | solution.py:252
  21.7 2.7 %collective-permute-done = bf16[8,16,1536]{2,1,0:T(8,128)(2,1)S(1)} collective-permute-done((bf16[8,16,1536]{2,1,0:T(8,128)(2,1)S(1)}, bf16[8,16,1536]{2,1,0:T(8,128)(2,1)S(1)}, u32[]{:S(2)}, u32[]{:S(2)}) %collective-permute-start) | collective-permute-done | bytes 393248 | tf_op jit(solution)/shard_map/cond/branch_0_fun/ppermute | solution.py:33
  24.5 1.5 %collective-permute-start.2 = (bf16[8,16,1536]{2,1,0:T(8,128)(2,1)S(1)}, bf16[8,16,1536]{2,1,0:T(8,128)(2,1)S(1)}, u32[]{:S(2)}, u32[]{:S(2)}) collective-permute-start(bf16[8,16,1536]{2,1,0:T(8,128)(2,1)S(1)} %norm_mixed.2), channel_id=1, source_target_pairs={{0,2},{1,3},{2,0},{3,1},{4,6},{5,7},{6,4},{7,5},{8,10},{9,11},{10,... | collective-permute-start | bytes 1179656 | tf_op jit(solution)/shard_map/cond/branch_0_fun/ppermute | solution.py:33
  26.2 3.9 %project.4 = bf16[4,3,512,128]{3,2,1,0:T(8,128)(2,1)S(1)} custom-call(s32[1,2]{1,0:T(1,128)S(1)} %copy-done.13, f32[1,4]{1,0:T(1,128)S(1)} %copy-done.16, bf16[128,1536]{1,0:T(8,128)(2,1)S(1)} %bitcast.51, bf16[128,1536]{1,0:T(8,128)(2,1)S(1)} %bitcast.55, bf16[128,1536]{1,0:T(8,128)(2,1)S(1)} %bitcast.59, bf16[128,1536]{1,0:T(8,128)(2,1)S(1)} %bitcast.63, ...), custom_call_target="tpu_custom_call" | custom-call | flops 1 | bytes 1 | tf_op jit(solution)/shard_map/cond/branch_0_fun/project/pallas_call | solution.py:222
  30.1 5.9 %collective-permute-done.2 = bf16[8,16,1536]{2,1,0:T(8,128)(2,1)S(1)} collective-permute-done((bf16[8,16,1536]{2,1,0:T(8,128)(2,1)S(1)}, bf16[8,16,1536]{2,1,0:T(8,128)(2,1)S(1)}, u32[]{:S(2)}, u32[]{:S(2)}) %collective-permute-start.2) | collective-permute-done | bytes 393248 | tf_op jit(solution)/shard_map/cond/branch_0_fun/ppermute | solution.py:33
  36.0 1.7 %collective-permute-done.6 = bf16[8,16,1536]{2,1,0:T(8,128)(2,1)S(1)} collective-permute-done((bf16[8,16,1536]{2,1,0:T(8,128)(2,1)S(1)}, bf16[8,16,1536]{2,1,0:T(8,128)(2,1)S(1)}, u32[]{:S(2)}, u32[]{:S(2)}) %collective-permute-start.6) | collective-permute-done | bytes 393248 | tf_op jit(solution)/shard_map/cond/branch_0_fun/ppermute | solution.py:33
  37.7 3.8 %project.5 = bf16[4,3,512,128]{3,2,1,0:T(8,128)(2,1)S(1)} custom-call(s32[1,2]{1,0:T(1,128)S(1)} %copy-done.13, f32[1,4]{1,0:T(1,128)S(1)} %copy-done.16, bf16[128,1536]{1,0:T(8,128)(2,1)S(1)} %bitcast.49, bf16[128,1536]{1,0:T(8,128)(2,1)S(1)} %bitcast.57, bf16[128,1536]{1,0:T(8,128)(2,1)S(1)} %bitcast.61, bf16[128,1536]{1,0:T(8,128)(2,1)S(1)} %bitcast.65, ...), custom_call_target="tpu_custom_call" | custom-call | flops 1 | bytes 1 | tf_op jit(solution)/shard_map/cond/branch_0_fun/project/pallas_call | solution.py:222
  41.8 5.5 %attend.2 = bf16[4,128,384]{2,1,0:T(8,128)(2,1)S(1)} custom-call(f32[1,4]{1,0:T(1,128)} %scales.3, bf16[4,3,512,128]{3,2,1,0:T(8,128)(2,1)S(1)} %get-tuple-element.65.queries.second, bf16[4,3,512,128]{3,2,1,0:T(8,128)(2,1)S(1)} %get-tuple-element.66.first.queries, bf16[4,3,512,128]{3,2,1,0:T(8,128)(2,1)S(1)} %get-tuple-element.65.queries.second), custom_call_target="tpu_custom_call" | custom-call | flops 1 | bytes 1 | tf_op jit(solution)/shard_map/attend/pallas_call | solution.py:289
  47.6 1.3 %collective-permute-done.15 = bf16[1,2,128,384]{3,2,1,0:T(8,128)(2,1)S(1)} collective-permute-done((bf16[1,2,128,384]{3,2,1,0:T(8,128)(2,1)S(1)}, bf16[1,2,128,384]{3,2,1,0:T(8,128)(2,1)S(1)}, u32[]{:S(2)}, u32[]{:S(2)}) %collective-permute-start.15) | collective-permute-done | bytes 196640 | tf_op jit(solution)/shard_map/ppermute | solution.py:33
  49.0 0.9 collective-permute-start.19
  49.9 5.4 %attend.3 = bf16[4,128,384]{2,1,0:T(8,128)(2,1)S(1)} custom-call(f32[1,4]{1,0:T(1,128)S(1)} %copy-done.15, bf16[4,3,512,128]{3,2,1,0:T(8,128)(2,1)S(1)} %get-tuple-element.66.first.queries, bf16[4,3,512,128]{3,2,1,0:T(8,128)(2,1)S(1)} %get-tuple-element.66.first.queries, bf16[4,3,512,128]{3,2,1,0:T(8,128)(2,1)S(1)} %copy-done.8), custom_call_target="tpu_custom_call" | custom-call | flops 1 | bytes 1 | tf_op jit(solution)/shard_map/attend/pallas_call | solution.py:289
  55.4 0.5 collective-permute-done.19
  56.5 2.4 %finish.3 = bf16[8,16,1536]{2,1,0:T(8,128)(2,1)S(1)} custom-call(s32[1]{0:T(128)S(6)} %copy.16.level, s32[1,2]{1,0:T(1,128)S(1)} %copy-done.12, bf16[8,32,1536]{2,1,0:T(8,128)(2,1)S(1)} %bitcast.71, bf16[8,16,1536]{2,1,0:T(8,128)(2,1)S(1)} %copy-done.11, bf16[128,384]{1,0:T(8,128)(2,1)S(1)} %slice_bitcast_fusion.2.refs_1_, ...), custom_call_target="tpu_custom_call" | custom-call | flops 1 | bytes 1 | tf_op jit(solution)/shard_map/finish/pallas_call | solution.py:320
  58.9 1.7 %collective-permute-start.20 = (bf16[8,16,1536]{2,1,0:T(8,128)(2,1)S(1)}, bf16[8,16,1536]{2,1,0:T(8,128)(2,1)S(1)}, u32[]{:S(2)}, u32[]{:S(2)}) collective-permute-start(bf16[8,16,1536]{2,1,0:T(8,128)(2,1)S(1)} %finish.3), channel_id=1, source_target_pairs={{0,12},{4,0},{8,4},{12,8},{1,13},{5,1},{9,5},{13,9},{2,14},{6,2},{... | collective-permute-start | bytes 1179656 | tf_op jit(solution)/shard_map/ppermute | solution.py:29
  60.6 0.4 collective-permute-start.21
  61.0 0.6 collective-permute-start.17
  61.6 5.6 %collective-permute-done.17 = bf16[2,1,128,384]{3,2,1,0:T(8,128)(2,1)S(1)} collective-permute-done((bf16[2,1,128,384]{3,2,1,0:T(8,128)(2,1)S(1)}, bf16[2,1,128,384]{3,2,1,0:T(8,128)(2,1)S(1)}, u32[]{:S(2)}, u32[]{:S(2)}) %collective-permute-start.17) | collective-permute-done | bytes 196640 | tf_op jit(solution)/shard_map/ppermute | solution.py:33
  67.2 2.4 %finish.2 = bf16[8,16,1536]{2,1,0:T(8,128)(2,1)S(1)} custom-call(s32[1]{0:T(128)S(6)} %copy.16.level, s32[1,2]{1,0:T(1,128)S(1)} %copy-done.12, bf16[8,32,1536]{2,1,0:T(8,128)(2,1)S(1)} %bitcast.72, bf16[128,384]{1,0:T(8,128)(2,1)S(1)} %slice_bitcast_fusion.6.refs_0_, bf16[128,384]{1,0:T(8,128)(2,1)S(1)} %slice_bitcast_fusion.5.refs_1_, ...), custom_call_target="tpu_custom_call" | custom-call | flops 1 | bytes 1 | tf_op jit(solution)/shard_map/finish/pallas_call | solution.py:320
  69.7 1.0 %collective-permute-done.20 = bf16[8,16,1536]{2,1,0:T(8,128)(2,1)S(1)} collective-permute-done((bf16[8,16,1536]{2,1,0:T(8,128)(2,1)S(1)}, bf16[8,16,1536]{2,1,0:T(8,128)(2,1)S(1)}, u32[]{:S(2)}, u32[]{:S(2)}) %collective-permute-start.20) | collective-permute-done | bytes 393248 | tf_op jit(solution)/shard_map/ppermute | solution.py:29
  70.7 7.6 %collective-permute-done.21 = bf16[8,16,1536]{2,1,0:T(8,128)(2,1)S(1)} collective-permute-done((bf16[8,16,1536]{2,1,0:T(8,128)(2,1)S(1)}, bf16[8,16,1536]{2,1,0:T(8,128)(2,1)S(1)}, u32[]{:S(2)}, u32[]{:S(2)}) %collective-permute-start.21) | collective-permute-done | bytes 393248 | tf_op jit(solution)/shard_map/ppermute | solution.py:29
  78.4 0.6 collective-permute-start.22
  79.0 9.6 %collective-permute-done.22.mixed = bf16[8,16,1536]{2,1,0:T(8,128)(2,1)S(1)} collective-permute-done((bf16[8,16,1536]{2,1,0:T(8,128)(2,1)S(1)}, bf16[8,16,1536]{2,1,0:T(8,128)(2,1)S(1)}, u32[]{:S(2)}, u32[]{:S(2)}) %collective-permute-start.22) | collective-permute-done | bytes 393248 | tf_op jit(solution)/shard_map/ppermute | solution.py:29
  88.7 1.5 %assemble.1 = bf16[1,8,32,1536]{3,2,1,0:T(8,128)(2,1)} custom-call(s32[1,2]{1,0:T(1,128)S(1)} %collective-permute-done.14.source_offsets, bf16[8,16,1536]{2,1,0:T(8,128)(2,1)S(1)} %collective-permute-done.18.local, bf16[8,16,1536]{2,1,0:T(8,128)(2,1)S(1)} %collective-permute-done.22.mixed), custom_call_target="tpu_custom_call" | custom-call | flops 1 | bytes 1 | tf_op jit(solution)/shard_map/assemble/pallas_call | solution.py:357
  (50 shorter events, 1.6 us)
Async XLA Ops:
  0.0 41.8 %collective-permute-start.14 = (s32[1,2]{1,0:T(1,128)}, s32[1,2]{1,0:T(1,128)S(1)}, u32[]{:S(2)}, u32[]{:S(2)}) collective-permute-start(s32[1,2]{1,0:T(1,128)} %offsets.3), channel_id=1, source_target_pairs={{0,16},{16,0},{1,17},{17,1},{2,18},{18,2},{3,19},{19,3},{4,20},{20... | collective-permute-start | bytes 32 | tf_op jit(solution)/shard_map/ppermute | solution.py:29
  6.2 12.9 %copy-start.5 = (bf16[8,32,1536]{2,1,0:T(8,128)(2,1)S(1)}, bf16[8,32,1536]{2,1,0:T(8,128)(2,1)}, u32[]{:S(2)}) copy-start(bf16[8,32,1536]{2,1,0:T(8,128)(2,1)} %get-tuple-element.35.tile) | copy-start | bytes 2359300 | tf_op jit(solution)/shard_map/cond
  6.2 12.9 %copy-start.13 = (s32[1,2]{1,0:T(1,128)S(1)}, s32[1,2]{1,0:T(1,128)}, u32[]{:S(2)}) copy-start(s32[1,2]{1,0:T(1,128)} %get-tuple-element.34.offsets) | copy-start | bytes 28 | tf_op jit(solution)/shard_map/cond
  7.3 11.7 %collective-permute-start.1 = (bf16[8,16,1536]{2,1,0:T(8,128)(2,1)S(1)}, bf16[8,16,1536]{2,1,0:T(8,128)(2,1)S(1)}, u32[]{:S(2)}, u32[]{:S(2)}) collective-permute-start(bf16[8,16,1536]{2,1,0:T(8,128)(2,1)S(1)} %slice.46), channel_id=1, source_target_pairs={{0,12},{4,0},{8,4},{12,8},{1,13},{5,1},{9,5},{13,9},{2,14},{6,2},{... | collective-permute-start | bytes 1179656 | tf_op jit(solution)/shard_map/cond/branch_0_fun/ppermute | solution.py:29
  11.0 15.2 %copy-start.2 = (bf16[4,288,1536]{2,1,0:T(8,128)(2,1)S(1)}, bf16[4,288,1536]{2,1,0:T(8,128)(2,1)}, u32[]{:S(2)}) copy-start(bf16[4,288,1536]{2,1,0:T(8,128)(2,1)} %get-tuple-element.41.refs_4_) | copy-start | bytes 10616836 | tf_op jit(solution)/shard_map/cond
  11.0 15.2 %copy-start.16 = (f32[1,4]{1,0:T(1,128)S(1)}, f32[1,4]{1,0:T(1,128)}, u32[]{:S(2)}) copy-start(f32[1,4]{1,0:T(1,128)} %get-tuple-element.39.scales) | copy-start | bytes 52 | tf_op jit(solution)/shard_map/cond
  14.1 10.4 %collective-permute-start = (bf16[8,16,1536]{2,1,0:T(8,128)(2,1)S(1)}, bf16[8,16,1536]{2,1,0:T(8,128)(2,1)S(1)}, u32[]{:S(2)}, u32[]{:S(2)}) collective-permute-start(bf16[8,16,1536]{2,1,0:T(8,128)(2,1)S(1)} %norm_local.2), channel_id=1, source_target_pairs={{0,2},{1,3},{2,0},{3,1},{4,6},{5,7},{6,4},{7,5},{8,10},{9,11},{10,... | collective-permute-start | bytes 1179656 | tf_op jit(solution)/shard_map/cond/branch_0_fun/ppermute | solution.py:33
  15.7 10.5 %collective-permute-start.3 = (bf16[8,16,1536]{2,1,0:T(8,128)(2,1)S(1)}, bf16[8,16,1536]{2,1,0:T(8,128)(2,1)S(1)}, u32[]{:S(2)}, u32[]{:S(2)}) collective-permute-start(bf16[8,16,1536]{2,1,0:T(8,128)(2,1)S(1)} %norm_local.2), channel_id=1, source_target_pairs={{0,1},{1,0},{2,3},{3,2},{4,5},{5,4},{6,7},{7,6},{8,9},{9,8},{10,11... | collective-permute-start | bytes 1179656 | tf_op jit(solution)/shard_map/cond/branch_0_fun/ppermute | solution.py:33
  19.1 11.0 %copy-start.9 = (bf16[8,16,1536]{2,1,0:T(8,128)(2,1)}, bf16[8,16,1536]{2,1,0:T(8,128)(2,1)S(1)}, u32[]{:S(2)}) copy-start(bf16[8,16,1536]{2,1,0:T(8,128)(2,1)S(1)} %collective-permute-done.1.borrowed) | copy-start | bytes 1179652 | tf_op jit(solution)/shard_map/cond
  24.5 1.7 %collective-permute-start.4 = (bf16[8,16,1536]{2,1,0:T(8,128)(2,1)S(1)}, bf16[8,16,1536]{2,1,0:T(8,128)(2,1)S(1)}, u32[]{:S(2)}, u32[]{:S(2)}) collective-permute-start(bf16[8,16,1536]{2,1,0:T(8,128)(2,1)S(1)} %collective-permute-done), channel_id=1, source_target_pairs={{0,1},{1,0},{2,3},{3,2},{4,5},{5,4},{6,7},{7,6},{8,9},{9,8},{10,11... | collective-permute-start | bytes 1179656 | tf_op jit(solution)/shard_map/cond/branch_0_fun/ppermute | solution.py:33
  24.5 11.5 %collective-permute-start.2 = (bf16[8,16,1536]{2,1,0:T(8,128)(2,1)S(1)}, bf16[8,16,1536]{2,1,0:T(8,128)(2,1)S(1)}, u32[]{:S(2)}, u32[]{:S(2)}) collective-permute-start(bf16[8,16,1536]{2,1,0:T(8,128)(2,1)S(1)} %norm_mixed.2), channel_id=1, source_target_pairs={{0,2},{1,3},{2,0},{3,1},{4,6},{5,7},{6,4},{7,5},{8,10},{9,11},{10,... | collective-permute-start | bytes 1179656 | tf_op jit(solution)/shard_map/cond/branch_0_fun/ppermute | solution.py:33
  26.0 10.0 %collective-permute-start.5 = (bf16[8,16,1536]{2,1,0:T(8,128)(2,1)S(1)}, bf16[8,16,1536]{2,1,0:T(8,128)(2,1)S(1)}, u32[]{:S(2)}, u32[]{:S(2)}) collective-permute-start(bf16[8,16,1536]{2,1,0:T(8,128)(2,1)S(1)} %norm_mixed.2), channel_id=1, source_target_pairs={{0,1},{1,0},{2,3},{3,2},{4,5},{5,4},{6,7},{7,6},{8,9},{9,8},{10,11... | collective-permute-start | bytes 1179656 | tf_op jit(solution)/shard_map/cond/branch_0_fun/ppermute | solution.py:33
  36.0 1.7 %collective-permute-start.6 = (bf16[8,16,1536]{2,1,0:T(8,128)(2,1)S(1)}, bf16[8,16,1536]{2,1,0:T(8,128)(2,1)S(1)}, u32[]{:S(2)}, u32[]{:S(2)}) collective-permute-start(bf16[8,16,1536]{2,1,0:T(8,128)(2,1)S(1)} %collective-permute-done.2), channel_id=1, source_target_pairs={{0,1},{1,0},{2,3},{3,2},{4,5},{5,4},{6,7},{7,6},{8,9},{9,8},{10,11... | collective-permute-start | bytes 1179656 | tf_op jit(solution)/shard_map/cond/branch_0_fun/ppermute | solution.py:33
  41.8 5.6 %copy-start.7 = (bf16[4,3,512,128]{3,2,1,0:T(8,128)(2,1)}, bf16[4,3,512,128]{3,2,1,0:T(8,128)(2,1)S(1)}, u32[]{:S(2)}) copy-start(bf16[4,3,512,128]{3,2,1,0:T(8,128)(2,1)S(1)} %get-tuple-element.65.queries.second) | copy-start | bytes 4718596
  47.3 2.5 %copy-start.15 = (f32[1,4]{1,0:T(1,128)S(1)}, f32[1,4]{1,0:T(1,128)}, u32[]{:S(2)}) copy-start(f32[1,4]{1,0:T(1,128)} %scales.3) | copy-start | bytes 52
  47.3 2.5 %copy-start.8 = (bf16[4,3,512,128]{3,2,1,0:T(8,128)(2,1)S(1)}, bf16[4,3,512,128]{3,2,1,0:T(8,128)(2,1)}, u32[]{:S(2)}) copy-start(bf16[4,3,512,128]{3,2,1,0:T(8,128)(2,1)} %copy-done.7) | copy-start | bytes 4718596
  47.4 1.5 %collective-permute-start.15 = (bf16[1,2,128,384]{3,2,1,0:T(8,128)(2,1)S(1)}, bf16[1,2,128,384]{3,2,1,0:T(8,128)(2,1)S(1)}, u32[]{:S(2)}, u32[]{:S(2)}) collective-permute-start(bf16[1,2,128,384]{3,2,1,0:T(8,128)(2,1)S(1)} %get-tuple-element.70), channel_id=1, source_target_pairs={{0,1},{1,0},{2,3},{3,2},{4,5},{5,4},{6,7},{7,6},{8,9},{9,8},{10,11... | collective-permute-start | bytes 589832 | tf_op jit(solution)/shard_map/ppermute | solution.py:33
  49.0 7.1 %copy-start.1 = (f32[1,32,1536]{2,1,0:T(8,128)S(1)}, f32[1,32,1536]{2,1,0:T(8,128)}, u32[]{:S(2)}) copy-start(f32[1,32,1536]{2,1,0:T(8,128)} %param.19) | copy-start | bytes 589828
  49.0 7.1 %copy-start.12 = (s32[1,2]{1,0:T(1,128)S(1)}, s32[1,2]{1,0:T(1,128)}, u32[]{:S(2)}) copy-start(s32[1,2]{1,0:T(1,128)} %offsets.3) | copy-start | bytes 28
  49.0 7.0 %collective-permute-start.19 = (bf16[2,1,128,384]{3,2,1,0:T(8,128)(2,1)S(1)}, bf16[2,1,128,384]{3,2,1,0:T(8,128)(2,1)S(1)}, u32[]{:S(2)}, u32[]{:S(2)}) collective-permute-start(bf16[2,1,128,384]{3,2,1,0:T(8,128)(2,1)S(1)} %pad_maximum_fusion), channel_id=1, source_target_pairs={{0,2},{1,3},{2,0},{3,1},{4,6},{5,7},{6,4},{7,5},{8,10},{9,11},{10,... | collective-permute-start | bytes 589832 | tf_op jit(solution)/shard_map/ppermute | solution.py:33
  49.9 6.2 %copy-start = (bf16[1,1536,1536]{2,1,0:T(8,128)(2,1)S(1)}, bf16[1,1536,1536]{2,1,0:T(8,128)(2,1)}, u32[]{:S(2)}) copy-start(bf16[1,1536,1536]{2,1,0:T(8,128)(2,1)} %param.16) | copy-start | bytes 14155780
  55.3 1.1 %copy-start.4 = (bf16[1,8,32,1536]{3,2,1,0:T(8,128)(2,1)S(1)}, bf16[1,8,32,1536]{3,2,1,0:T(8,128)(2,1)}, u32[]{:S(2)}) copy-start(bf16[1,8,32,1536]{3,2,1,0:T(8,128)(2,1)} %param.11) | copy-start | bytes 2359300
  55.3 1.2 %copy-start.11 = (bf16[8,16,1536]{2,1,0:T(8,128)(2,1)S(1)}, bf16[8,16,1536]{2,1,0:T(8,128)(2,1)}, u32[]{:S(2)}) copy-start(bf16[8,16,1536]{2,1,0:T(8,128)(2,1)} %get-tuple-element.67.refs_0_) | copy-start | bytes 1179652
  55.3 5.6 %collective-permute-start.16 = (bf16[1,2,128,384]{3,2,1,0:T(8,128)(2,1)S(1)}, bf16[1,2,128,384]{3,2,1,0:T(8,128)(2,1)S(1)}, u32[]{:S(2)}, u32[]{:S(2)}) collective-permute-start(bf16[1,2,128,384]{3,2,1,0:T(8,128)(2,1)S(1)} %get-tuple-element.72), channel_id=1, source_target_pairs={{0,1},{1,0},{2,3},{3,2},{4,5},{5,4},{6,7},{7,6},{8,9},{9,8},{10,11... | collective-permute-start | bytes 589832 | tf_op jit(solution)/shard_map/ppermute | solution.py:33
  58.9 11.7 %collective-permute-start.20 = (bf16[8,16,1536]{2,1,0:T(8,128)(2,1)S(1)}, bf16[8,16,1536]{2,1,0:T(8,128)(2,1)S(1)}, u32[]{:S(2)}, u32[]{:S(2)}) collective-permute-start(bf16[8,16,1536]{2,1,0:T(8,128)(2,1)S(1)} %finish.3), channel_id=1, source_target_pairs={{0,12},{4,0},{8,4},{12,8},{1,13},{5,1},{9,5},{13,9},{2,14},{6,2},{... | collective-permute-start | bytes 1179656 | tf_op jit(solution)/shard_map/ppermute | solution.py:29
  60.6 17.7 %collective-permute-start.21 = (bf16[8,16,1536]{2,1,0:T(8,128)(2,1)S(1)}, bf16[8,16,1536]{2,1,0:T(8,128)(2,1)S(1)}, u32[]{:S(2)}, u32[]{:S(2)}) collective-permute-start(bf16[8,16,1536]{2,1,0:T(8,128)(2,1)S(1)} %finish.3), channel_id=1, source_target_pairs={{0,4},{4,8},{8,12},{12,0},{1,5},{5,9},{9,13},{13,1},{2,6},{6,10},{... | collective-permute-start | bytes 1179656 | tf_op jit(solution)/shard_map/ppermute | solution.py:29
  61.0 6.2 %collective-permute-start.17 = (bf16[2,1,128,384]{3,2,1,0:T(8,128)(2,1)S(1)}, bf16[2,1,128,384]{3,2,1,0:T(8,128)(2,1)S(1)}, u32[]{:S(2)}, u32[]{:S(2)}) collective-permute-start(bf16[2,1,128,384]{3,2,1,0:T(8,128)(2,1)S(1)} %pad_maximum_fusion.1), channel_id=1, source_target_pairs={{0,2},{1,3},{2,0},{3,1},{4,6},{5,7},{6,4},{7,5},{8,10},{9,11},{10,... | collective-permute-start | bytes 589832 | tf_op jit(solution)/shard_map/ppermute | solution.py:33
  69.6 9.5 %collective-permute-start.18 = (bf16[8,16,1536]{2,1,0:T(8,128)(2,1)S(1)}, bf16[8,16,1536]{2,1,0:T(8,128)(2,1)S(1)}, u32[]{:S(2)}, u32[]{:S(2)}) collective-permute-start(bf16[8,16,1536]{2,1,0:T(8,128)(2,1)S(1)} %finish.2), channel_id=1, source_target_pairs={{0,16},{16,0},{1,17},{17,1},{2,18},{18,2},{3,19},{19,3},{4,20},{20... | collective-permute-start | bytes 1179656 | tf_op jit(solution)/shard_map/ppermute | solution.py:29
  78.4 10.3 %collective-permute-start.22 = (bf16[8,16,1536]{2,1,0:T(8,128)(2,1)S(1)}, bf16[8,16,1536]{2,1,0:T(8,128)(2,1)S(1)}, u32[]{:S(2)}, u32[]{:S(2)}) collective-permute-start(bf16[8,16,1536]{2,1,0:T(8,128)(2,1)S(1)} %select_select_fusion), channel_id=1, source_target_pairs={{0,16},{16,0},{1,17},{17,1},{2,18},{18,2},{3,19},{19,3},{4,20},{20... | collective-permute-start | bytes 1179656 | tf_op jit(solution)/shard_map/ppermute | solution.py:29

commit v3 on v2

v3 whole, which is shorter than its diff:
```python
import functools
import math

import jax
import jax.numpy as jnp
from jax import lax
from jax.experimental import pallas as pl
from jax.experimental.pallas import tpu as pltpu
from jax.sharding import PartitionSpec as P

eps_norm = 1e-06
lane = 128
far = 1e30
constant_shift_scale = 32.0

SMEM = pl.BlockSpec(memory_space=pltpu.SMEM)
VMEM = pl.BlockSpec(memory_space=pltpu.VMEM)


small = pl.CostEstimate(flops=1, bytes_accessed=1, transcendentals=0)


def params(mib=40):
    return pltpu.CompilerParams(vmem_limit_bytes=mib << 20)


def passed_along(block, axis, distance):
    n = lax.axis_size(axis)
    return lax.ppermute(block, axis, [(i, (i + distance) % n) for i in range(n)])


def swapped(block, axis, mask):
    return lax.ppermute(block, axis, [(i, i ^ mask) for i in range(lax.axis_size(axis))])


def places_of(masks):
    me = lax.axis_index("seq")
    return [me ^ m for m in masks]


def gathered_masks(held, bits):
    for bit in reversed(bits[:-1]):
        held = held + [m | bit for m in held]
    return held


def all_gentle(scales):
    top = scales[0, 0]
    for h in range(1, scales.shape[1]):
        top = jnp.maximum(top, scales[0, h])
    return top <= constant_shift_scale


def normalise(x, scale_row, shift_row):
    x = x - jnp.mean(x, -1, keepdims=True)
    variance = jnp.mean(x * x, -1, keepdims=True)
    return (x * lax.rsqrt(variance + eps_norm) * scale_row + shift_row).astype(jnp.bfloat16)


def project_kernel(masks, rows, size, level, offsets, scales, *refs):
    count = len(masks)
    places = places_of(masks)
    pieces = refs[:count]
    weight, shift, scale, out, tokens, padded, query_extra, key_extra = refs[count:]
    piece_rows = pieces[0].shape[0]
    half = piece_rows // rows
    group = weight.shape[0]
    step = pl.program_id(0)

    @pl.when(step == 0)
    def _():
        padded[...] = jnp.zeros_like(padded)
        shift_row, scale_row = shift[pl.ds(level[0], 1), :], scale[pl.ds(level[0], 1), :]
        column = lax.broadcasted_iota(jnp.int32, (piece_rows, lane), 1)
        local_row = lax.broadcasted_iota(jnp.int32, (piece_rows, lane), 0) // half
        chunk = math.gcd(piece_rows, 32)
        for j in range(count):
            for begin in range(0, piece_rows, chunk):
                x = pieces[j][begin : begin + chunk, :].astype(jnp.float32)
                at = j * piece_rows + begin
                tokens[at : at + chunk, :] = normalise(x, scale_row, shift_row)
            low = jnp.where(local_row + places[j] * rows < offsets[0, 0], 1.0, 0.0)
            span = slice(j * piece_rows, (j + 1) * piece_rows)
            query_extra[span, :] = jnp.where(
                column == size, low, jnp.where(column == size + 1, 1.0 - low, jnp.where(column == size + 2, 1.0, 0.0))
            )
            key_extra[span, :] = jnp.where(
                column == size,
                far * (low - 1.0),
                jnp.where(column == size + 1, -far * low, jnp.where(column == size + 2, -1.0, 0.0)),
            )

    for g in range(group):
        for i in range(3):
            begin = (3 * g + i) * lane
            padded[begin : begin + size, :] = weight[g, i * size : (i + 1) * size, :]
    mixture = lax.dot_general(
        tokens[...], padded[...], (((1,), (1,)), ((), ())), preferred_element_type=jnp.float32
    )
    ones = jnp.where(lax.broadcasted_iota(jnp.int32, (1, lane), 1) == size, 1.0, 0.0)
    fast = all_gentle(scales)
    for g in range(group):
        strength = jnp.where(fast, scales[0, step * group + g] * math.log2(math.e), 1.0)
        query, key, value = (mixture[:, (3 * g + i) * lane : (3 * g + i + 1) * lane] for i in range(3))
        query = query * (lax.rsqrt(jnp.sum(query * query, -1, keepdims=True) + eps_norm) * strength) + query_extra[...]
        key = key * lax.rsqrt(jnp.sum(key * key, -1, keepdims=True) + eps_norm) + key_extra[...] * strength
        out[g, 0] = query.astype(jnp.bfloat16)
        out[g, 1] = key.astype(jnp.bfloat16)
        out[g, 2] = (value + ones).astype(jnp.bfloat16)


def attend_kernel(own_count, own_masks, out_masks, size, scales, *refs):
    queries, parts, out, held = refs[:own_count], refs[own_count:-2], refs[-2], refs[-1]
    fast = all_gentle(scales)
    head = pl.program_id(0)
    heads = held.shape[0]
    piece_rows = out.shape[1]
    contract = (((1,), (1,)), ((), ()))

    def body(with_max):
        at = 0
        for own in queries:
            block = math.gcd(own.shape[2], 256)
            for begin in range(0, own.shape[2], block):
                query = own[0, 0, begin : begin + block, :]
                scores = [
                    lax.dot_general(query, part[0, 1], contract, preferred_element_type=jnp.float32) for part in parts
                ]
                if with_max:
                    strength = scales[0, head] * math.log2(math.e)
                    top = functools.reduce(jnp.maximum, [jnp.max(s, -1, keepdims=True) for s in scores])
                    scores = [(s - top) * strength for s in scores]
                mixed = sum(
                    jnp.dot(jnp.exp2(s).astype(jnp.bfloat16), part[0, 2], preferred_element_type=jnp.float32)
                    for s, part in zip(scores, parts)
                )
                held[head, at : at + block, :] = mixed[:, :size] / mixed[:, size : size + 1]
                at += block

    @pl.when(fast)
    def _():
        body(False)

    @pl.when(jnp.logical_not(fast))
    def _():
        body(True)

    @pl.when(head == heads - 1)
    def _():
        for j, mask in enumerate(out_masks):
            begin = own_masks.index(mask) * piece_rows
            out[j] = jnp.concatenate(
                [held[h, begin : begin + piece_rows, :] for h in range(heads)], -1
            ).astype(jnp.bfloat16)


def finish_kernel(masks, level, tile, *refs):
    count = len(masks)
    places = places_of(masks)
    pieces, weight, gate, out = refs[:count], refs[count], refs[count + 1], refs[count + 2]
    inner = pieces[0].shape[-1]
    rows, half, _ = tile.shape
    total = 0.0
    for j in range(count):
        begin = pl.multiple_of(places[j] * inner, inner)
        total = total + jnp.dot(pieces[j][...], weight[pl.ds(begin, inner), :], preferred_element_type=jnp.float32)
    branch = gate[pl.ds(level[0], 1), :] * total.astype(jnp.bfloat16).astype(jnp.float32)
    for r in range(rows):
        out[r] = (tile[r].astype(jnp.float32) + branch[r * half : (r + 1) * half]).astype(jnp.bfloat16)


def assemble_kernel(offsets, local, mixed, moved, out):
    rows, half, _ = local.shape
    lon = offsets[0, 1]
    big = lon > half
    first = pl.multiple_of(jnp.where(big, 0, half), half)
    second = pl.multiple_of(jnp.where(big, half, 0), half)
    column = lax.broadcasted_iota(jnp.int32, (half, 1), 0) + second
    far_side = jnp.where(big, (column >= lon).astype(jnp.int32), (column < lon).astype(jnp.int32)) == 1
    out[0, :, pl.ds(first, half), :] = local[...]
    for r in range(rows):
        out[0, r, pl.ds(second, half), :] = jnp.where(
            far_side, moved[r].astype(jnp.float32), mixed[r].astype(jnp.float32)
        ).astype(jnp.bfloat16)


def shards(
    latents, timesteps, offsets, qkv_weight, logit_scale, out_weight, mod_shift, mod_scale, mod_gate
):
    tile = latents[0]
    rows, cols, width = tile.shape
    half = cols // 2
    heads = qkv_weight.shape[2]
    size = qkv_weight.shape[3] // 3
    inner = heads * size
    n = lax.axis_size("seq")
    masks = [0]
    bits = [1 << i for i in range(n.bit_length() - 1)]
    for bit in reversed(bits):
        masks = masks + [m | bit for m in masks]
    shift, scale, gate = mod_shift[0], mod_scale[0], mod_gate[0]
    piece_rows = rows * half
    half_tokens = n * piece_rows

    weight = jnp.transpose(qkv_weight[0], (1, 2, 0))
    group = 2 if heads % 2 == 0 else 1

    source_offsets = passed_along(offsets, "segment", 1)
    lon = offsets[0, 1]
    big = lon > half

    half_shape = jax.ShapeDtypeStruct((rows, half, width), jnp.bfloat16)

    def gathered(pieces):
        for bit in reversed(bits[:-1]):
            pieces = pieces + [swapped(p, "seq", bit) for p in pieces]
        return pieces

    def projected(pieces, held_masks):
        tokens = len(pieces) * piece_rows
        table = pl.BlockSpec(shift.shape, lambda h: (0, 0))
        return pl.pallas_call(
            functools.partial(project_kernel, held_masks, rows, size),
            grid=(heads // group,),
            out_shape=jax.ShapeDtypeStruct((heads, 3, tokens, lane), jnp.bfloat16),
            in_specs=[SMEM, SMEM, SMEM]
            + [pl.BlockSpec((piece_rows, width), lambda h: (0, 0))] * len(pieces)
            + [pl.BlockSpec((group, 3 * size, width), lambda h: (h, 0, 0)), table, table],
            out_specs=pl.BlockSpec((group, 3, tokens, lane), lambda h: (h, 0, 0, 0)),
            scratch_shapes=[
                pltpu.VMEM((tokens, width), jnp.bfloat16),
                pltpu.VMEM((group * 3 * lane, width), jnp.bfloat16),
                pltpu.VMEM((tokens, lane), jnp.float32),
                pltpu.VMEM((tokens, lane), jnp.float32),
            ],
            compiler_params=params(),
            cost_estimate=small,
            name="project",
        )(timesteps, offsets, logit_scale, *[p.reshape(piece_rows, width) for p in pieces], weight, shift, scale)

    top = bits[-1]
    local_masks = gathered_masks([0, top], bits)
    near_masks = gathered_masks([0], bits)
    far_masks = [m | top for m in near_masks]

    low, high = tile[:, :half], tile[:, half:]
    local = jnp.where(big, low, high)
    local_far = swapped(local, "seq", top)

    def mixed_half(from_before, tile, lon):
        low, high = tile[:, :half], tile[:, half:]
        own = high if from_before else low
        borrowed = passed_along(own, "win", 1 if from_before else -1)
        column = lax.broadcasted_iota(jnp.int32, own.shape, 1)
        return jnp.where(column + half >= lon if from_before else column < lon, borrowed, own)

    mixed = lax.cond(big, functools.partial(mixed_half, True), functools.partial(mixed_half, False), tile, lon)
    local_far, mixed = lax.optimization_barrier((local_far, mixed))
    local_heads = projected(gathered([local, local_far]), local_masks)
    mixed_far = swapped(mixed, "seq", top)
    near_heads = projected(gathered([mixed]), near_masks)
    mixed_far, local_heads, near_heads, source_offsets = lax.optimization_barrier(
        (mixed_far, local_heads, near_heads, source_offsets)
    )
    far_heads = projected(gathered([mixed_far]), far_masks)

    def attended(own, own_masks, local_heads):
        def block(array, kinds):
            return pl.BlockSpec((1, kinds, array.shape[2], lane), lambda h: (h, 0, 0, 0))

        parts = [local_heads, near_heads, far_heads]
        total = sum(o.shape[2] for o in own)
        return pl.pallas_call(
            functools.partial(attend_kernel, len(own), own_masks, masks, size),
            grid=(heads,),
            in_specs=[SMEM] + [block(o, 1) for o in own] + [block(p, 3) for p in parts],
            out_specs=pl.BlockSpec((n, piece_rows, inner), lambda h: (0, 0, 0)),
            scratch_shapes=[pltpu.VMEM((heads, total, size), jnp.float32)],
            out_shape=jax.ShapeDtypeStruct((n, piece_rows, inner), jnp.bfloat16),
            compiler_params=params(),
            cost_estimate=small,
            name="attend",
        )(logit_scale, *own, *parts)

    def hop(held, bit):
        middle = held.shape[1] // 2
        return held[:, :middle], swapped(held[:, middle:], "seq", bit)

    def returned(held):
        held = jnp.concatenate(held, 0)
        for bit in bits[1:]:
            held = jnp.concatenate(hop(held, bit), 0)
        return [held[g, 0] for g in range(n)]

    order = [0]
    for bit in bits:
        order = order + [m | bit for m in order]

    def finished(groups, residual):
        block = width // 3 if width % (3 * lane) == 0 else width
        sides = pl.BlockSpec((rows, half, block), lambda i: (0, 0, i))
        return pl.pallas_call(
            functools.partial(finish_kernel, order),
            grid=(width // block,),
            in_specs=[SMEM, sides]
            + [pl.BlockSpec((piece_rows, inner), lambda i: (0, 0))] * n
            + [pl.BlockSpec((width, block), lambda i: (0, i)), pl.BlockSpec((gate.shape[0], block), lambda i: (0, i))],
            out_specs=sides,
            out_shape=half_shape,
            compiler_params=params(),
            cost_estimate=small,
            name="finish",
        )(timesteps, residual, *groups, out_weight[0], gate)

    mixed_kept, mixed_received = hop(attended([near_heads, far_heads], near_masks + far_masks, local_heads)[None], bits[0])
    local_query, mixed_received = lax.optimization_barrier((local_heads, mixed_received))
    mixed_out = returned((mixed_kept, mixed_received))
    local_kept, local_received = hop(attended([local_query], local_masks, local_query)[None], bits[0])
    mixed_done, local_received = lax.optimization_barrier((finished(mixed_out, mixed), local_received))
    mixed_sent = passed_along(mixed_done, "segment", 1)
    local_done = finished(returned((local_kept, local_received)), local)
    local_sent = passed_along(local_done, "segment", 1)
    mixed_sent, _ = lax.optimization_barrier((mixed_sent, local_done))
    moved = lax.cond(
        source_offsets[0, 1] > half,
        lambda block: passed_along(block, "win", -1),
        lambda block: passed_along(block, "win", 1),
        mixed_sent,
    )
    return pl.pallas_call(
        assemble_kernel,
        out_shape=jax.ShapeDtypeStruct((1, rows, cols, width), jnp.bfloat16),
        in_specs=[SMEM, VMEM, VMEM, VMEM],
        out_specs=VMEM,
        compiler_params=params(),
        cost_estimate=small,
        name="assemble",
    )(source_offsets, local_sent, mixed_sent, moved)


def solution(mesh):
    in_specs = (
        P("segment", "seq", "win", None),
        P("segment"),
        P("segment", None),
        P("segment", None, "seq", None),
        P("segment", "seq"),
        P("segment", None, None),
        P("segment", None, None),
        P("segment", None, None),
        P("segment", None, None),
    )
    out_specs = P("segment", "seq", "win", None)
    return jax.shard_map(shards, mesh=mesh, in_specs=in_specs, out_specs=out_specs, check_vma=False)
```

time: 90.2 us -> 87.9 us (0.975)
  waiting for transfers between devices: 39.5 us -> 29 us
  starting transfers between devices: 14.4 us -> 18.7 us
  other arithmetic: 0.82 us -> 4.45 us
  Pallas kernels: 30.6 us -> 27.9 us
  local copies, waits for them, and re-layouts: 3.06 us -> 5.11 us
    ppermute x6 -> x5, waiting for transfers between devices: 21.7 us -> 16.4 us  [passed_along(): lax.ppermute(block, axis, [(i, (i + distance) % n) for i in range(n)])]
    ppermute x10, waiting for transfers between devices: 17.8 us -> 12.6 us  [swapped(): lax.ppermute(block, axis, [(i, i ^ mask) for i in range(lax.axis_size(axi...]
    ppermute x10, starting transfers between devices: 5.04 us -> 9.78 us  [swapped(): lax.ppermute(block, axis, [(i, i ^ mask) for i in range(lax.axis_size(axi...]
    pallas_call x8 -> x7, Pallas kernels: 29.1 us -> 25.9 us  [the longest x3 12.2 us: projected(): pl.pallas_call(functools.partial(project_kernel, held_masks, rows, size),...]
    select_n x2, other arithmetic: 0.76 us -> 3.76 us  [the longest x1 1.91 us: shards(): local = jnp.where(big, low, high)]
    unnamed x16 -> x20, local copies, waits for them, and re-layouts: 0.5 us -> 1.89 us
    ppermute x6 -> x5, starting transfers between devices: 9.34 us -> 8.96 us  [passed_along(): lax.ppermute(block, axis, [(i, (i + distance) % n) for i in range(n)])]
  transfers between devices with their start and end apart: 16 -> 15, of which waited for: 11 -> 7; matrix products, arithmetic and copies ran while one was open for 4% -> 5% of each run, Pallas kernels for 26% -> 16%
where the time goes in v3:
time: 87.9 us; the launch traced here: 87.5 us
  waiting for transfers between devices  29 us (33%)
  Pallas kernels  27.9 us (32%)
  starting transfers between devices  18.7 us (21%)
  local copies, waits for them, and re-layouts  5.11 us (6%)
  other arithmetic  4.45 us (5%)
  between operations  2.22 us (3%)
    ppermute x5, waiting for transfers between devices, passed_along(): lax.ppermute(block, axis, [(i, (i + distance) % n) for i in range(n)])  16.4 us
    ppermute x10, waiting for transfers between devices, swapped(): lax.ppermute(block, axis, [(i, i ^ mask) for i in range(lax.axis_size(axi...  12.6 us
    pallas_call x3, Pallas kernels, projected(): pl.pallas_call(functools.partial(project_kernel, held_masks, rows, size),...  12.2 us
    ppermute x10, starting transfers between devices, swapped(): lax.ppermute(block, axis, [(i, i ^ mask) for i in range(lax.axis_size(axi...  9.78 us
    pallas_call x2, Pallas kernels, attended(): pl.pallas_call(functools.partial(attend_kernel, len(own), own_masks, mask...  9.07 us
    ppermute x5, starting transfers between devices, passed_along(): lax.ppermute(block, axis, [(i, (i + distance) % n) for i in range(n)])  8.96 us
    pallas_call x2, Pallas kernels, finished(): pl.pallas_call(functools.partial(finish_kernel, order), grid=(width // bl...  4.6 us
    pallas_call x1, Pallas kernels, shards(): pl.pallas_call(assemble_kernel, out_shape=jax.ShapeDtypeStruct((1, rows,...  2.01 us
  transfers between devices with their start and end apart: 15, of which 7 were waited for; matrix products, arithmetic and copies ran while one was open for 5% of the time, Pallas kernels for 16%

profile of v3, /device:TPU:0, one launch (start us, length us, event | category | flops | bytes accessed | tf_op | source)
XLA Modules:
  0.0 87.5 jit_solution(7762658949907739000)
XLA Ops:
  0.0 1.5 %slice.72 = s32[1,1]{1,0:T(1,128)} slice(s32[1,2]{1,0:T(1,128)} %offsets.5), slice={[0:1], [1:2]} | slice | bytes 8 | tf_op jit(solution)/shard_map/slice | solution.py:209
  2.1 1.9 %slice_select_fusion.tile = bf16[8,16,1536]{2,1,0:T(8,128)(2,1)} fusion(bf16[8,32,1536]{2,1,0:T(8,128)(2,1)} %bitcast.60, pred[]{:T(512)S(6)} %gt.7), kind=kLoop, calls=%fused_computation.4 | loop fusion | flops 196608 | bytes 1179649 | tf_op jit(solution)/shard_map/jit(_where)/select_n | solution.py:247
  4.0 2.9 %collective-permute-start.4 = (bf16[8,16,1536]{2,1,0:T(8,128)(2,1)}, bf16[8,16,1536]{2,1,0:T(8,128)(2,1)}, u32[]{:S(2)}, u32[]{:S(2)}) collective-permute-start(bf16[8,16,1536]{2,1,0:T(8,128)(2,1)} %slice_select_fusion.tile), channel_id=1, source_target_pairs={{0,2},{1,3},{2,0},{3,1},{4,6},{5,7},{6,4},{7,5},{8,10},{9,11},{10,... | collective-permute-start | bytes 1179656 | tf_op jit(solution)/shard_map/ppermute | solution.py:33
  7.0 14.6 %conditional.2 = (bf16[8,16,1536]{2,1,0:T(8,128)(2,1)}) conditional(s32[]{:T(128)} %convert_element_type.9, (s32[]{:T(128)}, bf16[8,32,1536]{2,1,0:T(8,128)(2,1)}) %tuple.36, (s32[]{:T(128)}, bf16[8,32,1536]{2,1,0:T(8,128)(2,1)}) %tuple.37), branch_computations={%region_0.1_spmd, %region_1.2_spmd} | conditional | flops 196640 | bytes 3539028 | solution.py:257
  7.0 1.0 %slice.52 = bf16[8,16,1536]{2,1,0:T(8,128)(2,1)S(1)} slice(bf16[8,32,1536]{2,1,0:T(8,128)(2,1)} %get-tuple-element.22), slice={[0:8], [0:16], [0:1536]} | slice | bytes 786432 | tf_op jit(solution)/shard_map/cond/branch_0_fun/slice | solution.py:251
  8.0 3.7 %collective-permute-start.2 = (bf16[8,16,1536]{2,1,0:T(8,128)(2,1)S(1)}, bf16[8,16,1536]{2,1,0:T(8,128)(2,1)S(1)}, u32[]{:S(2)}, u32[]{:S(2)}) collective-permute-start(bf16[8,16,1536]{2,1,0:T(8,128)(2,1)S(1)} %slice.52), channel_id=1, source_target_pairs={{0,12},{4,0},{8,4},{12,8},{1,13},{5,1},{9,5},{13,9},{2,14},{6,2},{... | collective-permute-start | bytes 1179656 | tf_op jit(solution)/shard_map/cond/branch_0_fun/ppermute | solution.py:29
  12.3 7.4 %collective-permute-done.2 = bf16[8,16,1536]{2,1,0:T(8,128)(2,1)S(1)} collective-permute-done((bf16[8,16,1536]{2,1,0:T(8,128)(2,1)S(1)}, bf16[8,16,1536]{2,1,0:T(8,128)(2,1)S(1)}, u32[]{:S(2)}, u32[]{:S(2)}) %collective-permute-start.2) | collective-permute-done | bytes 393248 | tf_op jit(solution)/shard_map/cond/branch_0_fun/ppermute | solution.py:29
  19.7 1.8 %broadcast_select_fusion = bf16[8,16,1536]{2,1,0:T(8,128)(2,1)} fusion(bf16[8,16,1536]{2,1,0:T(8,128)(2,1)S(1)} %collective-permute-done.2, pred[16]{0:T(512)(128)(4,1)S(1)} %iota_compare_fusion, bf16[8,32,1536]{2,1,0:T(8,128)(2,1)} %get-tuple-element.22), kind=kLoop, calls=%fused_computation | loop fusion | flops 196608 | bytes 1179664 | tf_op jit(solution)/shard_map/cond/branch_0_fun/jit(_where)/select_n | solution.py:255
  22.6 2.3 %collective-permute-start.9 = (s32[1,2]{1,0:T(1,128)S(1)}, s32[1,2]{1,0:T(1,128)S(1)}, u32[]{:S(2)}, u32[]{:S(2)}) collective-permute-start(s32[1,2]{1,0:T(1,128)S(1)} %copy-done.6), channel_id=1, source_target_pairs={{0,16},{16,0},{1,17},{17,1},{2,18},{18,2},{3,19},{19,3},{4,20},{20... | collective-permute-start | bytes 32 | tf_op jit(solution)/shard_map/ppermute | solution.py:29
  25.6 0.9 %copy-done.1 = f32[1,32,1536]{2,1,0:T(8,128)S(1)} copy-done((f32[1,32,1536]{2,1,0:T(8,128)S(1)}, f32[1,32,1536]{2,1,0:T(8,128)}, u32[]{:S(2)}) %copy-start.1) | copy-done | bytes 196632
  26.5 0.9 %copy-done.3 = f32[1,32,1536]{2,1,0:T(8,128)S(1)} copy-done((f32[1,32,1536]{2,1,0:T(8,128)S(1)}, f32[1,32,1536]{2,1,0:T(8,128)}, u32[]{:S(2)}) %copy-start.3) | copy-done | bytes 196632
  27.4 3.6 %project.4.refs_0_.refs_3_.refs_2_ = bf16[4,3,256,128]{3,2,1,0:T(8,128)(2,1)S(1)} custom-call(s32[1]{0:T(128)S(6)} %copy.14.level, s32[1,2]{1,0:T(1,128)S(1)} %copy-done.6, f32[1,4]{1,0:T(1,128)S(1)} %copy-done.5, bf16[128,1536]{1,0:T(8,128)(2,1)} %bitcast.63, bf16[128,1536]{1,0:T(8,128)(2,1)S(1)} %bitcast.56, bf16[4,288,1536]{2,1,0:T(8,128)(2,1)S(1)} %bitcast.36, ...), custom_call_target="tpu_custom_call" | custom-call | flops 1 | bytes 1 | tf_op jit(solution)/shard_map/project/pallas_call | solution.py:222
  31.1 5.6 %project.3.refs_2_.refs_0_.refs_1_ = bf16[4,3,512,128]{3,2,1,0:T(8,128)(2,1)S(1)} custom-call(s32[1]{0:T(128)S(6)} %copy.14.level, s32[1,2]{1,0:T(1,128)S(1)} %copy-done.6, f32[1,4]{1,0:T(1,128)S(1)} %copy-done.5, bf16[128,1536]{1,0:T(8,128)(2,1)} %bitcast.2.refs_0_, bf16[128,1536]{1,0:T(8,128)(2,1)} %bitcast.3.refs_1_, bf16[128,1536]{1,0:T(8,128)(2,1)S(1)} %bitcast.58, ...), custom_call_target="tpu_custom_call" | custom-call | flops 1 | bytes 1 | tf_op jit(solution)/shard_map/project/pallas_call | solution.py:222
  36.7 1.7 %collective-permute-done.10 = bf16[8,16,1536]{2,1,0:T(8,128)(2,1)S(1)} collective-permute-done((bf16[8,16,1536]{2,1,0:T(8,128)(2,1)S(1)}, bf16[8,16,1536]{2,1,0:T(8,128)(2,1)S(1)}, u32[]{:S(2)}, u32[]{:S(2)}) %collective-permute-start.10) | collective-permute-done | bytes 393248 | tf_op jit(solution)/shard_map/ppermute | solution.py:33
  38.4 3.1 %project.5.refs_1_.refs_4_.refs_3_ = bf16[4,3,256,128]{3,2,1,0:T(8,128)(2,1)S(1)} custom-call(s32[1]{0:T(128)S(6)} %copy.14.level, s32[1,2]{1,0:T(1,128)S(1)} %copy-done.6, f32[1,4]{1,0:T(1,128)S(1)} %copy-done.5, bf16[128,1536]{1,0:T(8,128)(2,1)S(1)} %bitcast.55, bf16[128,1536]{1,0:T(8,128)(2,1)S(1)} %bitcast.57, bf16[4,288,1536]{2,1,0:T(8,128)(2,1)S(1)} %bitcast.38, ...), custom_call_target="tpu_custom_call" | custom-call | flops 1 | bytes 1 | tf_op jit(solution)/shard_map/project/pallas_call | solution.py:222
  41.5 4.5 %attend.2 = bf16[4,128,384]{2,1,0:T(8,128)(2,1)S(1)} custom-call(f32[1,4]{1,0:T(1,128)S(1)} %copy-done.5, bf16[4,3,256,128]{3,2,1,0:T(8,128)(2,1)S(1)} %project.4.refs_0_.refs_3_.refs_2_, bf16[4,3,256,128]{3,2,1,0:T(8,128)(2,1)S(1)} %project.5.refs_1_.refs_4_.refs_3_, bf16[4,3,512,128]{3,2,1,0:T(8,128)(2,1)S(1)} %project.3.refs_2_.refs_0_.refs_1_, ...), custom_call_target="tpu_custom_call" | custom-call | flops 1 | bytes 1 | tf_op jit(solution)/shard_map/attend/pallas_call | solution.py:273
  46.1 1.2 %collective-permute-start.11 = (bf16[1,2,128,384]{3,2,1,0:T(8,128)(2,1)S(1)}, bf16[1,2,128,384]{3,2,1,0:T(8,128)(2,1)S(1)}, u32[]{:S(2)}, u32[]{:S(2)}) collective-permute-start(bf16[1,2,128,384]{3,2,1,0:T(8,128)(2,1)S(1)} %get-tuple-element.50), channel_id=1, source_target_pairs={{0,1},{1,0},{2,3},{3,2},{4,5},{5,4},{6,7},{7,6},{8,9},{9,8},{10,11... | collective-permute-start | bytes 589832 | tf_op jit(solution)/shard_map/ppermute | solution.py:33
  47.4 1.0 %collective-permute-done.11 = bf16[1,2,128,384]{3,2,1,0:T(8,128)(2,1)S(1)} collective-permute-done((bf16[1,2,128,384]{3,2,1,0:T(8,128)(2,1)S(1)}, bf16[1,2,128,384]{3,2,1,0:T(8,128)(2,1)S(1)}, u32[]{:S(2)}, u32[]{:S(2)}) %collective-permute-start.11) | collective-permute-done | bytes 196640 | tf_op jit(solution)/shard_map/ppermute | solution.py:33
  48.4 4.5 %attend.3 = bf16[4,128,384]{2,1,0:T(8,128)(2,1)S(1)} custom-call(f32[1,4]{1,0:T(1,128)S(1)} %copy-done.5, bf16[4,3,512,128]{3,2,1,0:T(8,128)(2,1)S(1)} %project.3.refs_2_.refs_0_.refs_1_, bf16[4,3,512,128]{3,2,1,0:T(8,128)(2,1)S(1)} %project.3.refs_2_.refs_0_.refs_1_, bf16[4,3,256,128]{3,2,1,0:T(8,128)(2,1)S(1)} %project.4.refs_0_.refs_3_.refs_2_, ...), custom_call_target="tpu_custom_call" | custom-call | flops 1 | bytes 1 | tf_op jit(solution)/shard_map/attend/pallas_call | solution.py:273
  53.1 1.5 %collective-permute-start.13 = (bf16[1,2,128,384]{3,2,1,0:T(8,128)(2,1)S(1)}, bf16[1,2,128,384]{3,2,1,0:T(8,128)(2,1)S(1)}, u32[]{:S(2)}, u32[]{:S(2)}) collective-permute-start(bf16[1,2,128,384]{3,2,1,0:T(8,128)(2,1)S(1)} %get-tuple-element.48), channel_id=1, source_target_pairs={{0,1},{1,0},{2,3},{3,2},{4,5},{5,4},{6,7},{7,6},{8,9},{9,8},{10,11... | collective-permute-start | bytes 589832 | tf_op jit(solution)/shard_map/ppermute | solution.py:33
  54.5 1.5 %collective-permute-start.12 = (bf16[2,1,128,384]{3,2,1,0:T(8,128)(2,1)S(1)}, bf16[2,1,128,384]{3,2,1,0:T(8,128)(2,1)S(1)}, u32[]{:S(2)}, u32[]{:S(2)}) collective-permute-start(bf16[2,1,128,384]{3,2,1,0:T(8,128)(2,1)S(1)} %pad_maximum_fusion.1), channel_id=1, source_target_pairs={{0,2},{1,3},{2,0},{3,1},{4,6},{5,7},{6,4},{7,5},{8,10},{9,11},{10,... | collective-permute-start | bytes 589832 | tf_op jit(solution)/shard_map/ppermute | solution.py:33
  56.0 5.4 %collective-permute-done.12 = bf16[2,1,128,384]{3,2,1,0:T(8,128)(2,1)S(1)} collective-permute-done((bf16[2,1,128,384]{3,2,1,0:T(8,128)(2,1)S(1)}, bf16[2,1,128,384]{3,2,1,0:T(8,128)(2,1)S(1)}, u32[]{:S(2)}, u32[]{:S(2)}) %collective-permute-start.12) | collective-permute-done | bytes 196640 | tf_op jit(solution)/shard_map/ppermute | solution.py:33
  61.5 1.8 %finish.2 = bf16[8,16,1536]{2,1,0:T(8,128)(2,1)S(1)} custom-call(s32[1]{0:T(128)S(6)} %copy.14.level, bf16[8,16,1536]{2,1,0:T(8,128)(2,1)S(1)} %copy-done.7, bf16[128,384]{1,0:T(8,128)(2,1)S(1)} %slice_bitcast_fusion.4.refs_0_, bf16[128,384]{1,0:T(8,128)(2,1)S(1)} %slice_bitcast_fusion.7.refs_1_, bf16[128,384]{1,0:T(8,128)(2,1)S(1)} %get-tuple-element.54.refs_2_, ...), custom_call_target="tpu_custom_call" | custom-call | flops 1 | bytes 1 | tf_op jit(solution)/shard_map/finish/pallas_call | solution.py:302
  63.4 1.6 %collective-permute-start.14 = (bf16[2,1,128,384]{3,2,1,0:T(8,128)(2,1)S(1)}, bf16[2,1,128,384]{3,2,1,0:T(8,128)(2,1)S(1)}, u32[]{:S(2)}, u32[]{:S(2)}) collective-permute-start(bf16[2,1,128,384]{3,2,1,0:T(8,128)(2,1)S(1)} %pad_maximum_fusion), channel_id=1, source_target_pairs={{0,2},{1,3},{2,0},{3,1},{4,6},{5,7},{6,4},{7,5},{8,10},{9,11},{10,... | collective-permute-start | bytes 589832 | tf_op jit(solution)/shard_map/ppermute | solution.py:33
  65.0 4.5 %collective-permute-done.14 = bf16[2,1,128,384]{3,2,1,0:T(8,128)(2,1)S(1)} collective-permute-done((bf16[2,1,128,384]{3,2,1,0:T(8,128)(2,1)S(1)}, bf16[2,1,128,384]{3,2,1,0:T(8,128)(2,1)S(1)}, u32[]{:S(2)}, u32[]{:S(2)}) %collective-permute-start.14) | collective-permute-done | bytes 196640 | tf_op jit(solution)/shard_map/ppermute | solution.py:33
  69.5 2.8 %finish.3 = bf16[8,16,1536]{2,1,0:T(8,128)(2,1)S(1)} custom-call(s32[1]{0:T(128)S(6)} %copy.14.level, bf16[8,16,1536]{2,1,0:T(8,128)(2,1)} %slice_select_fusion.tile, bf16[128,384]{1,0:T(8,128)(2,1)S(1)} %slice_bitcast_fusion.5.refs_0_, bf16[128,384]{1,0:T(8,128)(2,1)S(1)} %slice_bitcast_fusion.6.refs_1_, bf16[128,384]{1,0:T(8,128)(2,1)S(1)} %get-tuple-element.52.refs_2_, ...), custom_call_target="tpu_custom_call" | custom-call | flops 1 | bytes 1 | tf_op jit(solution)/shard_map/finish/pallas_call | solution.py:302
  72.3 1.0 %collective-permute-start.15 = (bf16[8,16,1536]{2,1,0:T(8,128)(2,1)S(1)}, bf16[8,16,1536]{2,1,0:T(8,128)(2,1)S(1)}, u32[]{:S(2)}, u32[]{:S(2)}) collective-permute-start(bf16[8,16,1536]{2,1,0:T(8,128)(2,1)S(1)} %finish.3), channel_id=1, source_target_pairs={{0,16},{16,0},{1,17},{17,1},{2,18},{18,2},{3,19},{19,3},{4,20},{20... | collective-permute-start | bytes 1179656 | tf_op jit(solution)/shard_map/ppermute | solution.py:29
  74.5 1.9 %collective-permute-done.16.mixed = bf16[8,16,1536]{2,1,0:T(8,128)(2,1)S(1)} collective-permute-done((bf16[8,16,1536]{2,1,0:T(8,128)(2,1)S(1)}, bf16[8,16,1536]{2,1,0:T(8,128)(2,1)S(1)}, u32[]{:S(2)}, u32[]{:S(2)}) %collective-permute-start.16) | collective-permute-done | bytes 393248 | tf_op jit(solution)/shard_map/ppermute | solution.py:29
  76.5 9.0 %conditional.3 = (bf16[8,16,1536]{2,1,0:T(8,128)(2,1)}) conditional(s32[]{:T(128)} %bitcast.27, bf16[8,16,1536]{2,1,0:T(8,128)(2,1)S(1)} %collective-permute-done.16.mixed, bf16[8,16,1536]{2,1,0:T(8,128)(2,1)S(1)} %collective-permute-done.16.mixed), branch_computations={%region_2.3_spmd, %region_3.4_spmd} | conditional | bytes 1572912 | solution.py:324
  76.5 2.0 %collective-permute-start.1 = (bf16[8,16,1536]{2,1,0:T(8,128)(2,1)S(1)}, bf16[8,16,1536]{2,1,0:T(8,128)(2,1)}, u32[]{:S(2)}, u32[]{:S(2)}) collective-permute-start(bf16[8,16,1536]{2,1,0:T(8,128)(2,1)S(1)} %param.3), channel_id=1, source_target_pairs={{0,12},{4,0},{8,4},{12,8},{1,13},{5,1},{9,5},{13,9},{2,14},{6,2},{... | collective-permute-start | bytes 1179656 | tf_op jit(solution)/shard_map/cond/branch_1_fun/ppermute | solution.py:29
  78.4 7.0 %collective-permute-done.1 = bf16[8,16,1536]{2,1,0:T(8,128)(2,1)} collective-permute-done((bf16[8,16,1536]{2,1,0:T(8,128)(2,1)S(1)}, bf16[8,16,1536]{2,1,0:T(8,128)(2,1)}, u32[]{:S(2)}, u32[]{:S(2)}) %collective-permute-start.1) | collective-permute-done | bytes 393248 | tf_op jit(solution)/shard_map/cond/branch_1_fun/ppermute | solution.py:29
  85.5 2.0 %assemble.1 = bf16[1,8,32,1536]{3,2,1,0:T(8,128)(2,1)} custom-call(s32[1,2]{1,0:T(1,128)S(1)} %collective-permute-done.9.offsets, bf16[8,16,1536]{2,1,0:T(8,128)(2,1)S(1)} %collective-permute-done.15.local, bf16[8,16,1536]{2,1,0:T(8,128)(2,1)S(1)} %collective-permute-done.16.mixed, bf16[8,16,1536]{2,1,0:T(8,128)(2,1)} %get-tuple-element.56.moved), custom_call_target="tpu_custom_call" | custom-call | flops 1 | bytes 1 | tf_op jit(solution)/shard_map/assemble/pallas_call | solution.py:330
  (45 shorter events, 2.7 us)
Async XLA Ops:
  0.0 22.6 %copy-start.6 = (s32[1,2]{1,0:T(1,128)S(1)}, s32[1,2]{1,0:T(1,128)}, u32[]{:S(2)}) copy-start(s32[1,2]{1,0:T(1,128)} %offsets.5) | copy-start | bytes 28
  0.0 25.6 %copy-start.5 = (f32[1,4]{1,0:T(1,128)S(1)}, f32[1,4]{1,0:T(1,128)}, u32[]{:S(2)}) copy-start(f32[1,4]{1,0:T(1,128)} %scales.9) | copy-start | bytes 52
  0.0 25.6 %copy-start = (bf16[1,1536,4,288]{1,3,2,0:T(8,128)(2,1)S(1)}, bf16[1,1536,4,288]{1,3,2,0:T(8,128)(2,1)}, u32[]{:S(2)}) copy-start(bf16[1,1536,4,288]{1,3,2,0:T(8,128)(2,1)} %param.16) | copy-start | bytes 10616836
  4.0 17.6 %collective-permute-start.4 = (bf16[8,16,1536]{2,1,0:T(8,128)(2,1)}, bf16[8,16,1536]{2,1,0:T(8,128)(2,1)}, u32[]{:S(2)}, u32[]{:S(2)}) collective-permute-start(bf16[8,16,1536]{2,1,0:T(8,128)(2,1)} %slice_select_fusion.tile), channel_id=1, source_target_pairs={{0,2},{1,3},{2,0},{3,1},{4,6},{5,7},{6,4},{7,5},{8,10},{9,11},{10,... | collective-permute-start | bytes 1179656 | tf_op jit(solution)/shard_map/ppermute | solution.py:33
  8.0 11.7 %collective-permute-start.2 = (bf16[8,16,1536]{2,1,0:T(8,128)(2,1)S(1)}, bf16[8,16,1536]{2,1,0:T(8,128)(2,1)S(1)}, u32[]{:S(2)}, u32[]{:S(2)}) collective-permute-start(bf16[8,16,1536]{2,1,0:T(8,128)(2,1)S(1)} %slice.52), channel_id=1, source_target_pairs={{0,12},{4,0},{8,4},{12,8},{1,13},{5,1},{9,5},{13,9},{2,14},{6,2},{... | collective-permute-start | bytes 1179656 | tf_op jit(solution)/shard_map/cond/branch_0_fun/ppermute | solution.py:29
  21.6 4.0 %collective-permute-start.8 = (bf16[8,16,1536]{2,1,0:T(8,128)(2,1)}, bf16[8,16,1536]{2,1,0:T(8,128)(2,1)S(1)}, u32[]{:S(2)}, u32[]{:S(2)}) collective-permute-start(bf16[8,16,1536]{2,1,0:T(8,128)(2,1)} %get-tuple-element.55.tile), channel_id=1, source_target_pairs={{0,1},{1,0},{2,3},{3,2},{4,5},{5,4},{6,7},{7,6},{8,9},{9,8},{10,11... | collective-permute-start | bytes 1179656 | tf_op jit(solution)/shard_map/ppermute | solution.py:33
  21.6 9.5 %collective-permute-start.6 = (bf16[8,16,1536]{2,1,0:T(8,128)(2,1)}, bf16[8,16,1536]{2,1,0:T(8,128)(2,1)S(1)}, u32[]{:S(2)}, u32[]{:S(2)}) collective-permute-start(bf16[8,16,1536]{2,1,0:T(8,128)(2,1)} %slice_select_fusion.tile), channel_id=1, source_target_pairs={{0,1},{1,0},{2,3},{3,2},{4,5},{5,4},{6,7},{7,6},{8,9},{9,8},{10,11... | collective-permute-start | bytes 1179656 | tf_op jit(solution)/shard_map/ppermute | solution.py:33
  22.1 9.0 %collective-permute-start.7 = (bf16[8,16,1536]{2,1,0:T(8,128)(2,1)}, bf16[8,16,1536]{2,1,0:T(8,128)(2,1)S(1)}, u32[]{:S(2)}, u32[]{:S(2)}) collective-permute-start(bf16[8,16,1536]{2,1,0:T(8,128)(2,1)} %collective-permute-done.4), channel_id=1, source_target_pairs={{0,1},{1,0},{2,3},{3,2},{4,5},{5,4},{6,7},{7,6},{8,9},{9,8},{10,11... | collective-permute-start | bytes 1179656 | tf_op jit(solution)/shard_map/ppermute | solution.py:33
  22.1 14.5 %collective-permute-start.5 = (bf16[8,16,1536]{2,1,0:T(8,128)(2,1)}, bf16[8,16,1536]{2,1,0:T(8,128)(2,1)S(1)}, u32[]{:S(2)}, u32[]{:S(2)}) collective-permute-start(bf16[8,16,1536]{2,1,0:T(8,128)(2,1)} %get-tuple-element.55.tile), channel_id=1, source_target_pairs={{0,2},{1,3},{2,0},{3,1},{4,6},{5,7},{6,4},{7,5},{8,10},{9,11},{10,... | collective-permute-start | bytes 1179656 | tf_op jit(solution)/shard_map/ppermute | solution.py:33
  22.6 14.0 %collective-permute-start.9 = (s32[1,2]{1,0:T(1,128)S(1)}, s32[1,2]{1,0:T(1,128)S(1)}, u32[]{:S(2)}, u32[]{:S(2)}) collective-permute-start(s32[1,2]{1,0:T(1,128)S(1)} %copy-done.6), channel_id=1, source_target_pairs={{0,16},{16,0},{1,17},{17,1},{2,18},{18,2},{3,19},{19,3},{4,20},{20... | collective-permute-start | bytes 32 | tf_op jit(solution)/shard_map/ppermute | solution.py:29
  25.6 0.9 %copy-start.1 = (f32[1,32,1536]{2,1,0:T(8,128)S(1)}, f32[1,32,1536]{2,1,0:T(8,128)}, u32[]{:S(2)}) copy-start(f32[1,32,1536]{2,1,0:T(8,128)} %param.19) | copy-start | bytes 589828
  26.5 0.9 %copy-start.3 = (f32[1,32,1536]{2,1,0:T(8,128)S(1)}, f32[1,32,1536]{2,1,0:T(8,128)}, u32[]{:S(2)}) copy-start(f32[1,32,1536]{2,1,0:T(8,128)} %param.20) | copy-start | bytes 589828
  27.4 3.6 %copy-start.2 = (f32[1,32,1536]{2,1,0:T(8,128)S(1)}, f32[1,32,1536]{2,1,0:T(8,128)}, u32[]{:S(2)}) copy-start(f32[1,32,1536]{2,1,0:T(8,128)} %param.19) | copy-start | bytes 589828
  36.6 1.8 %collective-permute-start.10 = (bf16[8,16,1536]{2,1,0:T(8,128)(2,1)S(1)}, bf16[8,16,1536]{2,1,0:T(8,128)(2,1)S(1)}, u32[]{:S(2)}, u32[]{:S(2)}) collective-permute-start(bf16[8,16,1536]{2,1,0:T(8,128)(2,1)S(1)} %collective-permute-done.5), channel_id=1, source_target_pairs={{0,1},{1,0},{2,3},{3,2},{4,5},{5,4},{6,7},{7,6},{8,9},{9,8},{10,11... | collective-permute-start | bytes 1179656 | tf_op jit(solution)/shard_map/ppermute | solution.py:33
  38.4 23.0 %slice-start = ((s8[4718592]{0:T(1024)(128)(4,1)}), s8[4194304]{0:T(1024)(128)(4,1)S(1)}, s32[]{:S(2)}) async-start(s8[4718592]{0:T(1024)(128)(4,1)} %bitcast.39), calls=%async_computation | async-start | bytes 8388608
  41.5 19.9 %slice-start.1 = ((s8[4718592]{0:T(1024)(128)(4,1)}), s8[524288]{0:T(1024)(128)(4,1)S(1)}, s32[]{:S(2)}) async-start(s8[4718592]{0:T(1024)(128)(4,1)} %bitcast.39), calls=%async_computation.1 | async-start | bytes 1048576
  46.1 2.3 %collective-permute-start.11 = (bf16[1,2,128,384]{3,2,1,0:T(8,128)(2,1)S(1)}, bf16[1,2,128,384]{3,2,1,0:T(8,128)(2,1)S(1)}, u32[]{:S(2)}, u32[]{:S(2)}) collective-permute-start(bf16[1,2,128,384]{3,2,1,0:T(8,128)(2,1)S(1)} %get-tuple-element.50), channel_id=1, source_target_pairs={{0,1},{1,0},{2,3},{3,2},{4,5},{5,4},{6,7},{7,6},{8,9},{9,8},{10,11... | collective-permute-start | bytes 589832 | tf_op jit(solution)/shard_map/ppermute | solution.py:33
  47.4 14.1 %copy-start.4 = (f32[1,32,1536]{2,1,0:T(8,128)S(1)}, f32[1,32,1536]{2,1,0:T(8,128)}, u32[]{:S(2)}) copy-start(f32[1,32,1536]{2,1,0:T(8,128)} %param.21) | copy-start | bytes 589828
  47.4 14.1 %copy-start.7 = (bf16[8,16,1536]{2,1,0:T(8,128)(2,1)S(1)}, bf16[8,16,1536]{2,1,0:T(8,128)(2,1)}, u32[]{:S(2)}) copy-start(bf16[8,16,1536]{2,1,0:T(8,128)(2,1)} %get-tuple-element.55.tile) | copy-start | bytes 1179652
  53.1 10.2 %collective-permute-start.13 = (bf16[1,2,128,384]{3,2,1,0:T(8,128)(2,1)S(1)}, bf16[1,2,128,384]{3,2,1,0:T(8,128)(2,1)S(1)}, u32[]{:S(2)}, u32[]{:S(2)}) collective-permute-start(bf16[1,2,128,384]{3,2,1,0:T(8,128)(2,1)S(1)} %get-tuple-element.48), channel_id=1, source_target_pairs={{0,1},{1,0},{2,3},{3,2},{4,5},{5,4},{6,7},{7,6},{8,9},{9,8},{10,11... | collective-permute-start | bytes 589832 | tf_op jit(solution)/shard_map/ppermute | solution.py:33
  54.5 6.9 %collective-permute-start.12 = (bf16[2,1,128,384]{3,2,1,0:T(8,128)(2,1)S(1)}, bf16[2,1,128,384]{3,2,1,0:T(8,128)(2,1)S(1)}, u32[]{:S(2)}, u32[]{:S(2)}) collective-permute-start(bf16[2,1,128,384]{3,2,1,0:T(8,128)(2,1)S(1)} %pad_maximum_fusion.1), channel_id=1, source_target_pairs={{0,2},{1,3},{2,0},{3,1},{4,6},{5,7},{6,4},{7,5},{8,10},{9,11},{10,... | collective-permute-start | bytes 589832 | tf_op jit(solution)/shard_map/ppermute | solution.py:33
  63.4 6.1 %collective-permute-start.14 = (bf16[2,1,128,384]{3,2,1,0:T(8,128)(2,1)S(1)}, bf16[2,1,128,384]{3,2,1,0:T(8,128)(2,1)S(1)}, u32[]{:S(2)}, u32[]{:S(2)}) collective-permute-start(bf16[2,1,128,384]{3,2,1,0:T(8,128)(2,1)S(1)} %pad_maximum_fusion), channel_id=1, source_target_pairs={{0,2},{1,3},{2,0},{3,1},{4,6},{5,7},{6,4},{7,5},{8,10},{9,11},{10,... | collective-permute-start | bytes 589832 | tf_op jit(solution)/shard_map/ppermute | solution.py:33
  64.9 11.5 %collective-permute-start.16 = (bf16[8,16,1536]{2,1,0:T(8,128)(2,1)S(1)}, bf16[8,16,1536]{2,1,0:T(8,128)(2,1)S(1)}, u32[]{:S(2)}, u32[]{:S(2)}) collective-permute-start(bf16[8,16,1536]{2,1,0:T(8,128)(2,1)S(1)} %finish.2), channel_id=1, source_target_pairs={{0,16},{16,0},{1,17},{17,1},{2,18},{18,2},{3,19},{19,3},{4,20},{20... | collective-permute-start | bytes 1179656 | tf_op jit(solution)/shard_map/ppermute | solution.py:29
  72.3 13.1 %collective-permute-start.15 = (bf16[8,16,1536]{2,1,0:T(8,128)(2,1)S(1)}, bf16[8,16,1536]{2,1,0:T(8,128)(2,1)S(1)}, u32[]{:S(2)}, u32[]{:S(2)}) collective-permute-start(bf16[8,16,1536]{2,1,0:T(8,128)(2,1)S(1)} %finish.3), channel_id=1, source_target_pairs={{0,16},{16,0},{1,17},{17,1},{2,18},{18,2},{3,19},{19,3},{4,20},{20... | collective-permute-start | bytes 1179656 | tf_op jit(solution)/shard_map/ppermute | solution.py:29
  76.5 9.0 %collective-permute-start.1 = (bf16[8,16,1536]{2,1,0:T(8,128)(2,1)S(1)}, bf16[8,16,1536]{2,1,0:T(8,128)(2,1)}, u32[]{:S(2)}, u32[]{:S(2)}) collective-permute-start(bf16[8,16,1536]{2,1,0:T(8,128)(2,1)S(1)} %param.3), channel_id=1, source_target_pairs={{0,12},{4,0},{8,4},{12,8},{1,13},{5,1},{9,5},{13,9},{2,14},{6,2},{... | collective-permute-start | bytes 1179656 | tf_op jit(solution)/shard_map/cond/branch_1_fun/ppermute | solution.py:29

commit v4 on v3

--- a/solution.py
+++ b/solution.py
@@ -57,11 +57,11 @@
     return (x * lax.rsqrt(variance + eps_norm) * scale_row + shift_row).astype(jnp.bfloat16)
 
 
-def project_kernel(masks, rows, size, level, offsets, scales, *refs):
+def project_kernel(masks, rows, size, offsets, scales, *refs):
     count = len(masks)
     places = places_of(masks)
     pieces = refs[:count]
-    weight, shift, scale, out, tokens, padded, query_extra, key_extra = refs[count:]
+    weight, rows_ref, out, tokens, padded, query_extra, key_extra = refs[count:]
     piece_rows = pieces[0].shape[0]
     half = piece_rows // rows
     group = weight.shape[0]
@@ -70,7 +70,7 @@
     @pl.when(step == 0)
     def _():
         padded[...] = jnp.zeros_like(padded)
-        shift_row, scale_row = shift[pl.ds(level[0], 1), :], scale[pl.ds(level[0], 1), :]
+        shift_row, scale_row = rows_ref[0:1, :], rows_ref[1:2, :]
         column = lax.broadcasted_iota(jnp.int32, (piece_rows, lane), 1)
         local_row = lax.broadcasted_iota(jnp.int32, (piece_rows, lane), 0) // half
         chunk = math.gcd(piece_rows, 32)
@@ -109,9 +109,9 @@
         out[g, 2] = (value + ones).astype(jnp.bfloat16)
 
 
-def attend_kernel(own_count, own_masks, out_masks, size, scales, *refs):
+def attend_kernel(own_count, own_masks, out_masks, size, gentle, scales, *refs):
     queries, parts, out, held = refs[:own_count], refs[own_count:-2], refs[-2], refs[-1]
-    fast = all_gentle(scales)
+    fast = all_gentle(scales) if gentle is None else None
     head = pl.program_id(0)
     heads = held.shape[0]
     piece_rows = out.shape[1]
@@ -137,13 +137,11 @@
                 held[head, at : at + block, :] = mixed[:, :size] / mixed[:, size : size + 1]
                 at += block
 
-    @pl.when(fast)
-    def _():
-        body(False)
-
-    @pl.when(jnp.logical_not(fast))
-    def _():
-        body(True)
+    if gentle is None:
+        pl.when(fast)(lambda: body(False))
+        pl.when(jnp.logical_not(fast))(lambda: body(True))
+    else:
+        body(not gentle)
 
     @pl.when(head == heads - 1)
     def _():
@@ -152,6 +150,20 @@
             out[j] = jnp.concatenate(
                 [held[h, begin : begin + piece_rows, :] for h in range(heads)], -1
             ).astype(jnp.bfloat16)
+
+
+def rows_kernel(level, shift, scale, out):
+    out[0:1, :] = shift[pl.ds(level[0], 1), :]
+    out[1:2, :] = scale[pl.ds(level[0], 1), :]
+
+
+def mix_kernel(from_before, offsets, own, borrowed, out):
+    rows, half, _ = own.shape
+    lon = offsets[0, 1]
+    column = lax.broadcasted_iota(jnp.int32, (half, 1), 0)
+    far_side = column + half >= lon if from_before else column < lon
+    for r in range(rows):
+        out[r] = jnp.where(far_side, borrowed[r].astype(jnp.float32), own[r].astype(jnp.float32)).astype(jnp.bfloat16)
 
 
 def finish_kernel(masks, level, tile, *refs):
@@ -216,16 +228,15 @@
             pieces = pieces + [swapped(p, "seq", bit) for p in pieces]
         return pieces
 
-    def projected(pieces, held_masks):
+    def projected(pieces, held_masks, table_rows):
         tokens = len(pieces) * piece_rows
-        table = pl.BlockSpec(shift.shape, lambda h: (0, 0))
         return pl.pallas_call(
             functools.partial(project_kernel, held_masks, rows, size),
             grid=(heads // group,),
             out_shape=jax.ShapeDtypeStruct((heads, 3, tokens, lane), jnp.bfloat16),
-            in_specs=[SMEM, SMEM, SMEM]
+            in_specs=[SMEM, SMEM]
             + [pl.BlockSpec((piece_rows, width), lambda h: (0, 0))] * len(pieces)
-            + [pl.BlockSpec((group, 3 * size, width), lambda h: (h, 0, 0)), table, table],
+            + [pl.BlockSpec((group, 3 * size, width), lambda h: (h, 0, 0)), pl.BlockSpec((2, width), lambda h: (0, 0))],
             out_specs=pl.BlockSpec((group, 3, tokens, lane), lambda h: (h, 0, 0, 0)),
             scratch_shapes=[
                 pltpu.VMEM((tokens, width), jnp.bfloat16),
@@ -236,10 +247,9 @@
             compiler_params=params(),
             cost_estimate=small,
             name="project",
-        )(timesteps, offsets, logit_scale, *[p.reshape(piece_rows, width) for p in pieces], weight, shift, scale)
+        )(offsets, logit_scale, *[p.reshape(piece_rows, width) for p in pieces], weight, table_rows)
 
     top = bits[-1]
-    local_masks = gathered_masks([0, top], bits)
     near_masks = gathered_masks([0], bits)
     far_masks = [m | top for m in near_masks]
 
@@ -247,31 +257,52 @@
     local = jnp.where(big, low, high)
     local_far = swapped(local, "seq", top)
 
-    def mixed_half(from_before, tile, lon):
-        low, high = tile[:, :half], tile[:, half:]
+    def mixed_half(from_before, low, high):
         own = high if from_before else low
         borrowed = passed_along(own, "win", 1 if from_before else -1)
-        column = lax.broadcasted_iota(jnp.int32, own.shape, 1)
-        return jnp.where(column + half >= lon if from_before else column < lon, borrowed, own)
-
-    mixed = lax.cond(big, functools.partial(mixed_half, True), functools.partial(mixed_half, False), tile, lon)
+        table_rows = pl.pallas_call(
+            rows_kernel,
+            out_shape=jax.ShapeDtypeStruct((2, width), jnp.float32),
+            in_specs=[SMEM, VMEM, VMEM],
+            out_specs=VMEM,
+            compiler_params=params(),
+            cost_estimate=small,
+            name="rows",
+        )(timesteps, shift, scale)
+        near_heads = projected(gathered([low if from_before else high]), near_masks, table_rows)
+        borrowed, near_heads = lax.optimization_barrier((borrowed, near_heads))
+        mixed = pl.pallas_call(
+            functools.partial(mix_kernel, from_before),
+            out_shape=half_shape,
+            in_specs=[SMEM, VMEM, VMEM],
+            out_specs=VMEM,
+            compiler_params=params(),
+            cost_estimate=small,
+            name="mix",
+        )(offsets, own, borrowed)
+        return mixed, near_heads, table_rows
+
+    mixed, local_near, table_rows = lax.cond(
+        big, functools.partial(mixed_half, True), functools.partial(mixed_half, False), low, high
+    )
     local_far, mixed = lax.optimization_barrier((local_far, mixed))
-    local_heads = projected(gathered([local, local_far]), local_masks)
+    local_heads = [local_near, projected(gathered([local_far]), far_masks, table_rows)]
     mixed_far = swapped(mixed, "seq", top)
-    near_heads = projected(gathered([mixed]), near_masks)
+    near_heads = projected(gathered([mixed]), near_masks, table_rows)
     mixed_far, local_heads, near_heads, source_offsets = lax.optimization_barrier(
         (mixed_far, local_heads, near_heads, source_offsets)
     )
-    far_heads = projected(gathered([mixed_far]), far_masks)
-
-    def attended(own, own_masks, local_heads):
+    far_heads = projected(gathered([mixed_far]), far_masks, table_rows)
+    own_masks = near_masks + far_masks
+
+    def attended(own, local_heads, gentle=None):
         def block(array, kinds):
             return pl.BlockSpec((1, kinds, array.shape[2], lane), lambda h: (h, 0, 0, 0))
 
-        parts = [local_heads, near_heads, far_heads]
+        parts = [*local_heads, near_heads, far_heads]
         total = sum(o.shape[2] for o in own)
         return pl.pallas_call(
-            functools.partial(attend_kernel, len(own), own_masks, masks, size),
+            functools.partial(attend_kernel, len(own), own_masks, masks, size, gentle),
             grid=(heads,),
             in_specs=[SMEM] + [block(o, 1) for o in own] + [block(p, 3) for p in parts],
             out_specs=pl.BlockSpec((n, piece_rows, inner), lambda h: (0, 0, 0)),
@@ -287,7 +318,6 @@
         return held[:, :middle], swapped(held[:, middle:], "seq", bit)
 
     def returned(held):
-        held = jnp.concatenate(held, 0)
         for bit in bits[1:]:
             held = jnp.concatenate(hop(held, bit), 0)
         return [held[g, 0] for g in range(n)]
@@ -312,13 +342,16 @@
             name="finish",
         )(timesteps, residual, *groups, out_weight[0], gate)
 
-    mixed_kept, mixed_received = hop(attended([near_heads, far_heads], near_masks + far_masks, local_heads)[None], bits[0])
-    local_query, mixed_received = lax.optimization_barrier((local_heads, mixed_received))
-    mixed_out = returned((mixed_kept, mixed_received))
-    local_kept, local_received = hop(attended([local_query], local_masks, local_query)[None], bits[0])
+    mixed_held = jnp.concatenate(
+        hop(attended([near_heads, far_heads], local_heads)[None], bits[0]), 0
+    )
+    local_query, mixed_held = lax.optimization_barrier((local_heads, mixed_held))
+    mixed_out = returned(mixed_held)
+    local_attended = attended(local_query, local_query)
+    local_kept, local_received = hop(local_attended[None], bits[0])
     mixed_done, local_received = lax.optimization_barrier((finished(mixed_out, mixed), local_received))
     mixed_sent = passed_along(mixed_done, "segment", 1)
-    local_done = finished(returned((local_kept, local_received)), local)
+    local_done = finished(returned(jnp.concatenate([local_kept, local_received], 0)), local)
     local_sent = passed_along(local_done, "segment", 1)
     mixed_sent, _ = lax.optimization_barrier((mixed_sent, local_done))
     moved = lax.cond(

time: 87.9 us -> 78.1 us (0.89)
  waiting for transfers between devices: 29 us -> 17.4 us
  starting transfers between devices: 18.7 us -> 23.5 us
  Pallas kernels: 27.9 us -> 31.3 us
  other arithmetic: 4.45 us -> 1.28 us
  local copies, waits for them, and re-layouts: 5.11 us -> 2.04 us
    ppermute x5, waiting for transfers between devices: 16.4 us -> 9.85 us  [passed_along(): lax.ppermute(block, axis, [(i, (i + distance) % n) for i in range(n)])]
    ppermute x5, starting transfers between devices: 8.96 us -> 14.6 us  [passed_along(): lax.ppermute(block, axis, [(i, (i + distance) % n) for i in range(n)])]
    ppermute x10, waiting for transfers between devices: 12.6 us -> 7.51 us  [swapped(): lax.ppermute(block, axis, [(i, i ^ mask) for i in range(lax.axis_size(axi...]
    select_n x2 -> x0, other arithmetic: 3.76 us -> none  [the longest x1 1.91 us: shards(): local = jnp.where(big, low, high)]
    pallas_call x0 -> x2, Pallas kernels: none -> 2.93 us  [the longest x1 2.27 us: mixed_half(): pl.pallas_call(rows_kernel, out_shape=jax.ShapeDtypeStruct((2, width), jn...]
    pallas_call x3 -> x4, Pallas kernels: 12.2 us -> 14.6 us  [projected(): pl.pallas_call(functools.partial(project_kernel, held_masks, rows, size),...]
    unnamed x20 -> x12, local copies, waits for them, and re-layouts: 1.89 us -> 0.03 us
    slice x0 -> x1, other arithmetic: none -> 1.2 us  [shards(): low, high = (tile[:, :half], tile[:, half:])]
  transfers between devices with their start and end apart: 15 -> 15, of which waited for: 7 -> 8; matrix products, arithmetic and copies ran while one was open for 5% -> 1% of each run, Pallas kernels for 16% -> 28%
where the time goes in v4:
time: 78.1 us; the launch traced here: 77.9 us
  Pallas kernels  31.3 us (40%)
  starting transfers between devices  23.5 us (30%)
  waiting for transfers between devices  17.4 us (22%)
  between operations  2.21 us (3%)
  local copies, waits for them, and re-layouts  2.04 us (3%)
  other arithmetic  1.28 us (2%)
    pallas_call x4, Pallas kernels, projected(): pl.pallas_call(functools.partial(project_kernel, held_masks, rows, size),...  14.6 us
    ppermute x5, starting transfers between devices, passed_along(): lax.ppermute(block, axis, [(i, (i + distance) % n) for i in range(n)])  14.6 us
    ppermute x5, waiting for transfers between devices, passed_along(): lax.ppermute(block, axis, [(i, (i + distance) % n) for i in range(n)])  9.85 us
    ppermute x10, starting transfers between devices, swapped(): lax.ppermute(block, axis, [(i, i ^ mask) for i in range(lax.axis_size(axi...  8.85 us
    pallas_call x2, Pallas kernels, attended(): pl.pallas_call(functools.partial(attend_kernel, len(own), own_masks, mask...  8.03 us
    ppermute x10, waiting for transfers between devices, swapped(): lax.ppermute(block, axis, [(i, i ^ mask) for i in range(lax.axis_size(axi...  7.51 us
    pallas_call x2, Pallas kernels, finished(): pl.pallas_call(functools.partial(finish_kernel, order), grid=(width // bl...  3.66 us
    pallas_call x1, Pallas kernels, mixed_half(): pl.pallas_call(rows_kernel, out_shape=jax.ShapeDtypeStruct((2, width), jn...  2.27 us
  transfers between devices with their start and end apart: 15, of which 8 were waited for; matrix products, arithmetic and copies ran while one was open for 1% of the time, Pallas kernels for 28%

profile of v4, /device:TPU:0, one launch (start us, length us, event | category | flops | bytes accessed | tf_op | source)
XLA Modules:
  0.0 77.9 jit_solution(8982703548244861004)
XLA Ops:
  0.0 1.2 %slice.63 = s32[1,1]{1,0:T(1,128)} slice(s32[1,2]{1,0:T(1,128)} %offsets.5), slice={[0:1], [1:2]} | slice | bytes 8 | tf_op jit(solution)/shard_map/slice | solution.py:221
  1.9 1.2 %fusion = (bf16[8,16,1536]{2,1,0:T(8,128)(2,1)S(1)}, bf16[8,16,1536]{2,1,0:T(8,128)(2,1)S(1)}, bf16[8,16,1536]{2,1,0:T(8,128)(2,1)S(1)}) fusion(bf16[8,32,1536]{2,1,0:T(8,128)(2,1)} %bitcast.62, pred[]{:T(512)} %bitcast.4), kind=kLoop, calls=%fused_computation.11 | loop fusion | flops 196608 | bytes 1966081 | tf_op jit(solution)/shard_map/slice | solution.py:256
  3.1 3.0 %collective-permute-start.6 = (bf16[8,16,1536]{2,1,0:T(8,128)(2,1)S(1)}, bf16[8,16,1536]{2,1,0:T(8,128)(2,1)S(1)}, u32[]{:S(2)}, u32[]{:S(2)}) collective-permute-start(bf16[8,16,1536]{2,1,0:T(8,128)(2,1)S(1)} %get-tuple-element.95.tile), channel_id=1, source_target_pairs={{0,2},{1,3},{2,0},{3,1},{4,6},{5,7},{6,4},{7,5},{8,10},{9,11},{10,... | collective-permute-start | bytes 1179656 | tf_op jit(solution)/shard_map/ppermute | solution.py:33
  6.1 13.5 %conditional.2 = (bf16[8,16,1536]{2,1,0:T(8,128)(2,1)S(1)}, bf16[4,3,256,128]{3,2,1,0:T(8,128)(2,1)S(1)}, f32[2,1536]{1,0:T(2,128)}) conditional(s32[]{:T(128)} %convert_element_type.9, (bf16[8,16,1536]{2,1,0:T(8,128)(2,1)S(1)}, bf16[8,16,1536]{2,1,0:T(8,128)(2,1)S(1)}, s32[1]{0:T(128)}, f32[32,1536]{1,0:T(8,128)}, f32[32,1536]{1,0:T(8,128)}, ...), branch_computations={%region_0.1_spmd, %region_1.2_spmd} | conditional | flops 3 | bytes 3145895 | solution.py:285
  6.1 3.6 %collective-permute-start = (bf16[8,16,1536]{2,1,0:T(8,128)(2,1)S(1)}, bf16[8,16,1536]{2,1,0:T(8,128)(2,1)S(1)}, u32[]{:S(2)}, u32[]{:S(2)}) collective-permute-start(bf16[8,16,1536]{2,1,0:T(8,128)(2,1)S(1)} %get-tuple-element.43.own), channel_id=1, source_target_pairs={{0,12},{4,0},{8,4},{12,8},{1,13},{5,1},{9,5},{13,9},{2,14},{6,2},{... | collective-permute-start | bytes 1179656 | tf_op jit(solution)/shard_map/cond/branch_0_fun/ppermute | solution.py:29
  9.8 2.3 %rows.2.refs_3_ = f32[2,1536]{1,0:T(2,128)} custom-call(s32[1]{0:T(128)} %get-tuple-element.47.level, f32[32,1536]{1,0:T(8,128)} %get-tuple-element.48.shift, f32[32,1536]{1,0:T(8,128)} %get-tuple-element.49.scale), custom_call_target="tpu_custom_call" | custom-call | flops 1 | bytes 1 | tf_op jit(solution)/shard_map/cond/branch_0_fun/rows/pallas_call | solution.py:263
  12.0 4.0 %project.5 = bf16[4,3,256,128]{3,2,1,0:T(8,128)(2,1)S(1)} custom-call(s32[1,2]{1,0:T(1,128)} %get-tuple-element.42.offsets, f32[1,4]{1,0:T(1,128)} %get-tuple-element.44.scales, bf16[128,1536]{1,0:T(8,128)(2,1)S(1)} %bitcast.60, bf16[128,1536]{1,0:T(8,128)(2,1)S(1)} %bitcast.51, bf16[4,288,1536]{2,1,0:T(8,128)(2,1)} %get-tuple-element.46.refs_2_, ...), custom_call_target="tpu_custom_call" | custom-call | flops 1 | bytes 1 | tf_op jit(solution)/shard_map/cond/branch_0_fun/project/pallas_call | solution.py:233
  16.0 2.7 %collective-permute-done.borrowed = bf16[8,16,1536]{2,1,0:T(8,128)(2,1)S(1)} collective-permute-done((bf16[8,16,1536]{2,1,0:T(8,128)(2,1)S(1)}, bf16[8,16,1536]{2,1,0:T(8,128)(2,1)S(1)}, u32[]{:S(2)}, u32[]{:S(2)}) %collective-permute-start) | collective-permute-done | bytes 393248 | tf_op jit(solution)/shard_map/cond/branch_0_fun/ppermute | solution.py:29
  18.8 0.7 mix.2
  20.8 2.2 %collective-permute-start.10 = (s32[1,2]{1,0:T(1,128)}, s32[1,2]{1,0:T(1,128)S(1)}, u32[]{:S(2)}, u32[]{:S(2)}) collective-permute-start(s32[1,2]{1,0:T(1,128)} %offsets.5), channel_id=1, source_target_pairs={{0,16},{16,0},{1,17},{17,1},{2,18},{18,2},{3,19},{19,3},{4,20},{20... | collective-permute-start | bytes 32 | tf_op jit(solution)/shard_map/ppermute | solution.py:29
  23.0 4.0 %project.8.refs_0_.refs_4_ = bf16[4,3,256,128]{3,2,1,0:T(8,128)(2,1)S(1)} custom-call(s32[1,2]{1,0:T(1,128)S(1)} %copy-done.2, f32[1,4]{1,0:T(1,128)} %scales.9, bf16[128,1536]{1,0:T(8,128)(2,1)S(1)} %bitcast.59, bf16[128,1536]{1,0:T(8,128)(2,1)S(1)} %bitcast.50, bf16[4,288,1536]{2,1,0:T(8,128)(2,1)} %bitcast.56, f32[2,1536]{1,0:T(2,128)} %get-tuple-element.82.refs_3_), custom_call_target="tpu_custom_call" | custom-call | flops 1 | bytes 1 | tf_op jit(solution)/shard_map/project/pallas_call | solution.py:233
  27.1 3.2 %project.7.refs_3_.refs_1_ = bf16[4,3,256,128]{3,2,1,0:T(8,128)(2,1)S(1)} custom-call(s32[1,2]{1,0:T(1,128)S(1)} %copy-done.2, f32[1,4]{1,0:T(1,128)S(1)} %copy-done.5, bf16[128,1536]{1,0:T(8,128)(2,1)S(1)} %bitcast.47, bf16[128,1536]{1,0:T(8,128)(2,1)S(1)} %bitcast.49, bf16[4,288,1536]{2,1,0:T(8,128)(2,1)S(1)} %bitcast.57, f32[2,1536]{1,0:T(2,128)} %get-tuple-element.82.refs_3_), custom_call_target="tpu_custom_call" | custom-call | flops 1 | bytes 1 | tf_op jit(solution)/shard_map/project/pallas_call | solution.py:233
  30.3 1.0 %collective-permute-done.7 = bf16[8,16,1536]{2,1,0:T(8,128)(2,1)S(1)} collective-permute-done((bf16[8,16,1536]{2,1,0:T(8,128)(2,1)S(1)}, bf16[8,16,1536]{2,1,0:T(8,128)(2,1)S(1)}, u32[]{:S(2)}, u32[]{:S(2)}) %collective-permute-start.7) | collective-permute-done | bytes 393248 | tf_op jit(solution)/shard_map/ppermute | solution.py:33
  31.3 1.7 %collective-permute-done.11 = bf16[8,16,1536]{2,1,0:T(8,128)(2,1)S(1)} collective-permute-done((bf16[8,16,1536]{2,1,0:T(8,128)(2,1)S(1)}, bf16[8,16,1536]{2,1,0:T(8,128)(2,1)S(1)}, u32[]{:S(2)}, u32[]{:S(2)}) %collective-permute-start.11) | collective-permute-done | bytes 393248 | tf_op jit(solution)/shard_map/ppermute | solution.py:33
  33.0 3.4 %project.9.refs_1_.refs_5_ = bf16[4,3,256,128]{3,2,1,0:T(8,128)(2,1)S(1)} custom-call(s32[1,2]{1,0:T(1,128)S(1)} %copy-done.2, f32[1,4]{1,0:T(1,128)S(1)} %copy-done.5, bf16[128,1536]{1,0:T(8,128)(2,1)S(1)} %bitcast.48, bf16[128,1536]{1,0:T(8,128)(2,1)S(1)} %bitcast.53, bf16[4,288,1536]{2,1,0:T(8,128)(2,1)S(1)} %bitcast.58, f32[2,1536]{1,0:T(2,128)} %get-tuple-element.82.refs_3_), custom_call_target="tpu_custom_call" | custom-call | flops 1 | bytes 1 | tf_op jit(solution)/shard_map/project/pallas_call | solution.py:233
  36.4 4.0 %attend.2 = bf16[4,128,384]{2,1,0:T(8,128)(2,1)S(1)} custom-call(f32[1,4]{1,0:T(1,128)S(1)} %copy-done.5, bf16[4,3,256,128]{3,2,1,0:T(8,128)(2,1)S(1)} %project.8.refs_0_.refs_4_, bf16[4,3,256,128]{3,2,1,0:T(8,128)(2,1)S(1)} %project.9.refs_1_.refs_5_, bf16[4,3,256,128]{3,2,1,0:T(8,128)(2,1)S(1)} %get-tuple-element.88.refs_2_.refs_0_, ...), custom_call_target="tpu_custom_call" | custom-call | flops 1 | bytes 1 | tf_op jit(solution)/shard_map/attend/pallas_call | solution.py:304
  40.5 1.7 %collective-permute-start.12 = (bf16[1,2,128,384]{3,2,1,0:T(8,128)(2,1)S(1)}, bf16[1,2,128,384]{3,2,1,0:T(8,128)(2,1)S(1)}, u32[]{:S(2)}, u32[]{:S(2)}) collective-permute-start(bf16[1,2,128,384]{3,2,1,0:T(8,128)(2,1)S(1)} %get-tuple-element.102), channel_id=1, source_target_pairs={{0,1},{1,0},{2,3},{3,2},{4,5},{5,4},{6,7},{7,6},{8,9},{9,8},{10,11... | collective-permute-start | bytes 589832 | tf_op jit(solution)/shard_map/ppermute | solution.py:33
  43.4 0.7 collective-permute-start.13
  44.1 4.0 %attend.3 = bf16[4,128,384]{2,1,0:T(8,128)(2,1)S(1)} custom-call(f32[1,4]{1,0:T(1,128)S(1)} %copy-done.5, bf16[4,3,256,128]{3,2,1,0:T(8,128)(2,1)S(1)} %get-tuple-element.88.refs_2_.refs_0_, bf16[4,3,256,128]{3,2,1,0:T(8,128)(2,1)S(1)} %project.7.refs_3_.refs_1_, bf16[4,3,256,128]{3,2,1,0:T(8,128)(2,1)S(1)} %get-tuple-element.88.refs_2_.refs_0_, ...), custom_call_target="tpu_custom_call" | custom-call | flops 1 | bytes 1 | tf_op jit(solution)/shard_map/attend/pallas_call | solution.py:304
  48.2 1.7 %collective-permute-start.14 = (bf16[1,2,128,384]{3,2,1,0:T(8,128)(2,1)S(1)}, bf16[1,2,128,384]{3,2,1,0:T(8,128)(2,1)S(1)}, u32[]{:S(2)}, u32[]{:S(2)}) collective-permute-start(bf16[1,2,128,384]{3,2,1,0:T(8,128)(2,1)S(1)} %get-tuple-element.98), channel_id=1, source_target_pairs={{0,1},{1,0},{2,3},{3,2},{4,5},{5,4},{6,7},{7,6},{8,9},{9,8},{10,11... | collective-permute-start | bytes 589832 | tf_op jit(solution)/shard_map/ppermute | solution.py:33
  49.8 0.8 %collective-permute-done.13 = bf16[2,1,128,384]{3,2,1,0:T(8,128)(2,1)S(1)} collective-permute-done((bf16[2,1,128,384]{3,2,1,0:T(8,128)(2,1)S(1)}, bf16[2,1,128,384]{3,2,1,0:T(8,128)(2,1)S(1)}, u32[]{:S(2)}, u32[]{:S(2)}) %collective-permute-start.13) | collective-permute-done | bytes 196640 | tf_op jit(solution)/shard_map/ppermute | solution.py:33
  50.7 1.8 %finish.2 = bf16[8,16,1536]{2,1,0:T(8,128)(2,1)S(1)} custom-call(s32[1]{0:T(128)S(6)} %copy.18.level, bf16[8,16,1536]{2,1,0:T(8,128)(2,1)S(1)} %get-tuple-element.79.tile, bf16[128,384]{1,0:T(8,128)(2,1)S(1)} %get-tuple-element.100.refs_0_, bf16[128,384]{1,0:T(8,128)(2,1)S(1)} %get-tuple-element.99.refs_1_, bf16[128,384]{1,0:T(8,128)(2,1)S(1)} %get-tuple-element.106.refs_2_, ...), custom_call_target="tpu_custom_call" | custom-call | flops 1 | bytes 1 | tf_op jit(solution)/shard_map/finish/pallas_call | solution.py:332
  52.6 0.7 collective-permute-start.15
  53.3 2.2 %collective-permute-start.17 = (bf16[8,16,1536]{2,1,0:T(8,128)(2,1)S(1)}, bf16[8,16,1536]{2,1,0:T(8,128)(2,1)S(1)}, u32[]{:S(2)}, u32[]{:S(2)}) collective-permute-start(bf16[8,16,1536]{2,1,0:T(8,128)(2,1)S(1)} %finish.2), channel_id=1, source_target_pairs={{0,16},{16,0},{1,17},{17,1},{2,18},{18,2},{3,19},{19,3},{4,20},{20... | collective-permute-start | bytes 1179656 | tf_op jit(solution)/shard_map/ppermute | solution.py:29
  55.5 3.5 %collective-permute-done.15 = bf16[2,1,128,384]{3,2,1,0:T(8,128)(2,1)S(1)} collective-permute-done((bf16[2,1,128,384]{3,2,1,0:T(8,128)(2,1)S(1)}, bf16[2,1,128,384]{3,2,1,0:T(8,128)(2,1)S(1)}, u32[]{:S(2)}, u32[]{:S(2)}) %collective-permute-start.15) | collective-permute-done | bytes 196640 | tf_op jit(solution)/shard_map/ppermute | solution.py:33
  59.1 1.8 %finish.3 = bf16[8,16,1536]{2,1,0:T(8,128)(2,1)S(1)} custom-call(s32[1]{0:T(128)S(6)} %copy.18.level, bf16[8,16,1536]{2,1,0:T(8,128)(2,1)S(1)} %get-tuple-element.95.tile, bf16[128,384]{1,0:T(8,128)(2,1)S(1)} %slice_bitcast_fusion.4.refs_0_, bf16[128,384]{1,0:T(8,128)(2,1)S(1)} %slice_bitcast_fusion.5.refs_1_, ...), custom_call_target="tpu_custom_call" | custom-call | flops 1 | bytes 1 | tf_op jit(solution)/shard_map/finish/pallas_call | solution.py:332
  60.9 2.3 %collective-permute-start.16 = (bf16[8,16,1536]{2,1,0:T(8,128)(2,1)S(1)}, bf16[8,16,1536]{2,1,0:T(8,128)(2,1)S(1)}, u32[]{:S(2)}, u32[]{:S(2)}) collective-permute-start(bf16[8,16,1536]{2,1,0:T(8,128)(2,1)S(1)} %finish.3), channel_id=1, source_target_pairs={{0,16},{16,0},{1,17},{17,1},{2,18},{18,2},{3,19},{19,3},{4,20},{20... | collective-permute-start | bytes 1179656 | tf_op jit(solution)/shard_map/ppermute | solution.py:29
  64.5 0.9 %collective-permute-done.17.mixed = bf16[8,16,1536]{2,1,0:T(8,128)(2,1)S(1)} collective-permute-done((bf16[8,16,1536]{2,1,0:T(8,128)(2,1)S(1)}, bf16[8,16,1536]{2,1,0:T(8,128)(2,1)S(1)}, u32[]{:S(2)}, u32[]{:S(2)}) %collective-permute-start.17) | collective-permute-done | bytes 393248 | tf_op jit(solution)/shard_map/ppermute | solution.py:29
  65.4 10.4 %conditional.3 = (bf16[8,16,1536]{2,1,0:T(8,128)(2,1)}) conditional(s32[]{:T(128)} %bitcast.29, bf16[8,16,1536]{2,1,0:T(8,128)(2,1)S(1)} %collective-permute-done.17.mixed, bf16[8,16,1536]{2,1,0:T(8,128)(2,1)S(1)} %collective-permute-done.17.mixed), branch_computations={%region_2.3_spmd, %region_3.4_spmd} | conditional | bytes 1572912 | solution.py:357
  65.4 4.2 %collective-permute-start.5 = (bf16[8,16,1536]{2,1,0:T(8,128)(2,1)S(1)}, bf16[8,16,1536]{2,1,0:T(8,128)(2,1)}, u32[]{:S(2)}, u32[]{:S(2)}) collective-permute-start(bf16[8,16,1536]{2,1,0:T(8,128)(2,1)S(1)} %param.3), channel_id=1, source_target_pairs={{0,12},{4,0},{8,4},{12,8},{1,13},{5,1},{9,5},{13,9},{2,14},{6,2},{... | collective-permute-start | bytes 1179656 | tf_op jit(solution)/shard_map/cond/branch_1_fun/ppermute | solution.py:29
  69.6 6.2 %collective-permute-done.5 = bf16[8,16,1536]{2,1,0:T(8,128)(2,1)} collective-permute-done((bf16[8,16,1536]{2,1,0:T(8,128)(2,1)S(1)}, bf16[8,16,1536]{2,1,0:T(8,128)(2,1)}, u32[]{:S(2)}, u32[]{:S(2)}) %collective-permute-start.5) | collective-permute-done | bytes 393248 | tf_op jit(solution)/shard_map/cond/branch_1_fun/ppermute | solution.py:29
  75.8 2.0 %assemble.1 = bf16[1,8,32,1536]{3,2,1,0:T(8,128)(2,1)} custom-call(s32[1,2]{1,0:T(1,128)S(1)} %collective-permute-done.10.offsets, bf16[8,16,1536]{2,1,0:T(8,128)(2,1)S(1)} %collective-permute-done.16.local, bf16[8,16,1536]{2,1,0:T(8,128)(2,1)S(1)} %collective-permute-done.17.mixed, bf16[8,16,1536]{2,1,0:T(8,128)(2,1)} %get-tuple-element.113.moved), custom_call_target="tpu_custom_call" | custom-call | flops 1 | bytes 1 | tf_op jit(solution)/shard_map/assemble/pallas_call | solution.py:363
  (39 shorter events, 2.4 us)
Async XLA Ops:
  3.1 16.5 %collective-permute-start.6 = (bf16[8,16,1536]{2,1,0:T(8,128)(2,1)S(1)}, bf16[8,16,1536]{2,1,0:T(8,128)(2,1)S(1)}, u32[]{:S(2)}, u32[]{:S(2)}) collective-permute-start(bf16[8,16,1536]{2,1,0:T(8,128)(2,1)S(1)} %get-tuple-element.95.tile), channel_id=1, source_target_pairs={{0,2},{1,3},{2,0},{3,1},{4,6},{5,7},{6,4},{7,5},{8,10},{9,11},{10,... | collective-permute-start | bytes 1179656 | tf_op jit(solution)/shard_map/ppermute | solution.py:33
  6.1 16.9 %copy-start.2 = (s32[1,2]{1,0:T(1,128)S(1)}, s32[1,2]{1,0:T(1,128)}, u32[]{:S(2)}) copy-start(s32[1,2]{1,0:T(1,128)} %offsets.5) | copy-start | bytes 28
  6.1 12.7 %copy-start.3 = (s32[1,2]{1,0:T(1,128)S(1)}, s32[1,2]{1,0:T(1,128)}, u32[]{:S(2)}) copy-start(s32[1,2]{1,0:T(1,128)} %get-tuple-element.42.offsets) | copy-start | bytes 28 | tf_op jit(solution)/shard_map/cond
  6.1 5.9 %collective-permute-start.1 = (bf16[8,16,1536]{2,1,0:T(8,128)(2,1)S(1)}, bf16[8,16,1536]{2,1,0:T(8,128)(2,1)S(1)}, u32[]{:S(2)}, u32[]{:S(2)}) collective-permute-start(bf16[8,16,1536]{2,1,0:T(8,128)(2,1)S(1)} %get-tuple-element.45), channel_id=1, source_target_pairs={{0,1},{1,0},{2,3},{3,2},{4,5},{5,4},{6,7},{7,6},{8,9},{9,8},{10,11... | collective-permute-start | bytes 1179656 | tf_op jit(solution)/shard_map/cond/branch_0_fun/ppermute | solution.py:33
  6.1 12.6 %collective-permute-start = (bf16[8,16,1536]{2,1,0:T(8,128)(2,1)S(1)}, bf16[8,16,1536]{2,1,0:T(8,128)(2,1)S(1)}, u32[]{:S(2)}, u32[]{:S(2)}) collective-permute-start(bf16[8,16,1536]{2,1,0:T(8,128)(2,1)S(1)} %get-tuple-element.43.own), channel_id=1, source_target_pairs={{0,12},{4,0},{8,4},{12,8},{1,13},{5,1},{9,5},{13,9},{2,14},{6,2},{... | collective-permute-start | bytes 1179656 | tf_op jit(solution)/shard_map/cond/branch_0_fun/ppermute | solution.py:29
  19.6 7.4 %copy-start.1 = (bf16[1,1536,4,288]{1,3,2,0:T(8,128)(2,1)S(1)}, bf16[1,1536,4,288]{1,3,2,0:T(8,128)(2,1)}, u32[]{:S(2)}) copy-start(bf16[1,1536,4,288]{1,3,2,0:T(8,128)(2,1)} %param.16) | copy-start | bytes 10616836
  19.6 7.4 %copy-start.5 = (f32[1,4]{1,0:T(1,128)S(1)}, f32[1,4]{1,0:T(1,128)}, u32[]{:S(2)}) copy-start(f32[1,4]{1,0:T(1,128)} %scales.9) | copy-start | bytes 52
  19.6 3.4 %collective-permute-start.9 = (bf16[8,16,1536]{2,1,0:T(8,128)(2,1)S(1)}, bf16[8,16,1536]{2,1,0:T(8,128)(2,1)S(1)}, u32[]{:S(2)}, u32[]{:S(2)}) collective-permute-start(bf16[8,16,1536]{2,1,0:T(8,128)(2,1)S(1)} %get-tuple-element.79.tile), channel_id=1, source_target_pairs={{0,1},{1,0},{2,3},{3,2},{4,5},{5,4},{6,7},{7,6},{8,9},{9,8},{10,11... | collective-permute-start | bytes 1179656 | tf_op jit(solution)/shard_map/ppermute | solution.py:33
  19.7 7.3 %collective-permute-start.8 = (bf16[8,16,1536]{2,1,0:T(8,128)(2,1)S(1)}, bf16[8,16,1536]{2,1,0:T(8,128)(2,1)S(1)}, u32[]{:S(2)}, u32[]{:S(2)}) collective-permute-start(bf16[8,16,1536]{2,1,0:T(8,128)(2,1)S(1)} %collective-permute-done.6), channel_id=1, source_target_pairs={{0,1},{1,0},{2,3},{3,2},{4,5},{5,4},{6,7},{7,6},{8,9},{9,8},{10,11... | collective-permute-start | bytes 1179656 | tf_op jit(solution)/shard_map/ppermute | solution.py:33
  20.2 11.1 %collective-permute-start.7 = (bf16[8,16,1536]{2,1,0:T(8,128)(2,1)S(1)}, bf16[8,16,1536]{2,1,0:T(8,128)(2,1)S(1)}, u32[]{:S(2)}, u32[]{:S(2)}) collective-permute-start(bf16[8,16,1536]{2,1,0:T(8,128)(2,1)S(1)} %get-tuple-element.79.tile), channel_id=1, source_target_pairs={{0,2},{1,3},{2,0},{3,1},{4,6},{5,7},{6,4},{7,5},{8,10},{9,11},{10,... | collective-permute-start | bytes 1179656 | tf_op jit(solution)/shard_map/ppermute | solution.py:33
  20.8 9.6 %collective-permute-start.10 = (s32[1,2]{1,0:T(1,128)}, s32[1,2]{1,0:T(1,128)S(1)}, u32[]{:S(2)}, u32[]{:S(2)}) collective-permute-start(s32[1,2]{1,0:T(1,128)} %offsets.5), channel_id=1, source_target_pairs={{0,16},{16,0},{1,17},{17,1},{2,18},{18,2},{3,19},{19,3},{4,20},{20... | collective-permute-start | bytes 32 | tf_op jit(solution)/shard_map/ppermute | solution.py:29
  31.3 1.7 %collective-permute-start.11 = (bf16[8,16,1536]{2,1,0:T(8,128)(2,1)S(1)}, bf16[8,16,1536]{2,1,0:T(8,128)(2,1)S(1)}, u32[]{:S(2)}, u32[]{:S(2)}) collective-permute-start(bf16[8,16,1536]{2,1,0:T(8,128)(2,1)S(1)} %collective-permute-done.7), channel_id=1, source_target_pairs={{0,1},{1,0},{2,3},{3,2},{4,5},{5,4},{6,7},{7,6},{8,9},{9,8},{10,11... | collective-permute-start | bytes 1179656 | tf_op jit(solution)/shard_map/ppermute | solution.py:33
  33.0 17.7 %slice-start = ((s8[4718592]{0:T(1024)(128)(4,1)}), s8[4194304]{0:T(1024)(128)(4,1)S(1)}, s32[]{:S(2)}) async-start(s8[4718592]{0:T(1024)(128)(4,1)} %bitcast.38), calls=%async_computation | async-start | bytes 8388608
  36.4 14.3 %slice-start.1 = ((s8[4718592]{0:T(1024)(128)(4,1)}), s8[524288]{0:T(1024)(128)(4,1)S(1)}, s32[]{:S(2)}) async-start(s8[4718592]{0:T(1024)(128)(4,1)} %bitcast.38), calls=%async_computation.1 | async-start | bytes 1048576
  40.5 10.3 %copy-start = (f32[1,32,1536]{2,1,0:T(8,128)S(1)}, f32[1,32,1536]{2,1,0:T(8,128)}, u32[]{:S(2)}) copy-start(f32[1,32,1536]{2,1,0:T(8,128)} %param.21) | copy-start | bytes 589828
  40.5 2.8 %collective-permute-start.12 = (bf16[1,2,128,384]{3,2,1,0:T(8,128)(2,1)S(1)}, bf16[1,2,128,384]{3,2,1,0:T(8,128)(2,1)S(1)}, u32[]{:S(2)}, u32[]{:S(2)}) collective-permute-start(bf16[1,2,128,384]{3,2,1,0:T(8,128)(2,1)S(1)} %get-tuple-element.102), channel_id=1, source_target_pairs={{0,1},{1,0},{2,3},{3,2},{4,5},{5,4},{6,7},{7,6},{8,9},{9,8},{10,11... | collective-permute-start | bytes 589832 | tf_op jit(solution)/shard_map/ppermute | solution.py:33
  43.4 7.2 %collective-permute-start.13 = (bf16[2,1,128,384]{3,2,1,0:T(8,128)(2,1)S(1)}, bf16[2,1,128,384]{3,2,1,0:T(8,128)(2,1)S(1)}, u32[]{:S(2)}, u32[]{:S(2)}) collective-permute-start(bf16[2,1,128,384]{3,2,1,0:T(8,128)(2,1)S(1)} %slice.71), channel_id=1, source_target_pairs={{0,2},{1,3},{2,0},{3,1},{4,6},{5,7},{6,4},{7,5},{8,10},{9,11},{10,... | collective-permute-start | bytes 589832 | tf_op jit(solution)/shard_map/ppermute | solution.py:33
  48.2 4.4 %collective-permute-start.14 = (bf16[1,2,128,384]{3,2,1,0:T(8,128)(2,1)S(1)}, bf16[1,2,128,384]{3,2,1,0:T(8,128)(2,1)S(1)}, u32[]{:S(2)}, u32[]{:S(2)}) collective-permute-start(bf16[1,2,128,384]{3,2,1,0:T(8,128)(2,1)S(1)} %get-tuple-element.98), channel_id=1, source_target_pairs={{0,1},{1,0},{2,3},{3,2},{4,5},{5,4},{6,7},{7,6},{8,9},{9,8},{10,11... | collective-permute-start | bytes 589832 | tf_op jit(solution)/shard_map/ppermute | solution.py:33
  52.6 6.4 %collective-permute-start.15 = (bf16[2,1,128,384]{3,2,1,0:T(8,128)(2,1)S(1)}, bf16[2,1,128,384]{3,2,1,0:T(8,128)(2,1)S(1)}, u32[]{:S(2)}, u32[]{:S(2)}) collective-permute-start(bf16[2,1,128,384]{3,2,1,0:T(8,128)(2,1)S(1)} %pad_maximum_fusion.1), channel_id=1, source_target_pairs={{0,2},{1,3},{2,0},{3,1},{4,6},{5,7},{6,4},{7,5},{8,10},{9,11},{10,... | collective-permute-start | bytes 589832 | tf_op jit(solution)/shard_map/ppermute | solution.py:33
  53.3 12.1 %collective-permute-start.17 = (bf16[8,16,1536]{2,1,0:T(8,128)(2,1)S(1)}, bf16[8,16,1536]{2,1,0:T(8,128)(2,1)S(1)}, u32[]{:S(2)}, u32[]{:S(2)}) collective-permute-start(bf16[8,16,1536]{2,1,0:T(8,128)(2,1)S(1)} %finish.2), channel_id=1, source_target_pairs={{0,16},{16,0},{1,17},{17,1},{2,18},{18,2},{3,19},{19,3},{4,20},{20... | collective-permute-start | bytes 1179656 | tf_op jit(solution)/shard_map/ppermute | solution.py:29
  60.9 14.9 %collective-permute-start.16 = (bf16[8,16,1536]{2,1,0:T(8,128)(2,1)S(1)}, bf16[8,16,1536]{2,1,0:T(8,128)(2,1)S(1)}, u32[]{:S(2)}, u32[]{:S(2)}) collective-permute-start(bf16[8,16,1536]{2,1,0:T(8,128)(2,1)S(1)} %finish.3), channel_id=1, source_target_pairs={{0,16},{16,0},{1,17},{17,1},{2,18},{18,2},{3,19},{19,3},{4,20},{20... | collective-permute-start | bytes 1179656 | tf_op jit(solution)/shard_map/ppermute | solution.py:29
  65.4 10.4 %collective-permute-start.5 = (bf16[8,16,1536]{2,1,0:T(8,128)(2,1)S(1)}, bf16[8,16,1536]{2,1,0:T(8,128)(2,1)}, u32[]{:S(2)}, u32[]{:S(2)}) collective-permute-start(bf16[8,16,1536]{2,1,0:T(8,128)(2,1)S(1)} %param.3), channel_id=1, source_target_pairs={{0,12},{4,0},{8,4},{12,8},{1,13},{5,1},{9,5},{13,9},{2,14},{6,2},{... | collective-permute-start | bytes 1179656 | tf_op jit(solution)/shard_map/cond/branch_1_fun/ppermute | solution.py:29

commit v5 on v4

--- a/solution.py
+++ b/solution.py
@@ -109,47 +109,42 @@
         out[g, 2] = (value + ones).astype(jnp.bfloat16)
 
 
-def attend_kernel(own_count, own_masks, out_masks, size, gentle, scales, *refs):
+def attend_kernel(own_count, own_masks, out_masks, size, scales, *refs):
     queries, parts, out, held = refs[:own_count], refs[own_count:-2], refs[-2], refs[-1]
-    fast = all_gentle(scales) if gentle is None else None
-    head = pl.program_id(0)
+    fast = all_gentle(scales)
     heads = held.shape[0]
     piece_rows = out.shape[1]
     contract = (((1,), (1,)), ((), ()))
 
     def body(with_max):
-        at = 0
-        for own in queries:
-            block = math.gcd(own.shape[2], 256)
-            for begin in range(0, own.shape[2], block):
-                query = own[0, 0, begin : begin + block, :]
-                scores = [
-                    lax.dot_general(query, part[0, 1], contract, preferred_element_type=jnp.float32) for part in parts
-                ]
-                if with_max:
-                    strength = scales[0, head] * math.log2(math.e)
-                    top = functools.reduce(jnp.maximum, [jnp.max(s, -1, keepdims=True) for s in scores])
-                    scores = [(s - top) * strength for s in scores]
-                mixed = sum(
-                    jnp.dot(jnp.exp2(s).astype(jnp.bfloat16), part[0, 2], preferred_element_type=jnp.float32)
-                    for s, part in zip(scores, parts)
-                )
-                held[head, at : at + block, :] = mixed[:, :size] / mixed[:, size : size + 1]
-                at += block
-
-    if gentle is None:
-        pl.when(fast)(lambda: body(False))
-        pl.when(jnp.logical_not(fast))(lambda: body(True))
-    else:
-        body(not gentle)
-
-    @pl.when(head == heads - 1)
-    def _():
-        for j, mask in enumerate(out_masks):
-            begin = own_masks.index(mask) * piece_rows
-            out[j] = jnp.concatenate(
-                [held[h, begin : begin + piece_rows, :] for h in range(heads)], -1
-            ).astype(jnp.bfloat16)
+        for head in range(heads):
+            at = 0
+            for own in queries:
+                block = math.gcd(own.shape[2], 256)
+                for begin in range(0, own.shape[2], block):
+                    query = own[head, 0, begin : begin + block, :]
+                    scores = [
+                        lax.dot_general(query, part[head, 1], contract, preferred_element_type=jnp.float32)
+                        for part in parts
+                    ]
+                    if with_max:
+                        strength = scales[0, head] * math.log2(math.e)
+                        top = functools.reduce(jnp.maximum, [jnp.max(s, -1, keepdims=True) for s in scores])
+                        scores = [(s - top) * strength for s in scores]
+                    mixed = sum(
+                        jnp.dot(jnp.exp2(s).astype(jnp.bfloat16), part[head, 2], preferred_element_type=jnp.float32)
+                        for s, part in zip(scores, parts)
+                    )
+                    held[head, at : at + block, :] = mixed[:, :size] / mixed[:, size : size + 1]
+                    at += block
+
+    pl.when(fast)(lambda: body(False))
+    pl.when(jnp.logical_not(fast))(lambda: body(True))
+    for j, mask in enumerate(out_masks):
+        begin = own_masks.index(mask) * piece_rows
+        out[j] = jnp.concatenate([held[h, begin : begin + piece_rows, :] for h in range(heads)], -1).astype(
+            jnp.bfloat16
+        )
 
 
 def rows_kernel(level, shift, scale, out):
@@ -295,17 +290,13 @@
     far_heads = projected(gathered([mixed_far]), far_masks, table_rows)
     own_masks = near_masks + far_masks
 
-    def attended(own, local_heads, gentle=None):
-        def block(array, kinds):
-            return pl.BlockSpec((1, kinds, array.shape[2], lane), lambda h: (h, 0, 0, 0))
-
+    def attended(own, local_heads):
         parts = [*local_heads, near_heads, far_heads]
         total = sum(o.shape[2] for o in own)
         return pl.pallas_call(
-            functools.partial(attend_kernel, len(own), own_masks, masks, size, gentle),
-            grid=(heads,),
-            in_specs=[SMEM] + [block(o, 1) for o in own] + [block(p, 3) for p in parts],
-            out_specs=pl.BlockSpec((n, piece_rows, inner), lambda h: (0, 0, 0)),
+            functools.partial(attend_kernel, len(own), own_masks, masks, size),
+            in_specs=[SMEM] + [VMEM] * (len(own) + len(parts)),
+            out_specs=VMEM,
             scratch_shapes=[pltpu.VMEM((heads, total, size), jnp.float32)],
             out_shape=jax.ShapeDtypeStruct((n, piece_rows, inner), jnp.bfloat16),
             compiler_params=params(),
@@ -360,11 +351,14 @@
         lambda block: passed_along(block, "win", 1),
         mixed_sent,
     )
+    block = math.gcd(rows, 4)
+    piece = pl.BlockSpec((block, half, width), lambda i: (i, 0, 0))
     return pl.pallas_call(
         assemble_kernel,
+        grid=(rows // block,),
         out_shape=jax.ShapeDtypeStruct((1, rows, cols, width), jnp.bfloat16),
-        in_specs=[SMEM, VMEM, VMEM, VMEM],
-        out_specs=VMEM,
+        in_specs=[SMEM, piece, piece, piece],
+        out_specs=pl.BlockSpec((1, block, cols, width), lambda i: (0, i, 0, 0)),
         compiler_params=params(),
         cost_estimate=small,
         name="assemble",

time: 78.1 us -> 76.6 us (0.981)
  Pallas kernels: 31.3 us -> 29.7 us
  waiting for transfers between devices: 17.4 us -> 16.6 us
    pallas_call x2, Pallas kernels: 8.03 us -> 6.63 us  [attended(): pl.pallas_call(functools.partial(attend_kernel, len(own), own_masks, mask...]
    ppermute x5, starting transfers between devices: 14.6 us -> 15.7 us  [passed_along(): lax.ppermute(block, axis, [(i, (i + distance) % n) for i in range(n)])]
    ppermute x5, waiting for transfers between devices: 9.85 us -> 8.98 us  [passed_along(): lax.ppermute(block, axis, [(i, (i + distance) % n) for i in range(n)])]
where the time goes in v5:
time: 76.6 us; the launch traced here: 75.8 us
  Pallas kernels  29.7 us (39%)
  starting transfers between devices  23.9 us (31%)
  waiting for transfers between devices  16.6 us (22%)
  between operations  2.22 us (3%)
  local copies, waits for them, and re-layouts  2.04 us (3%)
  other arithmetic  1.28 us (2%)
    ppermute x5, starting transfers between devices, passed_along(): lax.ppermute(block, axis, [(i, (i + distance) % n) for i in range(n)])  15.7 us
    pallas_call x4, Pallas kernels, projected(): pl.pallas_call(functools.partial(project_kernel, held_masks, rows, size),...  14.6 us
    ppermute x5, waiting for transfers between devices, passed_along(): lax.ppermute(block, axis, [(i, (i + distance) % n) for i in range(n)])  8.98 us
    ppermute x10, starting transfers between devices, swapped(): lax.ppermute(block, axis, [(i, i ^ mask) for i in range(lax.axis_size(axi...  8.23 us
    ppermute x10, waiting for transfers between devices, swapped(): lax.ppermute(block, axis, [(i, i ^ mask) for i in range(lax.axis_size(axi...  7.63 us
    pallas_call x2, Pallas kernels, attended(): pl.pallas_call(functools.partial(attend_kernel, len(own), own_masks, mask...  6.63 us
    pallas_call x2, Pallas kernels, finished(): pl.pallas_call(functools.partial(finish_kernel, order), grid=(width // bl...  3.64 us
    pallas_call x1, Pallas kernels, mixed_half(): pl.pallas_call(rows_kernel, out_shape=jax.ShapeDtypeStruct((2, width), jn...  2.27 us
  transfers between devices with their start and end apart: 15, of which 8 were waited for; matrix products, arithmetic and copies ran while one was open for 1% of the time, Pallas kernels for 28%

profile of v5, /device:TPU:0, one launch (start us, length us, event | category | flops | bytes accessed | tf_op | source)
XLA Modules:
  0.0 75.8 jit_solution(15335718538934988000)
XLA Ops:
  0.0 1.2 %slice.63 = s32[1,1]{1,0:T(1,128)} slice(s32[1,2]{1,0:T(1,128)} %offsets.5), slice={[0:1], [1:2]} | slice | bytes 8 | tf_op jit(solution)/shard_map/slice | solution.py:216
  1.9 1.2 %fusion = (bf16[8,16,1536]{2,1,0:T(8,128)(2,1)S(1)}, bf16[8,16,1536]{2,1,0:T(8,128)(2,1)S(1)}, bf16[8,16,1536]{2,1,0:T(8,128)(2,1)S(1)}) fusion(bf16[8,32,1536]{2,1,0:T(8,128)(2,1)} %bitcast.62, pred[]{:T(512)} %bitcast.4), kind=kLoop, calls=%fused_computation.11 | loop fusion | flops 196608 | bytes 1966081 | tf_op jit(solution)/shard_map/slice | solution.py:251
  3.1 3.0 %collective-permute-start.6 = (bf16[8,16,1536]{2,1,0:T(8,128)(2,1)S(1)}, bf16[8,16,1536]{2,1,0:T(8,128)(2,1)S(1)}, u32[]{:S(2)}, u32[]{:S(2)}) collective-permute-start(bf16[8,16,1536]{2,1,0:T(8,128)(2,1)S(1)} %get-tuple-element.95.tile), channel_id=1, source_target_pairs={{0,2},{1,3},{2,0},{3,1},{4,6},{5,7},{6,4},{7,5},{8,10},{9,11},{10,... | collective-permute-start | bytes 1179656 | tf_op jit(solution)/shard_map/ppermute | solution.py:33
  6.1 13.3 %conditional.2 = (bf16[8,16,1536]{2,1,0:T(8,128)(2,1)S(1)}, bf16[4,3,256,128]{3,2,1,0:T(8,128)(2,1)S(1)}, f32[2,1536]{1,0:T(2,128)}) conditional(s32[]{:T(128)} %convert_element_type.9, (bf16[8,16,1536]{2,1,0:T(8,128)(2,1)S(1)}, bf16[8,16,1536]{2,1,0:T(8,128)(2,1)S(1)}, s32[1]{0:T(128)}, f32[32,1536]{1,0:T(8,128)}, f32[32,1536]{1,0:T(8,128)}, ...), branch_computations={%region_0.1_spmd, %region_1.2_spmd} | conditional | flops 3 | bytes 3145895 | solution.py:280
  6.1 3.6 %collective-permute-start = (bf16[8,16,1536]{2,1,0:T(8,128)(2,1)S(1)}, bf16[8,16,1536]{2,1,0:T(8,128)(2,1)S(1)}, u32[]{:S(2)}, u32[]{:S(2)}) collective-permute-start(bf16[8,16,1536]{2,1,0:T(8,128)(2,1)S(1)} %get-tuple-element.43.own), channel_id=1, source_target_pairs={{0,12},{4,0},{8,4},{12,8},{1,13},{5,1},{9,5},{13,9},{2,14},{6,2},{... | collective-permute-start | bytes 1179656 | tf_op jit(solution)/shard_map/cond/branch_0_fun/ppermute | solution.py:29
  9.8 2.3 %rows.2.refs_3_ = f32[2,1536]{1,0:T(2,128)} custom-call(s32[1]{0:T(128)} %get-tuple-element.47.level, f32[32,1536]{1,0:T(8,128)} %get-tuple-element.48.shift, f32[32,1536]{1,0:T(8,128)} %get-tuple-element.49.scale), custom_call_target="tpu_custom_call" | custom-call | flops 1 | bytes 1 | tf_op jit(solution)/shard_map/cond/branch_0_fun/rows/pallas_call | solution.py:258
  12.0 4.0 %project.5 = bf16[4,3,256,128]{3,2,1,0:T(8,128)(2,1)S(1)} custom-call(s32[1,2]{1,0:T(1,128)} %get-tuple-element.42.offsets, f32[1,4]{1,0:T(1,128)} %get-tuple-element.44.scales, bf16[128,1536]{1,0:T(8,128)(2,1)S(1)} %bitcast.60, bf16[128,1536]{1,0:T(8,128)(2,1)S(1)} %bitcast.51, bf16[4,288,1536]{2,1,0:T(8,128)(2,1)} %get-tuple-element.46.refs_2_, ...), custom_call_target="tpu_custom_call" | custom-call | flops 1 | bytes 1 | tf_op jit(solution)/shard_map/cond/branch_0_fun/project/pallas_call | solution.py:228
  16.0 2.7 %collective-permute-done.borrowed = bf16[8,16,1536]{2,1,0:T(8,128)(2,1)S(1)} collective-permute-done((bf16[8,16,1536]{2,1,0:T(8,128)(2,1)S(1)}, bf16[8,16,1536]{2,1,0:T(8,128)(2,1)S(1)}, u32[]{:S(2)}, u32[]{:S(2)}) %collective-permute-start) | collective-permute-done | bytes 393248 | tf_op jit(solution)/shard_map/cond/branch_0_fun/ppermute | solution.py:29
  18.8 0.7 mix.2
  20.6 2.2 %collective-permute-start.10 = (s32[1,2]{1,0:T(1,128)}, s32[1,2]{1,0:T(1,128)S(1)}, u32[]{:S(2)}, u32[]{:S(2)}) collective-permute-start(s32[1,2]{1,0:T(1,128)} %offsets.5), channel_id=1, source_target_pairs={{0,16},{16,0},{1,17},{17,1},{2,18},{18,2},{3,19},{19,3},{4,20},{20... | collective-permute-start | bytes 32 | tf_op jit(solution)/shard_map/ppermute | solution.py:29
  22.8 4.0 %project.8.refs_0_.refs_4_ = bf16[4,3,256,128]{3,2,1,0:T(8,128)(2,1)S(1)} custom-call(s32[1,2]{1,0:T(1,128)S(1)} %copy-done.2, f32[1,4]{1,0:T(1,128)} %scales.9, bf16[128,1536]{1,0:T(8,128)(2,1)S(1)} %bitcast.59, bf16[128,1536]{1,0:T(8,128)(2,1)S(1)} %bitcast.50, bf16[4,288,1536]{2,1,0:T(8,128)(2,1)} %bitcast.56, f32[2,1536]{1,0:T(2,128)} %get-tuple-element.82.refs_3_), custom_call_target="tpu_custom_call" | custom-call | flops 1 | bytes 1 | tf_op jit(solution)/shard_map/project/pallas_call | solution.py:228
  26.9 3.2 %project.7.refs_3_.refs_1_ = bf16[4,3,256,128]{3,2,1,0:T(8,128)(2,1)S(1)} custom-call(s32[1,2]{1,0:T(1,128)S(1)} %copy-done.2, f32[1,4]{1,0:T(1,128)S(1)} %copy-done.5, bf16[128,1536]{1,0:T(8,128)(2,1)S(1)} %bitcast.47, bf16[128,1536]{1,0:T(8,128)(2,1)S(1)} %bitcast.49, bf16[4,288,1536]{2,1,0:T(8,128)(2,1)S(1)} %bitcast.57, f32[2,1536]{1,0:T(2,128)} %get-tuple-element.82.refs_3_), custom_call_target="tpu_custom_call" | custom-call | flops 1 | bytes 1 | tf_op jit(solution)/shard_map/project/pallas_call | solution.py:228
  30.1 1.0 %collective-permute-done.7 = bf16[8,16,1536]{2,1,0:T(8,128)(2,1)S(1)} collective-permute-done((bf16[8,16,1536]{2,1,0:T(8,128)(2,1)S(1)}, bf16[8,16,1536]{2,1,0:T(8,128)(2,1)S(1)}, u32[]{:S(2)}, u32[]{:S(2)}) %collective-permute-start.7) | collective-permute-done | bytes 393248 | tf_op jit(solution)/shard_map/ppermute | solution.py:33
  31.1 1.7 %collective-permute-done.11 = bf16[8,16,1536]{2,1,0:T(8,128)(2,1)S(1)} collective-permute-done((bf16[8,16,1536]{2,1,0:T(8,128)(2,1)S(1)}, bf16[8,16,1536]{2,1,0:T(8,128)(2,1)S(1)}, u32[]{:S(2)}, u32[]{:S(2)}) %collective-permute-start.11) | collective-permute-done | bytes 393248 | tf_op jit(solution)/shard_map/ppermute | solution.py:33
  32.9 3.4 %project.9.refs_1_.refs_5_ = bf16[4,3,256,128]{3,2,1,0:T(8,128)(2,1)S(1)} custom-call(s32[1,2]{1,0:T(1,128)S(1)} %copy-done.2, f32[1,4]{1,0:T(1,128)S(1)} %copy-done.5, bf16[128,1536]{1,0:T(8,128)(2,1)S(1)} %bitcast.48, bf16[128,1536]{1,0:T(8,128)(2,1)S(1)} %bitcast.53, bf16[4,288,1536]{2,1,0:T(8,128)(2,1)S(1)} %bitcast.58, f32[2,1536]{1,0:T(2,128)} %get-tuple-element.82.refs_3_), custom_call_target="tpu_custom_call" | custom-call | flops 1 | bytes 1 | tf_op jit(solution)/shard_map/project/pallas_call | solution.py:228
  36.3 3.4 %attend.2 = bf16[4,128,384]{2,1,0:T(8,128)(2,1)S(1)} custom-call(f32[1,4]{1,0:T(1,128)S(1)} %copy-done.5, bf16[4,3,256,128]{3,2,1,0:T(8,128)(2,1)S(1)} %project.8.refs_0_.refs_4_, bf16[4,3,256,128]{3,2,1,0:T(8,128)(2,1)S(1)} %project.9.refs_1_.refs_5_, bf16[4,3,256,128]{3,2,1,0:T(8,128)(2,1)S(1)} %get-tuple-element.88.refs_2_.refs_0_, ...), custom_call_target="tpu_custom_call" | custom-call | flops 1 | bytes 1 | tf_op jit(solution)/shard_map/attend/pallas_call | solution.py:296
  40.6 0.7 collective-permute-done.12
  41.3 2.0 %collective-permute-start.13 = (bf16[2,1,128,384]{3,2,1,0:T(8,128)(2,1)S(1)}, bf16[2,1,128,384]{3,2,1,0:T(8,128)(2,1)S(1)}, u32[]{:S(2)}, u32[]{:S(2)}) collective-permute-start(bf16[2,1,128,384]{3,2,1,0:T(8,128)(2,1)S(1)} %slice.71), channel_id=1, source_target_pairs={{0,2},{1,3},{2,0},{3,1},{4,6},{5,7},{6,4},{7,5},{8,10},{9,11},{10,... | collective-permute-start | bytes 589832 | tf_op jit(solution)/shard_map/ppermute | solution.py:33
  43.4 3.2 %attend.3 = bf16[4,128,384]{2,1,0:T(8,128)(2,1)S(1)} custom-call(f32[1,4]{1,0:T(1,128)S(1)} %copy-done.5, bf16[4,3,256,128]{3,2,1,0:T(8,128)(2,1)S(1)} %get-tuple-element.88.refs_2_.refs_0_, bf16[4,3,256,128]{3,2,1,0:T(8,128)(2,1)S(1)} %project.7.refs_3_.refs_1_, bf16[4,3,256,128]{3,2,1,0:T(8,128)(2,1)S(1)} %get-tuple-element.88.refs_2_.refs_0_, ...), custom_call_target="tpu_custom_call" | custom-call | flops 1 | bytes 1 | tf_op jit(solution)/shard_map/attend/pallas_call | solution.py:296
  46.8 1.8 %collective-permute-done.13 = bf16[2,1,128,384]{3,2,1,0:T(8,128)(2,1)S(1)} collective-permute-done((bf16[2,1,128,384]{3,2,1,0:T(8,128)(2,1)S(1)}, bf16[2,1,128,384]{3,2,1,0:T(8,128)(2,1)S(1)}, u32[]{:S(2)}, u32[]{:S(2)}) %collective-permute-start.13) | collective-permute-done | bytes 196640 | tf_op jit(solution)/shard_map/ppermute | solution.py:33
  48.7 1.8 %finish.2 = bf16[8,16,1536]{2,1,0:T(8,128)(2,1)S(1)} custom-call(s32[1]{0:T(128)S(6)} %copy.18.level, bf16[8,16,1536]{2,1,0:T(8,128)(2,1)S(1)} %get-tuple-element.79.tile, bf16[128,384]{1,0:T(8,128)(2,1)S(1)} %get-tuple-element.100.refs_0_, bf16[128,384]{1,0:T(8,128)(2,1)S(1)} %get-tuple-element.99.refs_1_, bf16[128,384]{1,0:T(8,128)(2,1)S(1)} %get-tuple-element.106.refs_2_, ...), custom_call_target="tpu_custom_call" | custom-call | flops 1 | bytes 1 | tf_op jit(solution)/shard_map/finish/pallas_call | solution.py:323
  50.5 1.8 %collective-permute-start.15 = (bf16[2,1,128,384]{3,2,1,0:T(8,128)(2,1)S(1)}, bf16[2,1,128,384]{3,2,1,0:T(8,128)(2,1)S(1)}, u32[]{:S(2)}, u32[]{:S(2)}) collective-permute-start(bf16[2,1,128,384]{3,2,1,0:T(8,128)(2,1)S(1)} %pad_maximum_fusion.1), channel_id=1, source_target_pairs={{0,2},{1,3},{2,0},{3,1},{4,6},{5,7},{6,4},{7,5},{8,10},{9,11},{10,... | collective-permute-start | bytes 589832 | tf_op jit(solution)/shard_map/ppermute | solution.py:33
  52.3 2.2 %collective-permute-start.17 = (bf16[8,16,1536]{2,1,0:T(8,128)(2,1)S(1)}, bf16[8,16,1536]{2,1,0:T(8,128)(2,1)S(1)}, u32[]{:S(2)}, u32[]{:S(2)}) collective-permute-start(bf16[8,16,1536]{2,1,0:T(8,128)(2,1)S(1)} %finish.2), channel_id=1, source_target_pairs={{0,16},{16,0},{1,17},{17,1},{2,18},{18,2},{3,19},{19,3},{4,20},{20... | collective-permute-start | bytes 1179656 | tf_op jit(solution)/shard_map/ppermute | solution.py:29
  54.6 2.4 %collective-permute-done.15 = bf16[2,1,128,384]{3,2,1,0:T(8,128)(2,1)S(1)} collective-permute-done((bf16[2,1,128,384]{3,2,1,0:T(8,128)(2,1)S(1)}, bf16[2,1,128,384]{3,2,1,0:T(8,128)(2,1)S(1)}, u32[]{:S(2)}, u32[]{:S(2)}) %collective-permute-start.15) | collective-permute-done | bytes 196640 | tf_op jit(solution)/shard_map/ppermute | solution.py:33
  57.0 1.8 %finish.3 = bf16[8,16,1536]{2,1,0:T(8,128)(2,1)S(1)} custom-call(s32[1]{0:T(128)S(6)} %copy.18.level, bf16[8,16,1536]{2,1,0:T(8,128)(2,1)S(1)} %get-tuple-element.95.tile, bf16[128,384]{1,0:T(8,128)(2,1)S(1)} %slice_bitcast_fusion.4.refs_0_, bf16[128,384]{1,0:T(8,128)(2,1)S(1)} %slice_bitcast_fusion.5.refs_1_, ...), custom_call_target="tpu_custom_call" | custom-call | flops 1 | bytes 1 | tf_op jit(solution)/shard_map/finish/pallas_call | solution.py:323
  58.8 3.4 %collective-permute-start.16 = (bf16[8,16,1536]{2,1,0:T(8,128)(2,1)S(1)}, bf16[8,16,1536]{2,1,0:T(8,128)(2,1)S(1)}, u32[]{:S(2)}, u32[]{:S(2)}) collective-permute-start(bf16[8,16,1536]{2,1,0:T(8,128)(2,1)S(1)} %finish.3), channel_id=1, source_target_pairs={{0,16},{16,0},{1,17},{17,1},{2,18},{18,2},{3,19},{19,3},{4,20},{20... | collective-permute-start | bytes 1179656 | tf_op jit(solution)/shard_map/ppermute | solution.py:29
  62.3 0.6 slice.80
  63.5 1.0 %collective-permute-done.17.mixed = bf16[8,16,1536]{2,1,0:T(8,128)(2,1)S(1)} collective-permute-done((bf16[8,16,1536]{2,1,0:T(8,128)(2,1)S(1)}, bf16[8,16,1536]{2,1,0:T(8,128)(2,1)S(1)}, u32[]{:S(2)}, u32[]{:S(2)}) %collective-permute-start.17) | collective-permute-done | bytes 393248 | tf_op jit(solution)/shard_map/ppermute | solution.py:29
  64.5 9.4 %conditional.3 = (bf16[8,16,1536]{2,1,0:T(8,128)(2,1)}) conditional(s32[]{:T(128)} %bitcast.29, bf16[8,16,1536]{2,1,0:T(8,128)(2,1)S(1)} %collective-permute-done.17.mixed, bf16[8,16,1536]{2,1,0:T(8,128)(2,1)S(1)} %collective-permute-done.17.mixed), branch_computations={%region_2.3_spmd, %region_3.4_spmd} | conditional | bytes 1572912 | solution.py:348
  64.5 4.1 %collective-permute-start.5 = (bf16[8,16,1536]{2,1,0:T(8,128)(2,1)S(1)}, bf16[8,16,1536]{2,1,0:T(8,128)(2,1)}, u32[]{:S(2)}, u32[]{:S(2)}) collective-permute-start(bf16[8,16,1536]{2,1,0:T(8,128)(2,1)S(1)} %param.3), channel_id=1, source_target_pairs={{0,12},{4,0},{8,4},{12,8},{1,13},{5,1},{9,5},{13,9},{2,14},{6,2},{... | collective-permute-start | bytes 1179656 | tf_op jit(solution)/shard_map/cond/branch_1_fun/ppermute | solution.py:29
  68.6 5.3 %collective-permute-done.5 = bf16[8,16,1536]{2,1,0:T(8,128)(2,1)} collective-permute-done((bf16[8,16,1536]{2,1,0:T(8,128)(2,1)S(1)}, bf16[8,16,1536]{2,1,0:T(8,128)(2,1)}, u32[]{:S(2)}, u32[]{:S(2)}) %collective-permute-start.5) | collective-permute-done | bytes 393248 | tf_op jit(solution)/shard_map/cond/branch_1_fun/ppermute | solution.py:29
  73.9 1.9 %assemble.1 = bf16[1,8,32,1536]{3,2,1,0:T(8,128)(2,1)} custom-call(s32[1,2]{1,0:T(1,128)S(1)} %collective-permute-done.10.offsets, bf16[8,16,1536]{2,1,0:T(8,128)(2,1)S(1)} %collective-permute-done.16.local, bf16[8,16,1536]{2,1,0:T(8,128)(2,1)S(1)} %collective-permute-done.17.mixed, bf16[8,16,1536]{2,1,0:T(8,128)(2,1)} %get-tuple-element.113.moved), custom_call_target="tpu_custom_call" | custom-call | flops 1 | bytes 1 | tf_op jit(solution)/shard_map/assemble/pallas_call | solution.py:356
  (39 shorter events, 1.7 us)
Async XLA Ops:
  3.1 16.4 %collective-permute-start.6 = (bf16[8,16,1536]{2,1,0:T(8,128)(2,1)S(1)}, bf16[8,16,1536]{2,1,0:T(8,128)(2,1)S(1)}, u32[]{:S(2)}, u32[]{:S(2)}) collective-permute-start(bf16[8,16,1536]{2,1,0:T(8,128)(2,1)S(1)} %get-tuple-element.95.tile), channel_id=1, source_target_pairs={{0,2},{1,3},{2,0},{3,1},{4,6},{5,7},{6,4},{7,5},{8,10},{9,11},{10,... | collective-permute-start | bytes 1179656 | tf_op jit(solution)/shard_map/ppermute | solution.py:33
  6.1 16.7 %copy-start.2 = (s32[1,2]{1,0:T(1,128)S(1)}, s32[1,2]{1,0:T(1,128)}, u32[]{:S(2)}) copy-start(s32[1,2]{1,0:T(1,128)} %offsets.5) | copy-start | bytes 28
  6.1 12.7 %copy-start.3 = (s32[1,2]{1,0:T(1,128)S(1)}, s32[1,2]{1,0:T(1,128)}, u32[]{:S(2)}) copy-start(s32[1,2]{1,0:T(1,128)} %get-tuple-element.42.offsets) | copy-start | bytes 28 | tf_op jit(solution)/shard_map/cond
  6.1 5.9 %collective-permute-start.1 = (bf16[8,16,1536]{2,1,0:T(8,128)(2,1)S(1)}, bf16[8,16,1536]{2,1,0:T(8,128)(2,1)S(1)}, u32[]{:S(2)}, u32[]{:S(2)}) collective-permute-start(bf16[8,16,1536]{2,1,0:T(8,128)(2,1)S(1)} %get-tuple-element.45), channel_id=1, source_target_pairs={{0,1},{1,0},{2,3},{3,2},{4,5},{5,4},{6,7},{7,6},{8,9},{9,8},{10,11... | collective-permute-start | bytes 1179656 | tf_op jit(solution)/shard_map/cond/branch_0_fun/ppermute | solution.py:33
  6.1 12.6 %collective-permute-start = (bf16[8,16,1536]{2,1,0:T(8,128)(2,1)S(1)}, bf16[8,16,1536]{2,1,0:T(8,128)(2,1)S(1)}, u32[]{:S(2)}, u32[]{:S(2)}) collective-permute-start(bf16[8,16,1536]{2,1,0:T(8,128)(2,1)S(1)} %get-tuple-element.43.own), channel_id=1, source_target_pairs={{0,12},{4,0},{8,4},{12,8},{1,13},{5,1},{9,5},{13,9},{2,14},{6,2},{... | collective-permute-start | bytes 1179656 | tf_op jit(solution)/shard_map/cond/branch_0_fun/ppermute | solution.py:29
  19.4 7.4 %copy-start.1 = (bf16[1,1536,4,288]{1,3,2,0:T(8,128)(2,1)S(1)}, bf16[1,1536,4,288]{1,3,2,0:T(8,128)(2,1)}, u32[]{:S(2)}) copy-start(bf16[1,1536,4,288]{1,3,2,0:T(8,128)(2,1)} %param.16) | copy-start | bytes 10616836
  19.4 7.4 %copy-start.5 = (f32[1,4]{1,0:T(1,128)S(1)}, f32[1,4]{1,0:T(1,128)}, u32[]{:S(2)}) copy-start(f32[1,4]{1,0:T(1,128)} %scales.9) | copy-start | bytes 52
  19.5 3.4 %collective-permute-start.9 = (bf16[8,16,1536]{2,1,0:T(8,128)(2,1)S(1)}, bf16[8,16,1536]{2,1,0:T(8,128)(2,1)S(1)}, u32[]{:S(2)}, u32[]{:S(2)}) collective-permute-start(bf16[8,16,1536]{2,1,0:T(8,128)(2,1)S(1)} %get-tuple-element.79.tile), channel_id=1, source_target_pairs={{0,1},{1,0},{2,3},{3,2},{4,5},{5,4},{6,7},{7,6},{8,9},{9,8},{10,11... | collective-permute-start | bytes 1179656 | tf_op jit(solution)/shard_map/ppermute | solution.py:33
  19.5 7.3 %collective-permute-start.8 = (bf16[8,16,1536]{2,1,0:T(8,128)(2,1)S(1)}, bf16[8,16,1536]{2,1,0:T(8,128)(2,1)S(1)}, u32[]{:S(2)}, u32[]{:S(2)}) collective-permute-start(bf16[8,16,1536]{2,1,0:T(8,128)(2,1)S(1)} %collective-permute-done.6), channel_id=1, source_target_pairs={{0,1},{1,0},{2,3},{3,2},{4,5},{5,4},{6,7},{7,6},{8,9},{9,8},{10,11... | collective-permute-start | bytes 1179656 | tf_op jit(solution)/shard_map/ppermute | solution.py:33
  20.0 11.1 %collective-permute-start.7 = (bf16[8,16,1536]{2,1,0:T(8,128)(2,1)S(1)}, bf16[8,16,1536]{2,1,0:T(8,128)(2,1)S(1)}, u32[]{:S(2)}, u32[]{:S(2)}) collective-permute-start(bf16[8,16,1536]{2,1,0:T(8,128)(2,1)S(1)} %get-tuple-element.79.tile), channel_id=1, source_target_pairs={{0,2},{1,3},{2,0},{3,1},{4,6},{5,7},{6,4},{7,5},{8,10},{9,11},{10,... | collective-permute-start | bytes 1179656 | tf_op jit(solution)/shard_map/ppermute | solution.py:33
  20.6 9.6 %collective-permute-start.10 = (s32[1,2]{1,0:T(1,128)}, s32[1,2]{1,0:T(1,128)S(1)}, u32[]{:S(2)}, u32[]{:S(2)}) collective-permute-start(s32[1,2]{1,0:T(1,128)} %offsets.5), channel_id=1, source_target_pairs={{0,16},{16,0},{1,17},{17,1},{2,18},{18,2},{3,19},{19,3},{4,20},{20... | collective-permute-start | bytes 32 | tf_op jit(solution)/shard_map/ppermute | solution.py:29
  31.1 1.7 %collective-permute-start.11 = (bf16[8,16,1536]{2,1,0:T(8,128)(2,1)S(1)}, bf16[8,16,1536]{2,1,0:T(8,128)(2,1)S(1)}, u32[]{:S(2)}, u32[]{:S(2)}) collective-permute-start(bf16[8,16,1536]{2,1,0:T(8,128)(2,1)S(1)} %collective-permute-done.7), channel_id=1, source_target_pairs={{0,1},{1,0},{2,3},{3,2},{4,5},{5,4},{6,7},{7,6},{8,9},{9,8},{10,11... | collective-permute-start | bytes 1179656 | tf_op jit(solution)/shard_map/ppermute | solution.py:33
  32.9 15.8 %slice-start = ((s8[4718592]{0:T(1024)(128)(4,1)}), s8[4194304]{0:T(1024)(128)(4,1)S(1)}, s32[]{:S(2)}) async-start(s8[4718592]{0:T(1024)(128)(4,1)} %bitcast.38), calls=%async_computation | async-start | bytes 8388608
  36.2 12.4 %slice-start.1 = ((s8[4718592]{0:T(1024)(128)(4,1)}), s8[524288]{0:T(1024)(128)(4,1)S(1)}, s32[]{:S(2)}) async-start(s8[4718592]{0:T(1024)(128)(4,1)} %bitcast.38), calls=%async_computation.1 | async-start | bytes 1048576
  39.7 9.0 %copy-start = (f32[1,32,1536]{2,1,0:T(8,128)S(1)}, f32[1,32,1536]{2,1,0:T(8,128)}, u32[]{:S(2)}) copy-start(f32[1,32,1536]{2,1,0:T(8,128)} %param.21) | copy-start | bytes 589828
  39.7 1.5 %collective-permute-start.12 = (bf16[1,2,128,384]{3,2,1,0:T(8,128)(2,1)S(1)}, bf16[1,2,128,384]{3,2,1,0:T(8,128)(2,1)S(1)}, u32[]{:S(2)}, u32[]{:S(2)}) collective-permute-start(bf16[1,2,128,384]{3,2,1,0:T(8,128)(2,1)S(1)} %get-tuple-element.102), channel_id=1, source_target_pairs={{0,1},{1,0},{2,3},{3,2},{4,5},{5,4},{6,7},{7,6},{8,9},{9,8},{10,11... | collective-permute-start | bytes 589832 | tf_op jit(solution)/shard_map/ppermute | solution.py:33
  41.3 7.3 %collective-permute-start.13 = (bf16[2,1,128,384]{3,2,1,0:T(8,128)(2,1)S(1)}, bf16[2,1,128,384]{3,2,1,0:T(8,128)(2,1)S(1)}, u32[]{:S(2)}, u32[]{:S(2)}) collective-permute-start(bf16[2,1,128,384]{3,2,1,0:T(8,128)(2,1)S(1)} %slice.71), channel_id=1, source_target_pairs={{0,2},{1,3},{2,0},{3,1},{4,6},{5,7},{6,4},{7,5},{8,10},{9,11},{10,... | collective-permute-start | bytes 589832 | tf_op jit(solution)/shard_map/ppermute | solution.py:33
  46.7 3.8 %collective-permute-start.14 = (bf16[1,2,128,384]{3,2,1,0:T(8,128)(2,1)S(1)}, bf16[1,2,128,384]{3,2,1,0:T(8,128)(2,1)S(1)}, u32[]{:S(2)}, u32[]{:S(2)}) collective-permute-start(bf16[1,2,128,384]{3,2,1,0:T(8,128)(2,1)S(1)} %get-tuple-element.98), channel_id=1, source_target_pairs={{0,1},{1,0},{2,3},{3,2},{4,5},{5,4},{6,7},{7,6},{8,9},{9,8},{10,11... | collective-permute-start | bytes 589832 | tf_op jit(solution)/shard_map/ppermute | solution.py:33
  50.5 6.5 %collective-permute-start.15 = (bf16[2,1,128,384]{3,2,1,0:T(8,128)(2,1)S(1)}, bf16[2,1,128,384]{3,2,1,0:T(8,128)(2,1)S(1)}, u32[]{:S(2)}, u32[]{:S(2)}) collective-permute-start(bf16[2,1,128,384]{3,2,1,0:T(8,128)(2,1)S(1)} %pad_maximum_fusion.1), channel_id=1, source_target_pairs={{0,2},{1,3},{2,0},{3,1},{4,6},{5,7},{6,4},{7,5},{8,10},{9,11},{10,... | collective-permute-start | bytes 589832 | tf_op jit(solution)/shard_map/ppermute | solution.py:33
  52.3 12.2 %collective-permute-start.17 = (bf16[8,16,1536]{2,1,0:T(8,128)(2,1)S(1)}, bf16[8,16,1536]{2,1,0:T(8,128)(2,1)S(1)}, u32[]{:S(2)}, u32[]{:S(2)}) collective-permute-start(bf16[8,16,1536]{2,1,0:T(8,128)(2,1)S(1)} %finish.2), channel_id=1, source_target_pairs={{0,16},{16,0},{1,17},{17,1},{2,18},{18,2},{3,19},{19,3},{4,20},{20... | collective-permute-start | bytes 1179656 | tf_op jit(solution)/shard_map/ppermute | solution.py:29
  58.8 15.1 %collective-permute-start.16 = (bf16[8,16,1536]{2,1,0:T(8,128)(2,1)S(1)}, bf16[8,16,1536]{2,1,0:T(8,128)(2,1)S(1)}, u32[]{:S(2)}, u32[]{:S(2)}) collective-permute-start(bf16[8,16,1536]{2,1,0:T(8,128)(2,1)S(1)} %finish.3), channel_id=1, source_target_pairs={{0,16},{16,0},{1,17},{17,1},{2,18},{18,2},{3,19},{19,3},{4,20},{20... | collective-permute-start | bytes 1179656 | tf_op jit(solution)/shard_map/ppermute | solution.py:29
  64.5 9.4 %collective-permute-start.5 = (bf16[8,16,1536]{2,1,0:T(8,128)(2,1)S(1)}, bf16[8,16,1536]{2,1,0:T(8,128)(2,1)}, u32[]{:S(2)}, u32[]{:S(2)}) collective-permute-start(bf16[8,16,1536]{2,1,0:T(8,128)(2,1)S(1)} %param.3), channel_id=1, source_target_pairs={{0,12},{4,0},{8,4},{12,8},{1,13},{5,1},{9,5},{13,9},{2,14},{6,2},{... | collective-permute-start | bytes 1179656 | tf_op jit(solution)/shard_map/cond/branch_1_fun/ppermute | solution.py:29

commit v6 on v5

--- a/solution.py
+++ b/solution.py
@@ -340,7 +340,7 @@
     mixed_out = returned(mixed_held)
     local_attended = attended(local_query, local_query)
     local_kept, local_received = hop(local_attended[None], bits[0])
-    mixed_done, local_received = lax.optimization_barrier((finished(mixed_out, mixed), local_received))
+    mixed_done = finished(mixed_out, mixed)
     mixed_sent = passed_along(mixed_done, "segment", 1)
     local_done = finished(returned(jnp.concatenate([local_kept, local_received], 0)), local)
     local_sent = passed_along(local_done, "segment", 1)

time: 76.6 us -> 75.4 us (0.984)
  starting transfers between devices: 23.9 us -> 20.6 us
  waiting for transfers between devices: 16.6 us -> 18.9 us
    ppermute x5, starting transfers between devices: 15.7 us -> 12.3 us  [passed_along(): lax.ppermute(block, axis, [(i, (i + distance) % n) for i in range(n)])]
    ppermute x10, waiting for transfers between devices: 7.63 us -> 9.54 us  [swapped(): lax.ppermute(block, axis, [(i, i ^ mask) for i in range(lax.axis_size(axi...]
  transfers between devices with their start and end apart: 15 -> 15, of which waited for: 8 -> 7; matrix products, arithmetic and copies ran while one was open for 1% -> 1% of each run, Pallas kernels for 28% -> 28%
where the time goes in v6:
time: 75.4 us; the launch traced here: 74.7 us
  Pallas kernels  29.7 us (39%)
  starting transfers between devices  20.6 us (27%)
  waiting for transfers between devices  18.9 us (25%)
  between operations  2.22 us (3%)
  local copies, waits for them, and re-layouts  2.04 us (3%)
  other arithmetic  1.27 us (2%)
    pallas_call x4, Pallas kernels, projected(): pl.pallas_call(functools.partial(project_kernel, held_masks, rows, size),...  14.6 us
    ppermute x5, starting transfers between devices, passed_along(): lax.ppermute(block, axis, [(i, (i + distance) % n) for i in range(n)])  12.3 us
    ppermute x10, waiting for transfers between devices, swapped(): lax.ppermute(block, axis, [(i, i ^ mask) for i in range(lax.axis_size(axi...  9.54 us
    ppermute x5, waiting for transfers between devices, passed_along(): lax.ppermute(block, axis, [(i, (i + distance) % n) for i in range(n)])  9.32 us
    ppermute x10, starting transfers between devices, swapped(): lax.ppermute(block, axis, [(i, i ^ mask) for i in range(lax.axis_size(axi...  8.24 us
    pallas_call x2, Pallas kernels, attended(): pl.pallas_call(functools.partial(attend_kernel, len(own), own_masks, mask...  6.63 us
    pallas_call x2, Pallas kernels, finished(): pl.pallas_call(functools.partial(finish_kernel, order), grid=(width // bl...  3.63 us
    pallas_call x1, Pallas kernels, mixed_half(): pl.pallas_call(rows_kernel, out_shape=jax.ShapeDtypeStruct((2, width), jn...  2.27 us
  transfers between devices with their start and end apart: 15, of which 7 were waited for; matrix products, arithmetic and copies ran while one was open for 1% of the time, Pallas kernels for 28%

profile of v6, /device:TPU:0, one launch (start us, length us, event | category | flops | bytes accessed | tf_op | source)
XLA Modules:
  0.0 74.7 jit_solution(11254065239918520834)
XLA Ops:
  0.0 1.2 %slice.63 = s32[1,1]{1,0:T(1,128)} slice(s32[1,2]{1,0:T(1,128)} %offsets.5), slice={[0:1], [1:2]} | slice | bytes 8 | tf_op jit(solution)/shard_map/slice | solution.py:216
  1.9 1.2 %fusion = (bf16[8,16,1536]{2,1,0:T(8,128)(2,1)S(1)}, bf16[8,16,1536]{2,1,0:T(8,128)(2,1)S(1)}, bf16[8,16,1536]{2,1,0:T(8,128)(2,1)S(1)}) fusion(bf16[8,32,1536]{2,1,0:T(8,128)(2,1)} %bitcast.62, pred[]{:T(512)} %bitcast.4), kind=kLoop, calls=%fused_computation.11 | loop fusion | flops 196608 | bytes 1966081 | tf_op jit(solution)/shard_map/slice | solution.py:251
  3.1 3.0 %collective-permute-start.6 = (bf16[8,16,1536]{2,1,0:T(8,128)(2,1)S(1)}, bf16[8,16,1536]{2,1,0:T(8,128)(2,1)S(1)}, u32[]{:S(2)}, u32[]{:S(2)}) collective-permute-start(bf16[8,16,1536]{2,1,0:T(8,128)(2,1)S(1)} %get-tuple-element.91.tile), channel_id=1, source_target_pairs={{0,2},{1,3},{2,0},{3,1},{4,6},{5,7},{6,4},{7,5},{8,10},{9,11},{10,... | collective-permute-start | bytes 1179656 | tf_op jit(solution)/shard_map/ppermute | solution.py:33
  6.1 13.3 %conditional.2 = (bf16[8,16,1536]{2,1,0:T(8,128)(2,1)S(1)}, bf16[4,3,256,128]{3,2,1,0:T(8,128)(2,1)S(1)}, f32[2,1536]{1,0:T(2,128)}) conditional(s32[]{:T(128)} %convert_element_type.9, (bf16[8,16,1536]{2,1,0:T(8,128)(2,1)S(1)}, bf16[8,16,1536]{2,1,0:T(8,128)(2,1)S(1)}, s32[1]{0:T(128)}, f32[32,1536]{1,0:T(8,128)}, f32[32,1536]{1,0:T(8,128)}, ...), branch_computations={%region_0.1_spmd, %region_1.2_spmd} | conditional | flops 3 | bytes 3145895 | solution.py:280
  6.1 3.6 %collective-permute-start = (bf16[8,16,1536]{2,1,0:T(8,128)(2,1)S(1)}, bf16[8,16,1536]{2,1,0:T(8,128)(2,1)S(1)}, u32[]{:S(2)}, u32[]{:S(2)}) collective-permute-start(bf16[8,16,1536]{2,1,0:T(8,128)(2,1)S(1)} %get-tuple-element.43.own), channel_id=1, source_target_pairs={{0,12},{4,0},{8,4},{12,8},{1,13},{5,1},{9,5},{13,9},{2,14},{6,2},{... | collective-permute-start | bytes 1179656 | tf_op jit(solution)/shard_map/cond/branch_0_fun/ppermute | solution.py:29
  9.8 2.3 %rows.2.refs_3_ = f32[2,1536]{1,0:T(2,128)} custom-call(s32[1]{0:T(128)} %get-tuple-element.47.level, f32[32,1536]{1,0:T(8,128)} %get-tuple-element.48.shift, f32[32,1536]{1,0:T(8,128)} %get-tuple-element.49.scale), custom_call_target="tpu_custom_call" | custom-call | flops 1 | bytes 1 | tf_op jit(solution)/shard_map/cond/branch_0_fun/rows/pallas_call | solution.py:258
  12.0 4.0 %project.5 = bf16[4,3,256,128]{3,2,1,0:T(8,128)(2,1)S(1)} custom-call(s32[1,2]{1,0:T(1,128)} %get-tuple-element.42.offsets, f32[1,4]{1,0:T(1,128)} %get-tuple-element.44.scales, bf16[128,1536]{1,0:T(8,128)(2,1)S(1)} %bitcast.60, bf16[128,1536]{1,0:T(8,128)(2,1)S(1)} %bitcast.51, bf16[4,288,1536]{2,1,0:T(8,128)(2,1)} %get-tuple-element.46.refs_2_, ...), custom_call_target="tpu_custom_call" | custom-call | flops 1 | bytes 1 | tf_op jit(solution)/shard_map/cond/branch_0_fun/project/pallas_call | solution.py:228
  16.0 2.7 %collective-permute-done.borrowed = bf16[8,16,1536]{2,1,0:T(8,128)(2,1)S(1)} collective-permute-done((bf16[8,16,1536]{2,1,0:T(8,128)(2,1)S(1)}, bf16[8,16,1536]{2,1,0:T(8,128)(2,1)S(1)}, u32[]{:S(2)}, u32[]{:S(2)}) %collective-permute-start) | collective-permute-done | bytes 393248 | tf_op jit(solution)/shard_map/cond/branch_0_fun/ppermute | solution.py:29
  18.8 0.7 mix.2
  19.5 0.5 collective-permute-start.8
  20.0 0.5 collective-permute-start.7
  20.6 2.2 %collective-permute-start.10 = (s32[1,2]{1,0:T(1,128)}, s32[1,2]{1,0:T(1,128)S(1)}, u32[]{:S(2)}, u32[]{:S(2)}) collective-permute-start(s32[1,2]{1,0:T(1,128)} %offsets.5), channel_id=1, source_target_pairs={{0,16},{16,0},{1,17},{17,1},{2,18},{18,2},{3,19},{19,3},{4,20},{20... | collective-permute-start | bytes 32 | tf_op jit(solution)/shard_map/ppermute | solution.py:29
  22.8 4.0 %project.8.refs_0_.refs_4_ = bf16[4,3,256,128]{3,2,1,0:T(8,128)(2,1)S(1)} custom-call(s32[1,2]{1,0:T(1,128)S(1)} %copy-done.2, f32[1,4]{1,0:T(1,128)} %scales.9, bf16[128,1536]{1,0:T(8,128)(2,1)S(1)} %bitcast.59, bf16[128,1536]{1,0:T(8,128)(2,1)S(1)} %bitcast.50, bf16[4,288,1536]{2,1,0:T(8,128)(2,1)} %bitcast.56, f32[2,1536]{1,0:T(2,128)} %get-tuple-element.80.refs_3_), custom_call_target="tpu_custom_call" | custom-call | flops 1 | bytes 1 | tf_op jit(solution)/shard_map/project/pallas_call | solution.py:228
  26.9 3.2 %project.7.refs_3_.refs_1_ = bf16[4,3,256,128]{3,2,1,0:T(8,128)(2,1)S(1)} custom-call(s32[1,2]{1,0:T(1,128)S(1)} %copy-done.2, f32[1,4]{1,0:T(1,128)S(1)} %copy-done.5, bf16[128,1536]{1,0:T(8,128)(2,1)S(1)} %bitcast.47, bf16[128,1536]{1,0:T(8,128)(2,1)S(1)} %bitcast.49, bf16[4,288,1536]{2,1,0:T(8,128)(2,1)S(1)} %bitcast.57, f32[2,1536]{1,0:T(2,128)} %get-tuple-element.80.refs_3_), custom_call_target="tpu_custom_call" | custom-call | flops 1 | bytes 1 | tf_op jit(solution)/shard_map/project/pallas_call | solution.py:228
  30.1 1.0 %collective-permute-done.7 = bf16[8,16,1536]{2,1,0:T(8,128)(2,1)S(1)} collective-permute-done((bf16[8,16,1536]{2,1,0:T(8,128)(2,1)S(1)}, bf16[8,16,1536]{2,1,0:T(8,128)(2,1)S(1)}, u32[]{:S(2)}, u32[]{:S(2)}) %collective-permute-start.7) | collective-permute-done | bytes 393248 | tf_op jit(solution)/shard_map/ppermute | solution.py:33
  31.1 1.7 %collective-permute-done.11 = bf16[8,16,1536]{2,1,0:T(8,128)(2,1)S(1)} collective-permute-done((bf16[8,16,1536]{2,1,0:T(8,128)(2,1)S(1)}, bf16[8,16,1536]{2,1,0:T(8,128)(2,1)S(1)}, u32[]{:S(2)}, u32[]{:S(2)}) %collective-permute-start.11) | collective-permute-done | bytes 393248 | tf_op jit(solution)/shard_map/ppermute | solution.py:33
  32.9 3.4 %project.9.refs_1_.refs_5_ = bf16[4,3,256,128]{3,2,1,0:T(8,128)(2,1)S(1)} custom-call(s32[1,2]{1,0:T(1,128)S(1)} %copy-done.2, f32[1,4]{1,0:T(1,128)S(1)} %copy-done.5, bf16[128,1536]{1,0:T(8,128)(2,1)S(1)} %bitcast.48, bf16[128,1536]{1,0:T(8,128)(2,1)S(1)} %bitcast.53, bf16[4,288,1536]{2,1,0:T(8,128)(2,1)S(1)} %bitcast.58, f32[2,1536]{1,0:T(2,128)} %get-tuple-element.80.refs_3_), custom_call_target="tpu_custom_call" | custom-call | flops 1 | bytes 1 | tf_op jit(solution)/shard_map/project/pallas_call | solution.py:228
  36.3 3.4 %attend.2 = bf16[4,128,384]{2,1,0:T(8,128)(2,1)S(1)} custom-call(f32[1,4]{1,0:T(1,128)S(1)} %copy-done.5, bf16[4,3,256,128]{3,2,1,0:T(8,128)(2,1)S(1)} %project.8.refs_0_.refs_4_, bf16[4,3,256,128]{3,2,1,0:T(8,128)(2,1)S(1)} %project.9.refs_1_.refs_5_, bf16[4,3,256,128]{3,2,1,0:T(8,128)(2,1)S(1)} %get-tuple-element.86.refs_2_.refs_0_, ...), custom_call_target="tpu_custom_call" | custom-call | flops 1 | bytes 1 | tf_op jit(solution)/shard_map/attend/pallas_call | solution.py:296
  40.6 0.7 collective-permute-done.12
  41.3 2.0 %collective-permute-start.16 = (bf16[2,1,128,384]{3,2,1,0:T(8,128)(2,1)S(1)}, bf16[2,1,128,384]{3,2,1,0:T(8,128)(2,1)S(1)}, u32[]{:S(2)}, u32[]{:S(2)}) collective-permute-start(bf16[2,1,128,384]{3,2,1,0:T(8,128)(2,1)S(1)} %slice.77), channel_id=1, source_target_pairs={{0,2},{1,3},{2,0},{3,1},{4,6},{5,7},{6,4},{7,5},{8,10},{9,11},{10,... | collective-permute-start | bytes 589832 | tf_op jit(solution)/shard_map/ppermute | solution.py:33
  43.4 3.2 %attend.3 = bf16[4,128,384]{2,1,0:T(8,128)(2,1)S(1)} custom-call(f32[1,4]{1,0:T(1,128)S(1)} %copy-done.5, bf16[4,3,256,128]{3,2,1,0:T(8,128)(2,1)S(1)} %get-tuple-element.86.refs_2_.refs_0_, bf16[4,3,256,128]{3,2,1,0:T(8,128)(2,1)S(1)} %project.7.refs_3_.refs_1_, bf16[4,3,256,128]{3,2,1,0:T(8,128)(2,1)S(1)} %get-tuple-element.86.refs_2_.refs_0_, ...), custom_call_target="tpu_custom_call" | custom-call | flops 1 | bytes 1 | tf_op jit(solution)/shard_map/attend/pallas_call | solution.py:296
  46.8 1.8 %collective-permute-done.16 = bf16[2,1,128,384]{3,2,1,0:T(8,128)(2,1)S(1)} collective-permute-done((bf16[2,1,128,384]{3,2,1,0:T(8,128)(2,1)S(1)}, bf16[2,1,128,384]{3,2,1,0:T(8,128)(2,1)S(1)}, u32[]{:S(2)}, u32[]{:S(2)}) %collective-permute-start.16) | collective-permute-done | bytes 196640 | tf_op jit(solution)/shard_map/ppermute | solution.py:33
  48.7 1.8 %finish.3 = bf16[8,16,1536]{2,1,0:T(8,128)(2,1)S(1)} custom-call(s32[1]{0:T(128)S(6)} %copy.18.level, bf16[8,16,1536]{2,1,0:T(8,128)(2,1)S(1)} %get-tuple-element.77.tile, bf16[128,384]{1,0:T(8,128)(2,1)S(1)} %get-tuple-element.94.refs_0_, bf16[128,384]{1,0:T(8,128)(2,1)S(1)} %get-tuple-element.93.refs_1_, bf16[128,384]{1,0:T(8,128)(2,1)S(1)} %get-tuple-element.100.refs_2_, ...), custom_call_target="tpu_custom_call" | custom-call | flops 1 | bytes 1 | tf_op jit(solution)/shard_map/finish/pallas_call | solution.py:323
  50.5 2.3 %collective-permute-start.17 = (bf16[8,16,1536]{2,1,0:T(8,128)(2,1)S(1)}, bf16[8,16,1536]{2,1,0:T(8,128)(2,1)S(1)}, u32[]{:S(2)}, u32[]{:S(2)}) collective-permute-start(bf16[8,16,1536]{2,1,0:T(8,128)(2,1)S(1)} %finish.3), channel_id=1, source_target_pairs={{0,16},{16,0},{1,17},{17,1},{2,18},{18,2},{3,19},{19,3},{4,20},{20... | collective-permute-start | bytes 1179656 | tf_op jit(solution)/shard_map/ppermute | solution.py:29
  52.8 1.8 %collective-permute-start.14 = (bf16[2,1,128,384]{3,2,1,0:T(8,128)(2,1)S(1)}, bf16[2,1,128,384]{3,2,1,0:T(8,128)(2,1)S(1)}, u32[]{:S(2)}, u32[]{:S(2)}) collective-permute-start(bf16[2,1,128,384]{3,2,1,0:T(8,128)(2,1)S(1)} %pad_maximum_fusion.1), channel_id=1, source_target_pairs={{0,2},{1,3},{2,0},{3,1},{4,6},{5,7},{6,4},{7,5},{8,10},{9,11},{10,... | collective-permute-start | bytes 589832 | tf_op jit(solution)/shard_map/ppermute | solution.py:33
  54.6 4.3 %collective-permute-done.14 = bf16[2,1,128,384]{3,2,1,0:T(8,128)(2,1)S(1)} collective-permute-done((bf16[2,1,128,384]{3,2,1,0:T(8,128)(2,1)S(1)}, bf16[2,1,128,384]{3,2,1,0:T(8,128)(2,1)S(1)}, u32[]{:S(2)}, u32[]{:S(2)}) %collective-permute-start.14) | collective-permute-done | bytes 196640 | tf_op jit(solution)/shard_map/ppermute | solution.py:33
  59.0 1.8 %finish.2 = bf16[8,16,1536]{2,1,0:T(8,128)(2,1)S(1)} custom-call(s32[1]{0:T(128)S(6)} %copy.18.level, bf16[8,16,1536]{2,1,0:T(8,128)(2,1)S(1)} %get-tuple-element.91.tile, bf16[128,384]{1,0:T(8,128)(2,1)S(1)} %slice_bitcast_fusion.5.refs_0_, bf16[128,384]{1,0:T(8,128)(2,1)S(1)} %slice_bitcast_fusion.4.refs_1_, ...), custom_call_target="tpu_custom_call" | custom-call | flops 1 | bytes 1 | tf_op jit(solution)/shard_map/finish/pallas_call | solution.py:323
  61.2 0.6 slice.80
  62.4 10.4 %conditional.3 = (bf16[8,16,1536]{2,1,0:T(8,128)(2,1)}) conditional(s32[]{:T(128)} %bitcast.29, bf16[8,16,1536]{2,1,0:T(8,128)(2,1)S(1)} %collective-permute-done.17.mixed, bf16[8,16,1536]{2,1,0:T(8,128)(2,1)S(1)} %collective-permute-done.17.mixed), branch_computations={%region_2.3_spmd, %region_3.4_spmd} | conditional | bytes 1572912 | solution.py:348
  62.4 3.8 %collective-permute-start.5 = (bf16[8,16,1536]{2,1,0:T(8,128)(2,1)S(1)}, bf16[8,16,1536]{2,1,0:T(8,128)(2,1)}, u32[]{:S(2)}, u32[]{:S(2)}) collective-permute-start(bf16[8,16,1536]{2,1,0:T(8,128)(2,1)S(1)} %param.3), channel_id=1, source_target_pairs={{0,12},{4,0},{8,4},{12,8},{1,13},{5,1},{9,5},{13,9},{2,14},{6,2},{... | collective-permute-start | bytes 1179656 | tf_op jit(solution)/shard_map/cond/branch_1_fun/ppermute | solution.py:29
  66.2 6.6 %collective-permute-done.5 = bf16[8,16,1536]{2,1,0:T(8,128)(2,1)} collective-permute-done((bf16[8,16,1536]{2,1,0:T(8,128)(2,1)S(1)}, bf16[8,16,1536]{2,1,0:T(8,128)(2,1)}, u32[]{:S(2)}, u32[]{:S(2)}) %collective-permute-start.5) | collective-permute-done | bytes 393248 | tf_op jit(solution)/shard_map/cond/branch_1_fun/ppermute | solution.py:29
  72.8 1.9 %assemble.1 = bf16[1,8,32,1536]{3,2,1,0:T(8,128)(2,1)} custom-call(s32[1,2]{1,0:T(1,128)S(1)} %collective-permute-done.10.offsets, bf16[8,16,1536]{2,1,0:T(8,128)(2,1)S(1)} %collective-permute-done.15.local, bf16[8,16,1536]{2,1,0:T(8,128)(2,1)S(1)} %collective-permute-done.17.mixed, bf16[8,16,1536]{2,1,0:T(8,128)(2,1)} %get-tuple-element.109.moved), custom_call_target="tpu_custom_call" | custom-call | flops 1 | bytes 1 | tf_op jit(solution)/shard_map/assemble/pallas_call | solution.py:356
  (39 shorter events, 1.0 us)
Async XLA Ops:
  3.1 16.4 %collective-permute-start.6 = (bf16[8,16,1536]{2,1,0:T(8,128)(2,1)S(1)}, bf16[8,16,1536]{2,1,0:T(8,128)(2,1)S(1)}, u32[]{:S(2)}, u32[]{:S(2)}) collective-permute-start(bf16[8,16,1536]{2,1,0:T(8,128)(2,1)S(1)} %get-tuple-element.91.tile), channel_id=1, source_target_pairs={{0,2},{1,3},{2,0},{3,1},{4,6},{5,7},{6,4},{7,5},{8,10},{9,11},{10,... | collective-permute-start | bytes 1179656 | tf_op jit(solution)/shard_map/ppermute | solution.py:33
  6.1 16.7 %copy-start.2 = (s32[1,2]{1,0:T(1,128)S(1)}, s32[1,2]{1,0:T(1,128)}, u32[]{:S(2)}) copy-start(s32[1,2]{1,0:T(1,128)} %offsets.5) | copy-start | bytes 28
  6.1 12.7 %copy-start.3 = (s32[1,2]{1,0:T(1,128)S(1)}, s32[1,2]{1,0:T(1,128)}, u32[]{:S(2)}) copy-start(s32[1,2]{1,0:T(1,128)} %get-tuple-element.42.offsets) | copy-start | bytes 28 | tf_op jit(solution)/shard_map/cond
  6.1 5.9 %collective-permute-start.1 = (bf16[8,16,1536]{2,1,0:T(8,128)(2,1)S(1)}, bf16[8,16,1536]{2,1,0:T(8,128)(2,1)S(1)}, u32[]{:S(2)}, u32[]{:S(2)}) collective-permute-start(bf16[8,16,1536]{2,1,0:T(8,128)(2,1)S(1)} %get-tuple-element.45), channel_id=1, source_target_pairs={{0,1},{1,0},{2,3},{3,2},{4,5},{5,4},{6,7},{7,6},{8,9},{9,8},{10,11... | collective-permute-start | bytes 1179656 | tf_op jit(solution)/shard_map/cond/branch_0_fun/ppermute | solution.py:33
  6.1 12.6 %collective-permute-start = (bf16[8,16,1536]{2,1,0:T(8,128)(2,1)S(1)}, bf16[8,16,1536]{2,1,0:T(8,128)(2,1)S(1)}, u32[]{:S(2)}, u32[]{:S(2)}) collective-permute-start(bf16[8,16,1536]{2,1,0:T(8,128)(2,1)S(1)} %get-tuple-element.43.own), channel_id=1, source_target_pairs={{0,12},{4,0},{8,4},{12,8},{1,13},{5,1},{9,5},{13,9},{2,14},{6,2},{... | collective-permute-start | bytes 1179656 | tf_op jit(solution)/shard_map/cond/branch_0_fun/ppermute | solution.py:29
  19.4 7.4 %copy-start.1 = (bf16[1,1536,4,288]{1,3,2,0:T(8,128)(2,1)S(1)}, bf16[1,1536,4,288]{1,3,2,0:T(8,128)(2,1)}, u32[]{:S(2)}) copy-start(bf16[1,1536,4,288]{1,3,2,0:T(8,128)(2,1)} %param.16) | copy-start | bytes 10616836
  19.4 7.4 %copy-start.5 = (f32[1,4]{1,0:T(1,128)S(1)}, f32[1,4]{1,0:T(1,128)}, u32[]{:S(2)}) copy-start(f32[1,4]{1,0:T(1,128)} %scales.9) | copy-start | bytes 52
  19.5 3.4 %collective-permute-start.9 = (bf16[8,16,1536]{2,1,0:T(8,128)(2,1)S(1)}, bf16[8,16,1536]{2,1,0:T(8,128)(2,1)S(1)}, u32[]{:S(2)}, u32[]{:S(2)}) collective-permute-start(bf16[8,16,1536]{2,1,0:T(8,128)(2,1)S(1)} %get-tuple-element.77.tile), channel_id=1, source_target_pairs={{0,1},{1,0},{2,3},{3,2},{4,5},{5,4},{6,7},{7,6},{8,9},{9,8},{10,11... | collective-permute-start | bytes 1179656 | tf_op jit(solution)/shard_map/ppermute | solution.py:33
  19.5 7.3 %collective-permute-start.8 = (bf16[8,16,1536]{2,1,0:T(8,128)(2,1)S(1)}, bf16[8,16,1536]{2,1,0:T(8,128)(2,1)S(1)}, u32[]{:S(2)}, u32[]{:S(2)}) collective-permute-start(bf16[8,16,1536]{2,1,0:T(8,128)(2,1)S(1)} %collective-permute-done.6), channel_id=1, source_target_pairs={{0,1},{1,0},{2,3},{3,2},{4,5},{5,4},{6,7},{7,6},{8,9},{9,8},{10,11... | collective-permute-start | bytes 1179656 | tf_op jit(solution)/shard_map/ppermute | solution.py:33
  20.0 11.1 %collective-permute-start.7 = (bf16[8,16,1536]{2,1,0:T(8,128)(2,1)S(1)}, bf16[8,16,1536]{2,1,0:T(8,128)(2,1)S(1)}, u32[]{:S(2)}, u32[]{:S(2)}) collective-permute-start(bf16[8,16,1536]{2,1,0:T(8,128)(2,1)S(1)} %get-tuple-element.77.tile), channel_id=1, source_target_pairs={{0,2},{1,3},{2,0},{3,1},{4,6},{5,7},{6,4},{7,5},{8,10},{9,11},{10,... | collective-permute-start | bytes 1179656 | tf_op jit(solution)/shard_map/ppermute | solution.py:33
  20.6 9.6 %collective-permute-start.10 = (s32[1,2]{1,0:T(1,128)}, s32[1,2]{1,0:T(1,128)S(1)}, u32[]{:S(2)}, u32[]{:S(2)}) collective-permute-start(s32[1,2]{1,0:T(1,128)} %offsets.5), channel_id=1, source_target_pairs={{0,16},{16,0},{1,17},{17,1},{2,18},{18,2},{3,19},{19,3},{4,20},{20... | collective-permute-start | bytes 32 | tf_op jit(solution)/shard_map/ppermute | solution.py:29
  31.1 1.7 %collective-permute-start.11 = (bf16[8,16,1536]{2,1,0:T(8,128)(2,1)S(1)}, bf16[8,16,1536]{2,1,0:T(8,128)(2,1)S(1)}, u32[]{:S(2)}, u32[]{:S(2)}) collective-permute-start(bf16[8,16,1536]{2,1,0:T(8,128)(2,1)S(1)} %collective-permute-done.7), channel_id=1, source_target_pairs={{0,1},{1,0},{2,3},{3,2},{4,5},{5,4},{6,7},{7,6},{8,9},{9,8},{10,11... | collective-permute-start | bytes 1179656 | tf_op jit(solution)/shard_map/ppermute | solution.py:33
  32.9 15.8 %slice-start = ((s8[4718592]{0:T(1024)(128)(4,1)}), s8[4194304]{0:T(1024)(128)(4,1)S(1)}, s32[]{:S(2)}) async-start(s8[4718592]{0:T(1024)(128)(4,1)} %bitcast.38), calls=%async_computation | async-start | bytes 8388608
  36.2 12.4 %slice-start.1 = ((s8[4718592]{0:T(1024)(128)(4,1)}), s8[524288]{0:T(1024)(128)(4,1)S(1)}, s32[]{:S(2)}) async-start(s8[4718592]{0:T(1024)(128)(4,1)} %bitcast.38), calls=%async_computation.1 | async-start | bytes 1048576
  39.7 9.0 %copy-start = (f32[1,32,1536]{2,1,0:T(8,128)S(1)}, f32[1,32,1536]{2,1,0:T(8,128)}, u32[]{:S(2)}) copy-start(f32[1,32,1536]{2,1,0:T(8,128)} %param.21) | copy-start | bytes 589828
  39.7 1.5 %collective-permute-start.12 = (bf16[1,2,128,384]{3,2,1,0:T(8,128)(2,1)S(1)}, bf16[1,2,128,384]{3,2,1,0:T(8,128)(2,1)S(1)}, u32[]{:S(2)}, u32[]{:S(2)}) collective-permute-start(bf16[1,2,128,384]{3,2,1,0:T(8,128)(2,1)S(1)} %get-tuple-element.98), channel_id=1, source_target_pairs={{0,1},{1,0},{2,3},{3,2},{4,5},{5,4},{6,7},{7,6},{8,9},{9,8},{10,11... | collective-permute-start | bytes 589832 | tf_op jit(solution)/shard_map/ppermute | solution.py:33
  41.3 7.3 %collective-permute-start.16 = (bf16[2,1,128,384]{3,2,1,0:T(8,128)(2,1)S(1)}, bf16[2,1,128,384]{3,2,1,0:T(8,128)(2,1)S(1)}, u32[]{:S(2)}, u32[]{:S(2)}) collective-permute-start(bf16[2,1,128,384]{3,2,1,0:T(8,128)(2,1)S(1)} %slice.77), channel_id=1, source_target_pairs={{0,2},{1,3},{2,0},{3,1},{4,6},{5,7},{6,4},{7,5},{8,10},{9,11},{10,... | collective-permute-start | bytes 589832 | tf_op jit(solution)/shard_map/ppermute | solution.py:33
  46.7 6.1 %collective-permute-start.13 = (bf16[1,2,128,384]{3,2,1,0:T(8,128)(2,1)S(1)}, bf16[1,2,128,384]{3,2,1,0:T(8,128)(2,1)S(1)}, u32[]{:S(2)}, u32[]{:S(2)}) collective-permute-start(bf16[1,2,128,384]{3,2,1,0:T(8,128)(2,1)S(1)} %get-tuple-element.96), channel_id=1, source_target_pairs={{0,1},{1,0},{2,3},{3,2},{4,5},{5,4},{6,7},{7,6},{8,9},{9,8},{10,11... | collective-permute-start | bytes 589832 | tf_op jit(solution)/shard_map/ppermute | solution.py:33
  50.5 11.9 %collective-permute-start.17 = (bf16[8,16,1536]{2,1,0:T(8,128)(2,1)S(1)}, bf16[8,16,1536]{2,1,0:T(8,128)(2,1)S(1)}, u32[]{:S(2)}, u32[]{:S(2)}) collective-permute-start(bf16[8,16,1536]{2,1,0:T(8,128)(2,1)S(1)} %finish.3), channel_id=1, source_target_pairs={{0,16},{16,0},{1,17},{17,1},{2,18},{18,2},{3,19},{19,3},{4,20},{20... | collective-permute-start | bytes 1179656 | tf_op jit(solution)/shard_map/ppermute | solution.py:29
  52.8 6.1 %collective-permute-start.14 = (bf16[2,1,128,384]{3,2,1,0:T(8,128)(2,1)S(1)}, bf16[2,1,128,384]{3,2,1,0:T(8,128)(2,1)S(1)}, u32[]{:S(2)}, u32[]{:S(2)}) collective-permute-start(bf16[2,1,128,384]{3,2,1,0:T(8,128)(2,1)S(1)} %pad_maximum_fusion.1), channel_id=1, source_target_pairs={{0,2},{1,3},{2,0},{3,1},{4,6},{5,7},{6,4},{7,5},{8,10},{9,11},{10,... | collective-permute-start | bytes 589832 | tf_op jit(solution)/shard_map/ppermute | solution.py:33
  60.8 12.0 %collective-permute-start.15 = (bf16[8,16,1536]{2,1,0:T(8,128)(2,1)S(1)}, bf16[8,16,1536]{2,1,0:T(8,128)(2,1)S(1)}, u32[]{:S(2)}, u32[]{:S(2)}) collective-permute-start(bf16[8,16,1536]{2,1,0:T(8,128)(2,1)S(1)} %finish.2), channel_id=1, source_target_pairs={{0,16},{16,0},{1,17},{17,1},{2,18},{18,2},{3,19},{19,3},{4,20},{20... | collective-permute-start | bytes 1179656 | tf_op jit(solution)/shard_map/ppermute | solution.py:29
  62.4 10.4 %collective-permute-start.5 = (bf16[8,16,1536]{2,1,0:T(8,128)(2,1)S(1)}, bf16[8,16,1536]{2,1,0:T(8,128)(2,1)}, u32[]{:S(2)}, u32[]{:S(2)}) collective-permute-start(bf16[8,16,1536]{2,1,0:T(8,128)(2,1)S(1)} %param.3), channel_id=1, source_target_pairs={{0,12},{4,0},{8,4},{12,8},{1,13},{5,1},{9,5},{13,9},{2,14},{6,2},{... | collective-permute-start | bytes 1179656 | tf_op jit(solution)/shard_map/cond/branch_1_fun/ppermute | solution.py:29
